TPU v7x, 32 devices: a whole 2x2x4 slice. The times are simulated.
32 devices in a mesh: ctx: 8 (over z, y), head: 4 (over x, core).
Axes of the slice: x: 2, y: 2, z: 4, core: 2. Of those that a mesh axis runs over, the one named last changes fastest.
Arguments:
- queries: bfloat16 [32, 8192, 128], P('head', 'ctx'), may hold values from -0.52734375 to 0.52734375
- key_rows: bfloat16 [32, 8192, 128], P('head', 'ctx'), may hold values from -0.52734375 to 0.52734375
- value_rows: bfloat16 [32, 8192, 128], P('head', 'ctx'), may hold values from -0.52734375 to 0.52734375
- level_weight: float32 [4, 8192], P(None, 'ctx'), may hold values from 0.2 to 2
- out_grad: bfloat16 [32, 8192, 128], P('head', 'ctx'), may hold values from -1.0546875 to 1.0546875
Outputs:
- query_grad: bfloat16 [32, 8192, 128], P('head', 'ctx')
- key_grad: bfloat16 [32, 8192, 128], P('head', 'ctx')
- value_grad: bfloat16 [32, 8192, 128], P('head', 'ctx')
- weight_grad: float32 [4, 8192], P(None, 'ctx')
All inputs are finite; a program needn't handle non-finite values.
Results may differ from a plain program's by a relative error of at most 0.0057.
Values sent between devices are 32-bit elements; how exact they have to be, the bound alone decides.
No kernel may reach another device: no remote copies, remote signals or barrier semaphores. Data moves between devices by JAX's collectives and lax.ppermute only.
A program may use at most 128 MiB of HBM per device.

v0:
```python
import jax
import jax.numpy as jnp
from jax import lax
from jax.sharding import PartitionSpec as P


def local_block(operands, first_weight):
    queries, key_rows, value_rows, out_grad = operands
    length = queries.shape[0]
    steps = jnp.arange(length, dtype=jnp.int32)
    causal = (steps[:, None] >= steps[None, :]).astype(jnp.float32)
    scale = causal * first_weight[:, None]
    raw = jnp.einsum("td,sd->ts", queries, key_rows, preferred_element_type=jnp.float32)
    attn = (scale * raw).astype(jnp.bfloat16)
    d_attn = jnp.einsum("td,sd->ts", out_grad, value_rows, preferred_element_type=jnp.float32)
    local_weight = jnp.sum(causal * raw * d_attn, axis=1)
    d_raw = (scale * d_attn).astype(jnp.bfloat16)
    local_q = jnp.einsum("ts,sd->td", d_raw, key_rows, preferred_element_type=jnp.float32)
    local_k = jnp.einsum("ts,td->sd", d_raw, queries, preferred_element_type=jnp.float32)
    local_v = jnp.einsum("ts,td->sd", attn, out_grad, preferred_element_type=jnp.float32)
    return (local_q, local_k, local_v, local_weight)


def per_device(queries, key_rows, value_rows, level_weight, out_grad):
    levels = lax.axis_size("ctx").bit_length() - 1
    position = lax.axis_index("ctx")
    bit_flags = [(position // 2**height % 2).astype(jnp.float32) for height in range(levels)]
    group_state = jnp.einsum(
        "hcd,hce->hde", key_rows, value_rows, preferred_element_type=jnp.float32
    )
    pending = []
    for height in range(levels):
        level_row = level_weight[height + 1]
        weighted = (level_row[None, :, None] * out_grad.astype(jnp.float32)).astype(jnp.bfloat16)
        state_grad = jnp.einsum(
            "htd,hte->hde", queries, weighted, preferred_element_type=jnp.float32
        )
        pending.append(bit_flags[height] * state_grad)
    piece = lax.all_gather(group_state[None], "ctx", axis=0, tiled=True)
    rows_here = jnp.arange(piece.shape[0], dtype=jnp.int32)
    sums = []
    for collect_height in range(levels):
        lower = position // 2 ** (collect_height + 1) * 2 ** (collect_height + 1)
        inside = (rows_here >= lower) & (rows_here < lower + 2**collect_height)
        column = bit_flags[collect_height] * inside.astype(jnp.float32)
        sums.append(jnp.sum(column[:, None, None, None] * piece, axis=0))
    state_stack = jnp.stack(sums, axis=0)
    states = [state_stack[height] for height in range(levels)]
    local_q, local_k, local_v, local_weight = lax.map(
        lambda operands: local_block(operands, level_weight[0]),
        (queries, key_rows, value_rows, out_grad),
    )
    query_sum = local_q
    q_float = queries.astype(jnp.float32)
    weight_rows = [jnp.sum(local_weight, axis=0)]
    for height in range(levels):
        state_bf = states[height].astype(jnp.bfloat16)
        level_row = level_weight[height + 1]
        z_part = jnp.einsum("hte,hde->htd", out_grad, state_bf, preferred_element_type=jnp.float32)
        query_sum = query_sum + level_row[None, :, None] * z_part
        weight_rows.append(jnp.sum(z_part * q_float, axis=(0, 2)))
    weight_grad = lax.psum(jnp.stack(weight_rows, axis=0), "head")
    rows_here = jnp.arange(1 * lax.axis_size("ctx"), dtype=jnp.int32)
    total = jnp.zeros((1 * lax.axis_size("ctx"),) + group_state.shape, jnp.float32)
    for height in range(levels):
        span = 2**height
        clear = rows_here // span % 2 == 0
        reader = position // span == rows_here // span + 1
        column = (clear & reader).astype(jnp.float32)
        total = total + column[:, None, None, None] * pending[height][None]
    group_grad = lax.psum_scatter(total, "ctx", scatter_dimension=0, tiled=True)[0]
    grad_bf = group_grad.astype(jnp.bfloat16)
    key_sum = local_k + jnp.einsum(
        "hse,hde->hsd", value_rows, grad_bf, preferred_element_type=jnp.float32
    )
    value_sum = local_v + jnp.einsum(
        "hsd,hde->hse", key_rows, grad_bf, preferred_element_type=jnp.float32
    )
    return (
        query_sum.astype(jnp.bfloat16),
        key_sum.astype(jnp.bfloat16),
        value_sum.astype(jnp.bfloat16),
        weight_grad,
    )


def solution(mesh):
    placed = (
        P("head", "ctx", None),
        P("head", "ctx", None),
        P("head", "ctx", None),
        P(None, "ctx"),
        P("head", "ctx", None),
    )
    return jax.shard_map(
        per_device,
        mesh=mesh,
        in_specs=placed,
        out_specs=(
            P("head", "ctx", None),
            P("head", "ctx", None),
            P("head", "ctx", None),
            P(None, "ctx"),
        ),
        check_vma=False,
    )
```

profile of v0, /device:TPU:0, one launch (start us, length us, event | category | flops | bytes accessed | tf_op | source)
XLA Modules:
  0.0 200.9 jit_solution(3947016827274191922)
XLA Ops:
  7.2 3.9 %fusion.92 = f32[8,128,128]{2,1,0:T(8,128)} fusion(bf16[8,1024,128]{2,1,0:T(8,128)(2,1)} %param.8, bf16[8,1024,128]{2,1,0:T(8,128)(2,1)} %param.9), kind=kOutput, calls=%fused_computation.111 | convolution fusion | flops 268435456 | bytes 4718592 | tf_op jit(solution)/shard_map/hcd,hce->hde/dot_general | solution.py:28
  11.3 2.6 %copy.21 = bf16[8,1024,128]{1,2,0:T(8,128)(2,1)} copy(bf16[8,1024,128]{2,1,0:T(8,128)(2,1)S(1)} %copy-done.1) | data formatting | bytes 4194304 | tf_op args[4]
  13.9 3.1 %fusion.70 = f32[8,128,128]{1,2,0:T(8,128)S(1)} fusion(bf16[8,1024,128]{2,1,0:T(8,128)(2,1)} %param.7, bf16[8,1024,128]{1,2,0:T(8,128)(2,1)} %copy.21, f32[1024]{0:T(1024)S(1)} %bitcast.133, f32[]{:T(128)S(6)} %convert_element_type.83), kind=kOutput, calls=%fused_computation.75 | convolution fusion | flops 271712256 | bytes 4722692 | tf_op jit(solution)/shard_map/htd,hte->hde/dot_general | solution.py:35
  18.8 2.7 %multiply_add_fusion = f32[8,8,128,128]{2,3,1,0:T(8,128)} fusion(f32[8,128,128]{1,2,0:T(8,128)S(1)} %fusion.76, f32[8]{0:T(128)S(1)} %get-tuple-element.105, f32[8,128,128]{1,2,0:T(8,128)S(1)} %fusion.70, f32[8]{0:T(128)S(1)} %get-tuple-element.106, f32[8,128,128]{1,2,0:T(8,128)S(1)} %fusion.64, f32[8]{0:T(128)S(1)} %and_convert_fusion.2), kind=kLoop, calls=%fused_computation.62 | loop fusion | flops 5242880 | bytes 5767264 | tf_op jit(solution)/shard_map/add | solution.py:70
  21.5 100.8 %while.16 = (s32[]{:T(128)}, f32[8,1024,128]{1,2,0:T(8,128)}, f32[8,1024,128]{1,2,0:T(8,128)}, f32[8,1024,128]{1,2,0:T(8,128)}, f32[8,1024]{1,0:T(8,128)S(1)}, /...) while((s32[]{:T(128)}, f32[8,1024,128]{1,2,0:T(8,128)}, ...), condition=%wide.region_2.3_spmd, body=%wide.region_0.2_spmd.sunk | while | flops 1358953472 | bytes 45388948 | solution.py:49
  21.5 1.8 fusion.128
  23.3 1.9 multiply_reduce_fusion.5
  25.3 2.4 %fusion.129 = f32[8,1024,128]{1,2,0:T(8,128)} fusion(f32[8,1024,128]{1,2,0:T(8,128)} %get-tuple-element.185, s32[]{:T(128)} %get-tuple-element.184, f32[1024,1024]{0,1:T(8,128)S(1)} %get-tuple-element.170, f32[1024]{0:T(1024)S(1)} %bitcast.126, bf16[8,1024,128]{2,1,0:T(8,128)(2,1)} %get-tuple-element.204), kind=kOutput, calls=%fused_computation.14.clone.1 | convolution fusion | flops 272629760 | bytes 4985856 | tf_op jit(solution)/shard_map/while/body/eval_jaxpr/ts,sd->td/dot_general | solution.py:18
  27.7 2.6 %fusion.130 = f32[8,1024,128]{1,2,0:T(8,128)} fusion(f32[8,1024,128]{1,2,0:T(8,128)} %get-tuple-element.186, s32[]{:T(128)} %get-tuple-element.184, f32[1024,1024]{0,1:T(8,128)S(1)} %get-tuple-element.170, f32[1024]{0:T(1024)S(1)} %bitcast.127, bf16[8,1024,128]{2,1,0:T(8,128)(2,1)} %get-tuple-element.205), kind=kOutput, calls=%fused_computation.12.clone.1 | convolution fusion | flops 272629760 | bytes 4985856 | tf_op jit(solution)/shard_map/while/body/eval_jaxpr/ts,td->sd/dot_general | solution.py:19
  30.3 3.9 %fusion.131 = f32[8,1024,128]{1,2,0:T(8,128)} fusion(f32[8,1024,128]{1,2,0:T(8,128)} %get-tuple-element.187, s32[]{:T(128)} %get-tuple-element.184, f32[1024,1024]{0,1:T(8,128)} %copy-done, f32[1024]{0:T(1024)S(1)} %bitcast.128, bf16[8,1024,128]{2,1,0:T(8,128)(2,1)S(1)} %get-tuple-element.202), kind=kOutput, calls=%fused_computation.10.clone.1 | convolution fusion | flops 272629760 | bytes 4985856 | tf_op jit(solution)/shard_map/while/body/eval_jaxpr/ts,td->sd/dot_general | solution.py:20
  35.9 1.9 multiply_reduce_fusion.5
  37.9 2.4 %fusion.129 = f32[8,1024,128]{1,2,0:T(8,128)} fusion(f32[8,1024,128]{1,2,0:T(8,128)} %get-tuple-element.185, s32[]{:T(128)} %get-tuple-element.184, f32[1024,1024]{0,1:T(8,128)S(1)} %get-tuple-element.170, f32[1024]{0:T(1024)S(1)} %bitcast.126, bf16[8,1024,128]{2,1,0:T(8,128)(2,1)} %get-tuple-element.204), kind=kOutput, calls=%fused_computation.14.clone.1 | convolution fusion | flops 272629760 | bytes 4985856 | tf_op jit(solution)/shard_map/while/body/eval_jaxpr/ts,sd->td/dot_general | solution.py:18
  40.3 2.6 %fusion.130 = f32[8,1024,128]{1,2,0:T(8,128)} fusion(f32[8,1024,128]{1,2,0:T(8,128)} %get-tuple-element.186, s32[]{:T(128)} %get-tuple-element.184, f32[1024,1024]{0,1:T(8,128)S(1)} %get-tuple-element.170, f32[1024]{0:T(1024)S(1)} %bitcast.127, bf16[8,1024,128]{2,1,0:T(8,128)(2,1)} %get-tuple-element.205), kind=kOutput, calls=%fused_computation.12.clone.1 | convolution fusion | flops 272629760 | bytes 4985856 | tf_op jit(solution)/shard_map/while/body/eval_jaxpr/ts,td->sd/dot_general | solution.py:19
  42.9 3.9 %fusion.131 = f32[8,1024,128]{1,2,0:T(8,128)} fusion(f32[8,1024,128]{1,2,0:T(8,128)} %get-tuple-element.187, s32[]{:T(128)} %get-tuple-element.184, f32[1024,1024]{0,1:T(8,128)} %copy-done, f32[1024]{0:T(1024)S(1)} %bitcast.128, bf16[8,1024,128]{2,1,0:T(8,128)(2,1)S(1)} %get-tuple-element.202), kind=kOutput, calls=%fused_computation.10.clone.1 | convolution fusion | flops 272629760 | bytes 4985856 | tf_op jit(solution)/shard_map/while/body/eval_jaxpr/ts,td->sd/dot_general | solution.py:20
  48.6 1.9 multiply_reduce_fusion.5
  50.5 2.3 %fusion.129 = f32[8,1024,128]{1,2,0:T(8,128)} fusion(f32[8,1024,128]{1,2,0:T(8,128)} %get-tuple-element.185, s32[]{:T(128)} %get-tuple-element.184, f32[1024,1024]{0,1:T(8,128)S(1)} %get-tuple-element.170, f32[1024]{0:T(1024)S(1)} %bitcast.126, bf16[8,1024,128]{2,1,0:T(8,128)(2,1)} %get-tuple-element.204), kind=kOutput, calls=%fused_computation.14.clone.1 | convolution fusion | flops 272629760 | bytes 4985856 | tf_op jit(solution)/shard_map/while/body/eval_jaxpr/ts,sd->td/dot_general | solution.py:18
  52.9 2.6 %fusion.130 = f32[8,1024,128]{1,2,0:T(8,128)} fusion(f32[8,1024,128]{1,2,0:T(8,128)} %get-tuple-element.186, s32[]{:T(128)} %get-tuple-element.184, f32[1024,1024]{0,1:T(8,128)S(1)} %get-tuple-element.170, f32[1024]{0:T(1024)S(1)} %bitcast.127, bf16[8,1024,128]{2,1,0:T(8,128)(2,1)} %get-tuple-element.205), kind=kOutput, calls=%fused_computation.12.clone.1 | convolution fusion | flops 272629760 | bytes 4985856 | tf_op jit(solution)/shard_map/while/body/eval_jaxpr/ts,td->sd/dot_general | solution.py:19
  55.6 3.9 %fusion.131 = f32[8,1024,128]{1,2,0:T(8,128)} fusion(f32[8,1024,128]{1,2,0:T(8,128)} %get-tuple-element.187, s32[]{:T(128)} %get-tuple-element.184, f32[1024,1024]{0,1:T(8,128)} %copy-done, f32[1024]{0:T(1024)S(1)} %bitcast.128, bf16[8,1024,128]{2,1,0:T(8,128)(2,1)S(1)} %get-tuple-element.202), kind=kOutput, calls=%fused_computation.10.clone.1 | convolution fusion | flops 272629760 | bytes 4985856 | tf_op jit(solution)/shard_map/while/body/eval_jaxpr/ts,td->sd/dot_general | solution.py:20
  61.2 1.9 multiply_reduce_fusion.5
  63.1 2.3 %fusion.129 = f32[8,1024,128]{1,2,0:T(8,128)} fusion(f32[8,1024,128]{1,2,0:T(8,128)} %get-tuple-element.185, s32[]{:T(128)} %get-tuple-element.184, f32[1024,1024]{0,1:T(8,128)S(1)} %get-tuple-element.170, f32[1024]{0:T(1024)S(1)} %bitcast.126, bf16[8,1024,128]{2,1,0:T(8,128)(2,1)} %get-tuple-element.204), kind=kOutput, calls=%fused_computation.14.clone.1 | convolution fusion | flops 272629760 | bytes 4985856 | tf_op jit(solution)/shard_map/while/body/eval_jaxpr/ts,sd->td/dot_general | solution.py:18
  65.5 2.6 %fusion.130 = f32[8,1024,128]{1,2,0:T(8,128)} fusion(f32[8,1024,128]{1,2,0:T(8,128)} %get-tuple-element.186, s32[]{:T(128)} %get-tuple-element.184, f32[1024,1024]{0,1:T(8,128)S(1)} %get-tuple-element.170, f32[1024]{0:T(1024)S(1)} %bitcast.127, bf16[8,1024,128]{2,1,0:T(8,128)(2,1)} %get-tuple-element.205), kind=kOutput, calls=%fused_computation.12.clone.1 | convolution fusion | flops 272629760 | bytes 4985856 | tf_op jit(solution)/shard_map/while/body/eval_jaxpr/ts,td->sd/dot_general | solution.py:19
  68.1 3.8 %fusion.131 = f32[8,1024,128]{1,2,0:T(8,128)} fusion(f32[8,1024,128]{1,2,0:T(8,128)} %get-tuple-element.187, s32[]{:T(128)} %get-tuple-element.184, f32[1024,1024]{0,1:T(8,128)} %copy-done, f32[1024]{0:T(1024)S(1)} %bitcast.128, bf16[8,1024,128]{2,1,0:T(8,128)(2,1)S(1)} %get-tuple-element.202), kind=kOutput, calls=%fused_computation.10.clone.1 | convolution fusion | flops 272629760 | bytes 4985856 | tf_op jit(solution)/shard_map/while/body/eval_jaxpr/ts,td->sd/dot_general | solution.py:20
  73.7 1.9 multiply_reduce_fusion.5
  75.7 2.3 %fusion.129 = f32[8,1024,128]{1,2,0:T(8,128)} fusion(f32[8,1024,128]{1,2,0:T(8,128)} %get-tuple-element.185, s32[]{:T(128)} %get-tuple-element.184, f32[1024,1024]{0,1:T(8,128)S(1)} %get-tuple-element.170, f32[1024]{0:T(1024)S(1)} %bitcast.126, bf16[8,1024,128]{2,1,0:T(8,128)(2,1)} %get-tuple-element.204), kind=kOutput, calls=%fused_computation.14.clone.1 | convolution fusion | flops 272629760 | bytes 4985856 | tf_op jit(solution)/shard_map/while/body/eval_jaxpr/ts,sd->td/dot_general | solution.py:18
  78.1 2.6 %fusion.130 = f32[8,1024,128]{1,2,0:T(8,128)} fusion(f32[8,1024,128]{1,2,0:T(8,128)} %get-tuple-element.186, s32[]{:T(128)} %get-tuple-element.184, f32[1024,1024]{0,1:T(8,128)S(1)} %get-tuple-element.170, f32[1024]{0:T(1024)S(1)} %bitcast.127, bf16[8,1024,128]{2,1,0:T(8,128)(2,1)} %get-tuple-element.205), kind=kOutput, calls=%fused_computation.12.clone.1 | convolution fusion | flops 272629760 | bytes 4985856 | tf_op jit(solution)/shard_map/while/body/eval_jaxpr/ts,td->sd/dot_general | solution.py:19
  80.7 3.8 %fusion.131 = f32[8,1024,128]{1,2,0:T(8,128)} fusion(f32[8,1024,128]{1,2,0:T(8,128)} %get-tuple-element.187, s32[]{:T(128)} %get-tuple-element.184, f32[1024,1024]{0,1:T(8,128)} %copy-done, f32[1024]{0:T(1024)S(1)} %bitcast.128, bf16[8,1024,128]{2,1,0:T(8,128)(2,1)S(1)} %get-tuple-element.202), kind=kOutput, calls=%fused_computation.10.clone.1 | convolution fusion | flops 272629760 | bytes 4985856 | tf_op jit(solution)/shard_map/while/body/eval_jaxpr/ts,td->sd/dot_general | solution.py:20
  86.3 1.9 multiply_reduce_fusion.5
  88.3 2.3 %fusion.129 = f32[8,1024,128]{1,2,0:T(8,128)} fusion(f32[8,1024,128]{1,2,0:T(8,128)} %get-tuple-element.185, s32[]{:T(128)} %get-tuple-element.184, f32[1024,1024]{0,1:T(8,128)S(1)} %get-tuple-element.170, f32[1024]{0:T(1024)S(1)} %bitcast.126, bf16[8,1024,128]{2,1,0:T(8,128)(2,1)} %get-tuple-element.204), kind=kOutput, calls=%fused_computation.14.clone.1 | convolution fusion | flops 272629760 | bytes 4985856 | tf_op jit(solution)/shard_map/while/body/eval_jaxpr/ts,sd->td/dot_general | solution.py:18
  90.6 2.6 %fusion.130 = f32[8,1024,128]{1,2,0:T(8,128)} fusion(f32[8,1024,128]{1,2,0:T(8,128)} %get-tuple-element.186, s32[]{:T(128)} %get-tuple-element.184, f32[1024,1024]{0,1:T(8,128)S(1)} %get-tuple-element.170, f32[1024]{0:T(1024)S(1)} %bitcast.127, bf16[8,1024,128]{2,1,0:T(8,128)(2,1)} %get-tuple-element.205), kind=kOutput, calls=%fused_computation.12.clone.1 | convolution fusion | flops 272629760 | bytes 4985856 | tf_op jit(solution)/shard_map/while/body/eval_jaxpr/ts,td->sd/dot_general | solution.py:19
  93.3 3.9 %fusion.131 = f32[8,1024,128]{1,2,0:T(8,128)} fusion(f32[8,1024,128]{1,2,0:T(8,128)} %get-tuple-element.187, s32[]{:T(128)} %get-tuple-element.184, f32[1024,1024]{0,1:T(8,128)} %copy-done, f32[1024]{0:T(1024)S(1)} %bitcast.128, bf16[8,1024,128]{2,1,0:T(8,128)(2,1)S(1)} %get-tuple-element.202), kind=kOutput, calls=%fused_computation.10.clone.1 | convolution fusion | flops 272629760 | bytes 4985856 | tf_op jit(solution)/shard_map/while/body/eval_jaxpr/ts,td->sd/dot_general | solution.py:20
  98.9 1.9 multiply_reduce_fusion.5
  100.9 2.3 %fusion.129 = f32[8,1024,128]{1,2,0:T(8,128)} fusion(f32[8,1024,128]{1,2,0:T(8,128)} %get-tuple-element.185, s32[]{:T(128)} %get-tuple-element.184, f32[1024,1024]{0,1:T(8,128)S(1)} %get-tuple-element.170, f32[1024]{0:T(1024)S(1)} %bitcast.126, bf16[8,1024,128]{2,1,0:T(8,128)(2,1)} %get-tuple-element.204), kind=kOutput, calls=%fused_computation.14.clone.1 | convolution fusion | flops 272629760 | bytes 4985856 | tf_op jit(solution)/shard_map/while/body/eval_jaxpr/ts,sd->td/dot_general | solution.py:18
  103.2 2.6 %fusion.130 = f32[8,1024,128]{1,2,0:T(8,128)} fusion(f32[8,1024,128]{1,2,0:T(8,128)} %get-tuple-element.186, s32[]{:T(128)} %get-tuple-element.184, f32[1024,1024]{0,1:T(8,128)S(1)} %get-tuple-element.170, f32[1024]{0:T(1024)S(1)} %bitcast.127, bf16[8,1024,128]{2,1,0:T(8,128)(2,1)} %get-tuple-element.205), kind=kOutput, calls=%fused_computation.12.clone.1 | convolution fusion | flops 272629760 | bytes 4985856 | tf_op jit(solution)/shard_map/while/body/eval_jaxpr/ts,td->sd/dot_general | solution.py:19
  105.8 3.9 %fusion.131 = f32[8,1024,128]{1,2,0:T(8,128)} fusion(f32[8,1024,128]{1,2,0:T(8,128)} %get-tuple-element.187, s32[]{:T(128)} %get-tuple-element.184, f32[1024,1024]{0,1:T(8,128)} %copy-done, f32[1024]{0:T(1024)S(1)} %bitcast.128, bf16[8,1024,128]{2,1,0:T(8,128)(2,1)S(1)} %get-tuple-element.202), kind=kOutput, calls=%fused_computation.10.clone.1 | convolution fusion | flops 272629760 | bytes 4985856 | tf_op jit(solution)/shard_map/while/body/eval_jaxpr/ts,td->sd/dot_general | solution.py:20
  111.5 1.9 multiply_reduce_fusion.5
  113.5 2.3 %fusion.129 = f32[8,1024,128]{1,2,0:T(8,128)} fusion(f32[8,1024,128]{1,2,0:T(8,128)} %get-tuple-element.185, s32[]{:T(128)} %get-tuple-element.184, f32[1024,1024]{0,1:T(8,128)S(1)} %get-tuple-element.170, f32[1024]{0:T(1024)S(1)} %bitcast.126, bf16[8,1024,128]{2,1,0:T(8,128)(2,1)} %get-tuple-element.204), kind=kOutput, calls=%fused_computation.14.clone.1 | convolution fusion | flops 272629760 | bytes 4985856 | tf_op jit(solution)/shard_map/while/body/eval_jaxpr/ts,sd->td/dot_general | solution.py:18
  115.8 2.6 %fusion.130 = f32[8,1024,128]{1,2,0:T(8,128)} fusion(f32[8,1024,128]{1,2,0:T(8,128)} %get-tuple-element.186, s32[]{:T(128)} %get-tuple-element.184, f32[1024,1024]{0,1:T(8,128)S(1)} %get-tuple-element.170, f32[1024]{0:T(1024)S(1)} %bitcast.127, bf16[8,1024,128]{2,1,0:T(8,128)(2,1)} %get-tuple-element.205), kind=kOutput, calls=%fused_computation.12.clone.1 | convolution fusion | flops 272629760 | bytes 4985856 | tf_op jit(solution)/shard_map/while/body/eval_jaxpr/ts,td->sd/dot_general | solution.py:19
  118.5 3.9 %fusion.131 = f32[8,1024,128]{1,2,0:T(8,128)} fusion(f32[8,1024,128]{1,2,0:T(8,128)} %get-tuple-element.187, s32[]{:T(128)} %get-tuple-element.184, f32[1024,1024]{0,1:T(8,128)} %copy-done, f32[1024]{0:T(1024)S(1)} %bitcast.128, bf16[8,1024,128]{2,1,0:T(8,128)(2,1)S(1)} %get-tuple-element.202), kind=kOutput, calls=%fused_computation.10.clone.1 | convolution fusion | flops 272629760 | bytes 4985856 | tf_op jit(solution)/shard_map/while/body/eval_jaxpr/ts,td->sd/dot_general | solution.py:20
  122.4 3.9 %copy.25 = bf16[8,1024,128]{1,2,0:T(8,128)(2,1)} copy(bf16[8,1024,128]{2,1,0:T(8,128)(2,1)} %get-tuple-element.215) | data formatting | bytes 4194304 | tf_op args[0]
  126.4 3.2 %multiply_reduce_fusion.3 = (bf16[8,128,128]{2,1,0:T(8,128)(2,1)S(1)}, bf16[8,128,128]{2,1,0:T(8,128)(2,1)S(1)}, bf16[8,128,128]{2,1,0:T(8,128)(2,1)S(1)}) fusion(f32[8,8,128,128]{3,2,1,0:T(8,128)} %bitcast.124, f32[8]{0:T(128)S(1)} %and_select_fusion.7, f32[8]{0:T(128)S(1)} %get-tuple-element.103, f32[8]{0:T(128)S(1)} %get-tuple-element.104), kind=kLoop, calls=%fused_computation.65 | loop fusion | flops 5898240 | bytes 4980832 | tf_op jit(solution)/shard_map/reduce_sum | solution.py:46
  133.2 3.3 %fusion.43 = (f32[1024]{0:T(1024)S(1)}, f32[1024]{0:T(1024)S(1)}, f32[1024]{0:T(1024)S(1)}, bf16[8,1024,128]{1,2,0:T(8,128)(2,1)}) fusion(bf16[8,1024,128]{1,2,0:T(8,128)(2,1)S(1)} %copy-done.4, f32[8,128,1024]{2,1,0:T(8,128)S(1)} %fusion.94, f32[8,128,1024]{2,1,0:T(8,128)S(1)} %fusion.93, f32[1024]{0:T(1024)S(1)} %bitcast.132, f32[1024]{0:T(1024)S(1)} %bitcast.134, ...), kind=kOutput, calls=%fused_computation.48 | convolution fusion | flops 283112448 | bytes 19161088 | tf_op jit(solution)/shard_map/hte,hde->htd/dot_general | solution.py:59
  136.5 4.1 %copy.26 = bf16[8,1024,128]{2,1,0:T(8,128)(2,1)} copy(bf16[8,1024,128]{1,2,0:T(8,128)(2,1)} %get-tuple-element.99) | data formatting | bytes 4194304
  140.6 13.4 %psum.7 = f32[4,1024]{1,0:T(4,128)} all-reduce(f32[4,1024]{1,0:T(4,128)S(1)} %pad_maximum_fusion), channel_id=1, replica_groups=mesh['ctx'=8,'head'=4] {'head'}, use_global_device_ids=true, to_apply=%region_11.12 | all-reduce | flops 4096 | bytes 32768 | tf_op jit(solution)/shard_map/psum | solution.py:62
  154.0 23.4 %reduce-scatter.2.cloned.1.call-done = f32[1,8,128,128]{2,3,1,0:T(8,128)} async-done(((f32[8,8,128,128]{2,3,1,0:T(8,128)}), f32[1,8,128,128]{2,3,1,0:T(8,128)}) %reduce-scatter.2.cloned.1.call-update) | async-done | bytes 524304 | tf_op jit(solution)/shard_map/reduce_scatter | solution.py:71
  177.4 4.4 %fusion.47 = bf16[8,1024,128]{1,2,0:T(8,128)(2,1)} fusion(f32[8,1024,128]{1,2,0:T(8,128)} %get-tuple-element.60, bf16[8,1024,128]{2,1,0:T(8,128)(2,1)S(1)} %copy-done.2, f32[1,8,128,128]{2,3,1,0:T(8,128)} %reduce-scatter.2.cloned.1.call-done), kind=kOutput, calls=%fused_computation.54 | convolution fusion | flops 270663680 | bytes 8912896 | tf_op jit(solution)/shard_map/hse,hde->hsd/dot_general | solution.py:73
  181.9 4.1 %copy.27 = bf16[8,1024,128]{2,1,0:T(8,128)(2,1)} copy(bf16[8,1024,128]{1,2,0:T(8,128)(2,1)} %fusion.47) | data formatting | bytes 4194304
  185.9 4.2 %fusion.46 = bf16[8,1024,128]{1,2,0:T(8,128)(2,1)} fusion(f32[8,1024,128]{1,2,0:T(8,128)} %get-tuple-element.61, bf16[8,1024,128]{2,1,0:T(8,128)(2,1)S(1)} %copy-done.3, f32[1,8,128,128]{2,3,1,0:T(8,128)S(1)} %copy-done.7), kind=kOutput, calls=%fused_computation.52 | convolution fusion | flops 270663680 | bytes 8912896 | tf_op jit(solution)/shard_map/hsd,hde->hse/dot_general | solution.py:76
  190.2 3.9 %copy.28 = bf16[8,1024,128]{2,1,0:T(8,128)(2,1)} copy(bf16[8,1024,128]{1,2,0:T(8,128)(2,1)} %fusion.46) | data formatting | bytes 4194304
  (77 shorter events, 19.1 us)
Async XLA Ops:
  7.2 4.1 %copy-start.1 = (bf16[8,1024,128]{2,1,0:T(8,128)(2,1)S(1)}, bf16[8,1024,128]{2,1,0:T(8,128)(2,1)}, u32[]{:S(2)}) copy-start(bf16[8,1024,128]{2,1,0:T(8,128)(2,1)} %param.11) | copy-start | bytes 6291460
  7.2 6.7 %copy-start.9 = (f32[4,1024]{1,0:T(4,128)S(1)}, f32[4,1024]{1,0:T(4,128)}, u32[]{:S(2)}) copy-start(f32[4,1024]{1,0:T(4,128)} %param.10) | copy-start | bytes 49156
  7.2 119.2 %all-gather.3.cloned.1.call-start = ((), (), s32[]{:S(2)}) async-start(), calls=%async_computation.2 | async-start | bytes 4718592 | tf_op jit(solution)/shard_map/all_gather | solution.py:39
  11.2 166.2 %reduce-scatter.2.cloned.1.call-start = ((), (), s32[]{:S(2)}) async-start(), calls=%async_computation.1 | async-start | bytes 4718592 | tf_op jit(solution)/shard_map/reduce_scatter | solution.py:71
  13.9 3.1 %copy-start.5 = (bf16[8,1024,128]{2,1,0:T(8,128)(2,1)S(1)}, bf16[8,1024,128]{2,1,0:T(8,128)(2,1)}, u32[]{:S(2)}) copy-start(bf16[8,1024,128]{2,1,0:T(8,128)(2,1)} %param.7) | copy-start | bytes 6291460
  13.9 3.5 %copy-start.8 = (bf16[8,1024,128]{1,2,0:T(8,128)(2,1)S(1)}, bf16[8,1024,128]{1,2,0:T(8,128)(2,1)}, u32[]{:S(2)}) copy-start(bf16[8,1024,128]{1,2,0:T(8,128)(2,1)} %copy.21) | copy-start | bytes 6291460
  23.3 2.0 copy-start
  35.9 2.0 copy-start
  48.6 2.0 copy-start
  61.1 2.0 copy-start
  73.7 2.0 copy-start
  86.3 2.0 copy-start
  98.9 2.0 copy-start
  111.5 2.0 copy-start
  130.3 1.6 copy-start.4
  130.3 2.9 %copy-start.6 = (f32[8,1024,128]{1,2,0:T(8,128)S(1)}, f32[8,1024,128]{1,2,0:T(8,128)}, u32[]{:S(2)}) copy-start(f32[8,1024,128]{1,2,0:T(8,128)} %get-tuple-element.59) | copy-start | bytes 12582916
  136.5 40.9 %copy-start.2 = (bf16[8,1024,128]{2,1,0:T(8,128)(2,1)S(1)}, bf16[8,1024,128]{2,1,0:T(8,128)(2,1)}, u32[]{:S(2)}) copy-start(bf16[8,1024,128]{2,1,0:T(8,128)(2,1)} %get-tuple-element.213) | copy-start | bytes 6291460
  181.8 4.1 %copy-start.3 = (bf16[8,1024,128]{2,1,0:T(8,128)(2,1)S(1)}, bf16[8,1024,128]{2,1,0:T(8,128)(2,1)}, u32[]{:S(2)}) copy-start(bf16[8,1024,128]{2,1,0:T(8,128)(2,1)} %get-tuple-element.214) | copy-start | bytes 6291460
  181.8 4.1 %copy-start.7 = (f32[1,8,128,128]{2,3,1,0:T(8,128)S(1)}, f32[1,8,128,128]{2,3,1,0:T(8,128)}, u32[]{:S(2)}) copy-start(f32[1,8,128,128]{2,3,1,0:T(8,128)} %reduce-scatter.2.cloned.1.call-done) | copy-start | bytes 1572868
Sparse Core Ops, SparseCore 0:
  11.3 76.2 all-gather.2
  91.2 86.1 reduce-scatter.1
where the time goes:
time: 203 us; the launch traced here: 201 us
  matrix products  121 us (60%)
  waiting for transfers between devices  23.5 us (12%)
  local copies, waits for them, and re-layouts  22.4 us (11%)
  between operations  14.3 us (7%)
  blocking collectives  13.4 us (7%)
  other arithmetic  5.92 us (3%)
    dot_general x8, matrix products, local_block(): jnp.einsum('ts,td->sd', attn, out_grad, preferred_element_type=jnp.float32)  30.8 us
    reduce_scatter x1, waiting for transfers between devices, per_device(): lax.psum_scatter(total, 'ctx', scatter_dimension=0, tiled=True)[0]  23.4 us
    unnamed x23, local copies, waits for them, and re-layouts  21.1 us
    dot_general x8, matrix products, local_block(): jnp.einsum('ts,td->sd', d_raw, queries, preferred_element_type=jnp.float32)  20.8 us
    dot_general x8, matrix products, local_block(): jnp.einsum('ts,sd->td', d_raw, key_rows, preferred_element_type=jnp.float32)  18.7 us
    dot_general x8, matrix products, local_block(): jnp.einsum('td,sd->ts', out_grad, value_rows, preferred_element_type=jnp....  14.9 us
    dot_general x8, matrix products, local_block(): jnp.einsum('td,sd->ts', queries, key_rows, preferred_element_type=jnp.flo...  14 us
    psum x1, blocking collectives, per_device(): weight_grad = lax.psum(jnp.stack(weight_rows, axis=0), 'head')  13.4 us
  transfers between devices with their start and end apart: 2, of which 1 were waited for; matrix products, arithmetic and copies ran while one was open for 63% of the time, Pallas kernels for 0%

commit v1 on v0

v1 whole, which is shorter than its diff:
```python
import jax
import jax.numpy as jnp
from jax import lax
from jax.experimental import pallas as pl
from jax.experimental.pallas import tpu as pltpu
from jax.sharding import PartitionSpec as P

F32, BF16 = jnp.float32, jnp.bfloat16
NN = (((1,), (0,)), ((), ()))
NT = (((1,), (1,)), ((), ()))
TN = (((0,), (0,)), ((), ()))
VMEM_BYTES = 40 * 2**20
PARTS = 2
GROUPS = (2, 1, 1, 2, 1, 1)


def dot(a, b, dims):
    return lax.dot_general(a, b, dims, preferred_element_type=F32)


def any_spec():
    return pl.BlockSpec(memory_space=pl.ANY)


def smem_spec():
    return pl.BlockSpec(memory_space=pltpu.SMEM)


def head_spec(shape, first):
    return pl.BlockSpec((1,) + shape[1:], lambda h: (first + h, 0, 0))


def params():
    return pltpu.CompilerParams(vmem_limit_bytes=VMEM_BYTES)


def cost(flops, bytes_accessed):
    return pl.CostEstimate(flops=int(flops), bytes_accessed=int(bytes_accessed), transcendentals=0)


def states_of(key_rows, value_rows, first, count, deps):
    _, length, depth = key_rows.shape

    def kernel(k_ref, v_ref, *rest):
        rest[-1][0] = dot(k_ref[0], v_ref[0], TN)

    return pl.pallas_call(
        kernel,
        grid=(count,),
        in_specs=[head_spec(key_rows.shape, first)] * 2 + [any_spec()] * len(deps),
        out_specs=pl.BlockSpec((1, depth, depth), lambda h: (h, 0, 0)),
        out_shape=jax.ShapeDtypeStruct((count, depth, depth), F32),
        compiler_params=params(),
        cost_estimate=cost(count * length * depth * depth * 8, count * length * depth * 4),
        name="states",
    )(key_rows, value_rows, *deps)


def state_grads_of(flags, queries, out_grad, level_weight, first, count, deps):
    _, length, depth = queries.shape
    levels = level_weight.shape[0] - 1

    def kernel(flag_ref, q_ref, g_ref, w_ref, *rest):
        outs, columns = rest[len(deps) : len(deps) + levels], rest[-1]

        @pl.when(pl.program_id(0) == 0)
        def _():
            for level in range(levels):
                row = w_ref[level + 1 : level + 2, :] * flag_ref[level]
                columns[level] = jnp.broadcast_to(row, (depth, length)).T

        g = g_ref[0].astype(F32)
        weighted = [(columns[level] * g).astype(BF16) for level in range(levels)]
        grads = dot(q_ref[0], jnp.concatenate(weighted, axis=1), TN)
        for level in range(levels):
            outs[level][0] = grads[:, level * depth : (level + 1) * depth]

    return pl.pallas_call(
        kernel,
        grid=(count,),
        in_specs=[smem_spec()]
        + [head_spec(queries.shape, first)] * 2
        + [pl.BlockSpec(level_weight.shape, lambda h: (0, 0))]
        + [any_spec()] * len(deps),
        out_specs=[pl.BlockSpec((1, depth, depth), lambda h: (h, 0, 0))] * levels,
        out_shape=[jax.ShapeDtypeStruct((count, depth, depth), F32)] * levels,
        scratch_shapes=[pltpu.VMEM((levels, length, depth), F32)],
        compiler_params=params(),
        cost_estimate=cost(
            levels * count * length * depth * depth * 8, count * length * depth * 4
        ),
        name="state_grads",
    )(flags, queries, out_grad, level_weight, *deps)


def local_of(level_weight, queries, key_rows, value_rows, out_grad, held, first, count, deps):
    heads, length, depth = queries.shape
    tile = min(256, length)

    def kernel(w_ref, q_ref, k_ref, v_ref, g_ref, *rest):
        lq_ref, lk_ref, lv_ref, lw_ref, k_sum, v_sum = rest[-6:]

        @pl.when(pl.program_id(0) == 0)
        def _():
            lw_ref[...] = jnp.zeros_like(lw_ref)

        k_turned = k_ref[0].T
        for i in range(length // tile):
            upto = (i + 1) * tile
            t = pl.ds(i * tile, tile)
            s = pl.ds(0, upto)
            q, g, w = q_ref[0, t, :], g_ref[0, t, :], w_ref[0:1, t]
            raw = dot(k_ref[0, s, :], q, NT)
            d_attn = dot(v_ref[0, s, :], g, NT)
            rows = lax.broadcasted_iota(jnp.int32, (upto, tile), 0)
            columns = lax.broadcasted_iota(jnp.int32, (upto, tile), 1) + i * tile
            raw = jnp.where(rows <= columns, raw, 0.0)
            d_attn = jnp.where(rows <= columns, d_attn, 0.0)
            lw_ref[0:1, t] += jnp.sum(raw * d_attn, axis=0, keepdims=True)
            attn = (raw * w).astype(BF16)
            d_raw = (d_attn * w).astype(BF16)
            k_part, v_part = dot(d_raw, q, NN), dot(attn, g, NN)
            k_sum[t, :] = k_part[i * tile :]
            v_sum[t, :] = v_part[i * tile :]
            if i:
                before = pl.ds(0, i * tile)
                k_sum[before, :] += k_part[: i * tile]
                v_sum[before, :] += v_part[: i * tile]
            lq_ref[0, t, :] = dot(k_turned[:, :upto], d_raw, NN).T
        lk_ref[0] = k_sum[...]
        lv_ref[0] = v_sum[...]

    spec = head_spec(queries.shape, first)
    extra = list(held) + list(deps)
    return pl.pallas_call(
        kernel,
        grid=(count,),
        in_specs=[pl.BlockSpec(level_weight.shape, lambda h: (0, 0))]
        + [spec] * 4
        + [any_spec()] * len(extra),
        out_specs=[spec] * 3 + [pl.BlockSpec((1, length), lambda h: (0, 0))],
        out_shape=[jax.ShapeDtypeStruct(queries.shape, F32)] * 3
        + [jax.ShapeDtypeStruct((1, length), F32)],
        scratch_shapes=[pltpu.VMEM((length, depth), F32)] * 2,
        input_output_aliases={5 + i: i for i in range(len(held))},
        compiler_params=params(),
        cost_estimate=cost(count * length * length * depth * 10, count * length * depth * 20),
        name="local",
    )(level_weight, queries, key_rows, value_rows, out_grad, *extra)


def query_side(flags, level_weight, queries, out_grad, sums, states, levels_here, held, kind, first, deps):
    _, length, depth = queries.shape
    number = len(levels_here)
    count = states[0][0].shape[0]
    flat = [part for parts in states for part in parts]

    def kernel(flag_ref, w_ref, q_ref, g_ref, sum_ref, *rest):
        out_ref, row_ref, columns, total = rest[-4:]

        @pl.when(pl.program_id(0) == 0)
        def _():
            for i, level in enumerate(levels_here):
                row = w_ref[level + 1 : level + 2, :]
                columns[i] = jnp.broadcast_to(row, (depth, length)).T
            total[...] = jnp.zeros_like(total)

        q, g = q_ref[0].astype(F32), g_ref[0]
        acc = sum_ref[0].astype(F32)
        at = 0
        for i, level in enumerate(levels_here):
            state = rest[at][0]
            for part in range(1, len(states[i])):
                state = state + rest[at + part][0]
            at += len(states[i])
            z = dot(g, (state * flag_ref[level]).astype(BF16), NT)
            acc += columns[i] * z
            total[i] += q * z
        out_ref[0] = acc.astype(kind)

        @pl.when(pl.program_id(0) == count - 1)
        def _():
            for i in range(number):
                row_ref[i : i + 1, :] = jnp.sum(total[i].T, axis=0, keepdims=True)

    spec = head_spec(queries.shape, first)
    small = pl.BlockSpec((1, depth, depth), lambda h: (h, 0, 0))
    extra = list(held) + list(deps)
    before = 5 + len(flat)
    aliases = {before: 0} if held else {}
    if not held and kind == sums.dtype:
        aliases = {4: 0}
    return pl.pallas_call(
        kernel,
        grid=(count,),
        in_specs=[smem_spec(), pl.BlockSpec(level_weight.shape, lambda h: (0, 0))]
        + [spec] * 3
        + [small] * len(flat)
        + [any_spec()] * len(extra),
        out_specs=[spec, pl.BlockSpec((number, length), lambda h: (0, 0))],
        out_shape=[
            jax.ShapeDtypeStruct(queries.shape, kind),
            jax.ShapeDtypeStruct((number, length), F32),
        ],
        scratch_shapes=[pltpu.VMEM((number, length, depth), F32)] * 2,
        input_output_aliases=aliases,
        compiler_params=params(),
        cost_estimate=cost(
            number * count * length * depth * depth * 8, count * length * depth * 12
        ),
        name="query_side",
    )(flags, level_weight, queries, out_grad, sums, *flat, *extra)


def key_side(key_rows, value_rows, key_sum, value_sum, parts, held, first, deps):
    _, length, depth = key_rows.shape
    count = parts[0].shape[0]

    def kernel(k_ref, v_ref, ks_ref, vs_ref, *rest):
        k_out, v_out = rest[-2:]
        grad = rest[0][0]
        for part in range(1, len(parts)):
            grad = grad + rest[part][0]
        grad = grad.astype(BF16)
        k_out[0] = (ks_ref[0] + dot(v_ref[0], grad, NT)).astype(BF16)
        v_out[0] = (vs_ref[0] + dot(k_ref[0], grad, NN)).astype(BF16)

    spec = head_spec(key_rows.shape, first)
    small = pl.BlockSpec((1, depth, depth), lambda h: (h, 0, 0))
    extra = list(held) + list(deps)
    before = 4 + len(parts)
    return pl.pallas_call(
        kernel,
        grid=(count,),
        in_specs=[spec] * 4 + [small] * len(parts) + [any_spec()] * len(extra),
        out_specs=[spec] * 2,
        out_shape=[jax.ShapeDtypeStruct(key_rows.shape, BF16)] * 2,
        input_output_aliases={before + i: i for i in range(len(held))},
        compiler_params=params(),
        cost_estimate=cost(count * length * depth * depth * 16, count * length * depth * 16),
        name="key_side",
    )(key_rows, value_rows, key_sum, value_sum, *parts, *extra)


def bit(n, level):
    return n >> level & 1


def state_steps(size, state):
    levels = size.bit_length() - 1
    states = []
    for level in range(levels):
        span = 2**level
        if level == levels - 1 and level >= 1:
            hop = span // 2
            near = [(n, n + hop) for n in range(size) if not bit(n, level) and bit(n, level - 1)]
            far = [(n, n + hop) for n in range(size) if bit(n, level) and not bit(n, level - 1)]
            first = lax.ppermute(state, "ctx", near)
            yield states, first
            second = lax.ppermute(first, "ctx", far)
            states = states + [[first, second]]
            yield states, second
        else:
            if level >= levels - 2:
                pairs = [(n, n + span) for n in range(size) if not bit(n, level)]
            else:
                pairs = [(n, n ^ span) for n in range(size)]
            got = lax.ppermute(state, "ctx", pairs)
            states = states + [[got]]
            if level < levels - 1:
                state = state + got
            yield states, got


def grad_steps(size, grads):
    levels = size.bit_length() - 1
    total = None
    for level in reversed(range(levels)):
        span = 2**level
        if level == levels - 1 and level >= 1:
            hop = span // 2
            far = [(n, n - hop) for n in range(size) if bit(n, level) and bit(n, level - 1)]
            near = [(n, n - hop) for n in range(size) if bit(n, level) and not bit(n, level - 1)]
            got = lax.ppermute(grads[level], "ctx", far)
            yield None, got
            total = lax.ppermute(grads[level] + got, "ctx", near)
            parts = [total]
            yield parts, total
        else:
            if level >= levels - 2:
                pairs = [(n, n - span) for n in range(size) if bit(n, level)]
            else:
                pairs = [(n, n ^ span) for n in range(size)]
            sent = grads[level] if total is None else grads[level] + total
            got = lax.ppermute(sent, "ctx", pairs)
            parts = [got] if total is None else [total, got]
            if level:
                total = got if total is None else total + got
            yield parts, got


def per_device(queries, key_rows, value_rows, level_weight, out_grad):
    size = lax.axis_size("ctx")
    levels = size.bit_length() - 1
    heads, length, depth = queries.shape
    position = lax.axis_index("ctx")
    flags = (position // 2 ** jnp.arange(levels, dtype=jnp.int32) % 2).astype(F32)
    parts = PARTS if heads % PARTS == 0 else 1
    count = heads // parts
    firsts = [part * count for part in range(parts)]
    ups, downs = [], []
    for first in firsts:
        ups.append(state_steps(size, states_of(key_rows, value_rows, first, count, [])))
    for first in firsts:
        grads = state_grads_of(flags, queries, out_grad, level_weight, first, count, [])
        downs.append(grad_steps(size, grads))
    groups = GROUPS if sum(GROUPS) == heads else (1,) * heads
    held, rows, start = [], [], 0
    up_state, down_state = [None] * parts, [None] * parts
    deps = []
    pending = list(groups)
    for step in range(levels + 1 if levels > 1 else levels):
        for part in range(parts):
            if pending:
                many = pending.pop(0)
                *held, row = local_of(
                    level_weight, queries, key_rows, value_rows, out_grad, held, start, many, deps
                )
                rows.append(row)
                start += many
            up_state[part], up_dep = next(ups[part])
            down_state[part], down_dep = next(downs[part])
            deps = [up_dep, down_dep]
    while pending:
        many = pending.pop(0)
        *held, row = local_of(
            level_weight, queries, key_rows, value_rows, out_grad, held, start, many, []
        )
        rows.append(row)
        start += many
    query_sum, key_sum, value_sum = held
    weight_row = sum(rows)
    level_rows = None
    query_out, key_out = [], []
    for part in range(parts):
        grad, some = query_side(
            flags,
            level_weight,
            queries,
            out_grad,
            query_sum,
            up_state[part],
            list(range(levels)),
            query_out,
            BF16,
            firsts[part],
            [],
        )
        query_out = [grad]
        level_rows = some if level_rows is None else level_rows + some
    weight_grad = jnp.concatenate([weight_row, level_rows], axis=0)
    ways = lax.axis_size("head")
    others = [
        lax.ppermute(weight_grad, "head", [(n, (n + shift) % ways) for n in range(ways)])
        for shift in range(1, ways)
    ]
    for other in others:
        weight_grad = weight_grad + other
    for part in range(parts):
        key_out = key_side(
            key_rows, value_rows, key_sum, value_sum, down_state[part], key_out, firsts[part], []
        )
    return query_out[0], key_out[0], key_out[1], weight_grad


def solution(mesh):
    placed = (
        P("head", "ctx", None),
        P("head", "ctx", None),
        P("head", "ctx", None),
        P(None, "ctx"),
        P("head", "ctx", None),
    )
    return jax.shard_map(
        per_device,
        mesh=mesh,
        in_specs=placed,
        out_specs=(
            P("head", "ctx", None),
            P("head", "ctx", None),
            P("head", "ctx", None),
            P(None, "ctx"),
        ),
        check_vma=False,
    )
```

time: 203 us -> 82.9 us (0.41)
  the two profiles are of different devices: /device:TPU:0 before, /device:TPU:24 now
where the time goes in v1:
time: 82.9 us; the launch traced here: 82.5 us
  Pallas kernels  41.3 us (50%)
  starting transfers between devices  26.1 us (31%)
  waiting for transfers between devices  8.93 us (11%)
  local copies, waits for them, and re-layouts  4.07 us (5%)
  other arithmetic  1.14 us (1%)
  between operations  0.95 us (1%)
    pallas_call x6, Pallas kernels, local_of(): pl.pallas_call(kernel, grid=(count,), in_specs=[pl.BlockSpec(level_weight...  20.4 us
    ppermute x4, starting transfers between devices, grad_steps(): got = lax.ppermute(sent, 'ctx', pairs)  9.43 us
    pallas_call x2, Pallas kernels, query_side(): pl.pallas_call(kernel, grid=(count,), in_specs=[smem_spec(), pl.BlockSpec...  8.71 us
    pallas_call x2, Pallas kernels, key_side(): pl.pallas_call(kernel, grid=(count,), in_specs=[spec] * 4 + [small] * len...  4.97 us
    pallas_call x2, Pallas kernels, state_grads_of(): pl.pallas_call(kernel, grid=(count,), in_specs=[smem_spec()] + [head_spec...  4.87 us
    ppermute x4, starting transfers between devices, state_steps(): got = lax.ppermute(state, 'ctx', pairs)  4.75 us
    ppermute x2, waiting for transfers between devices, state_steps(): second = lax.ppermute(first, 'ctx', far)  4.7 us
    unnamed x18, local copies, waits for them, and re-layouts  4.07 us
  transfers between devices with their start and end apart: 19, of which 3 were waited for; matrix products, arithmetic and copies ran while one was open for 0% of the time, Pallas kernels for 47%

profile of v1, /device:TPU:24, one launch (start us, length us, event | category | flops | bytes accessed | tf_op | source)
XLA Modules:
  0.0 82.5 jit_solution(1945929053908661380)
XLA Ops:
  0.7 0.1 fusion.2.flag_ref
  0.8 0.0 copy-start.4
  0.8 1.7 %copy-done.4 = bf16[8,1024,128]{2,1,0:T(8,128)(2,1)S(1)} copy-done((bf16[8,1024,128]{2,1,0:T(8,128)(2,1)S(1)}, bf16[8,1024,128]{2,1,0:T(8,128)(2,1)}, u32[]{:S(2)}) %copy-start.4) | copy-done | bytes 2097176
  2.5 1.6 %copy-done.5 = bf16[8,1024,128]{2,1,0:T(8,128)(2,1)S(1)} copy-done((bf16[8,1024,128]{2,1,0:T(8,128)(2,1)S(1)}, bf16[8,1024,128]{2,1,0:T(8,128)(2,1)}, u32[]{:S(2)}) %copy-start.5) | copy-done | bytes 2097176
  4.1 0.7 copy-done.8
  4.9 2.4 %state_grads.2 = (f32[4,128,128]{2,1,0:T(8,128)S(1)}, f32[4,128,128]{2,1,0:T(8,128)S(1)}, f32[4,128,128]{2,1,0:T(8,128)S(1)}) custom-call(f32[3]{0:T(128)S(1)} %fusion.2.flag_ref, bf16[8,1024,128]{2,1,0:T(8,128)(2,1)S(1)} %copy-done.4, bf16[8,1024,128]{2,1,0:T(8,128)(2,1)S(1)} %copy-done.5, f32[4,1024]{1,0:T(4,128)S(1)} %copy-done.8), custom_call_target="tpu_custom_call" | custom-call | flops 1610612736 | bytes 2097152 | tf_op jit(solution)/shard_map/state_grads/pallas_call | solution.py:78
  7.3 2.4 %collective-permute-start.1 = (f32[4,128,128]{2,1,0:T(8,128)S(1)}, f32[4,128,128]{2,1,0:T(8,128)S(1)}, u32[]{:S(2)}, u32[]{:S(2)}) collective-permute-start(f32[4,128,128]{2,1,0:T(8,128)S(1)} %get-tuple-element.45), channel_id=1, source_target_pairs={{24,16},{28,20},{25,17},{29,21},{26,18},{30,22},{27,19},{31,23}} | collective-permute-start | bytes 786440 | tf_op jit(solution)/shard_map/ppermute | solution.py:284
  9.7 1.2 %states.2 = f32[4,128,128]{2,1,0:T(8,128)S(1)} custom-call(bf16[8,1024,128]{2,1,0:T(8,128)(2,1)S(1)} %copy-done.2, bf16[8,1024,128]{2,1,0:T(8,128)(2,1)S(1)} %copy-done.3), custom_call_target="tpu_custom_call" | custom-call | flops 536870912 | bytes 2097152 | tf_op jit(solution)/shard_map/states/pallas_call | solution.py:47
  10.9 1.6 %collective-permute-start = (f32[4,128,128]{2,1,0:T(8,128)S(1)}, f32[4,128,128]{2,1,0:T(8,128)S(1)}, u32[]{:S(2)}, u32[]{:S(2)}) collective-permute-start(f32[4,128,128]{2,1,0:T(8,128)S(1)} %states.2), channel_id=1, source_target_pairs={{0,4},{4,0},{8,12},{12,8},{16,20},{20,16},{24,28},{28,24},{1,5},{5... | collective-permute-start | bytes 786440 | tf_op jit(solution)/shard_map/ppermute | solution.py:268
  12.4 2.4 %state_grads.3 = (f32[4,128,128]{2,1,0:T(8,128)S(1)}, f32[4,128,128]{2,1,0:T(8,128)S(1)}, f32[4,128,128]{2,1,0:T(8,128)S(1)}) custom-call(f32[3]{0:T(128)S(1)} %fusion.2.flag_ref, bf16[8,1024,128]{2,1,0:T(8,128)(2,1)S(1)} %copy-done.4, bf16[8,1024,128]{2,1,0:T(8,128)(2,1)S(1)} %copy-done.6, f32[4,1024]{1,0:T(4,128)S(1)} %copy-done.8), custom_call_target="tpu_custom_call" | custom-call | flops 1610612736 | bytes 2097152 | tf_op jit(solution)/shard_map/state_grads/pallas_call | solution.py:78
  14.9 1.3 %collective-permute-start.3 = (f32[4,128,128]{2,1,0:T(8,128)S(1)}, f32[4,128,128]{2,1,0:T(8,128)S(1)}, u32[]{:S(2)}, u32[]{:S(2)}) collective-permute-start(f32[4,128,128]{2,1,0:T(8,128)S(1)} %get-tuple-element.49), channel_id=1, source_target_pairs={{24,16},{28,20},{25,17},{29,21},{26,18},{30,22},{27,19},{31,23}} | collective-permute-start | bytes 786440 | tf_op jit(solution)/shard_map/ppermute | solution.py:284
  16.2 1.2 %states.3 = f32[4,128,128]{2,1,0:T(8,128)S(1)} custom-call(bf16[8,1024,128]{2,1,0:T(8,128)(2,1)S(1)} %copy-done.2, bf16[8,1024,128]{2,1,0:T(8,128)(2,1)S(1)} %copy-done.3), custom_call_target="tpu_custom_call" | custom-call | flops 536870912 | bytes 2097152 | tf_op jit(solution)/shard_map/states/pallas_call | solution.py:47
  17.4 0.6 collective-permute-start.2
  18.0 0.7 collective-permute-start.5
  18.7 0.0 collective-permute-done.rest_3_.rest_0_
  18.7 1.3 %collective-permute-start.4 = (f32[4,128,128]{2,1,0:T(8,128)S(1)}, f32[4,128,128]{2,1,0:T(8,128)S(1)}, u32[]{:S(2)}, u32[]{:S(2)}) collective-permute-start(f32[4,128,128]{2,1,0:T(8,128)S(1)} %add.71), channel_id=1, source_target_pairs={{0,8},{4,12},{16,24},{20,28},{1,9},{5,13},{17,25},{21,29},{2,10},{... | collective-permute-start | bytes 786440 | tf_op jit(solution)/shard_map/ppermute | solution.py:268
  20.0 1.4 %collective-permute-done.3.rest_4_ = f32[4,128,128]{2,1,0:T(8,128)S(1)} collective-permute-done((f32[4,128,128]{2,1,0:T(8,128)S(1)}, f32[4,128,128]{2,1,0:T(8,128)S(1)}, u32[]{:S(2)}, u32[]{:S(2)}) %collective-permute-start.3) | collective-permute-done | bytes 262176 | tf_op jit(solution)/shard_map/ppermute | solution.py:284
  21.5 0.7 collective-permute-start.7
  22.2 2.7 %collective-permute-done.2.rest_3_.rest_0_ = f32[4,128,128]{2,1,0:T(8,128)S(1)} collective-permute-done((f32[4,128,128]{2,1,0:T(8,128)S(1)}, f32[4,128,128]{2,1,0:T(8,128)S(1)}, u32[]{:S(2)}, u32[]{:S(2)}) %collective-permute-start.2) | collective-permute-done | bytes 262176 | tf_op jit(solution)/shard_map/ppermute | solution.py:268
  25.0 1.3 %collective-permute-start.6 = (f32[4,128,128]{2,1,0:T(8,128)S(1)}, f32[4,128,128]{2,1,0:T(8,128)S(1)}, u32[]{:S(2)}, u32[]{:S(2)}) collective-permute-start(f32[4,128,128]{2,1,0:T(8,128)S(1)} %add.73), channel_id=1, source_target_pairs={{0,8},{4,12},{16,24},{20,28},{1,9},{5,13},{17,25},{21,29},{2,10},{... | collective-permute-start | bytes 786440 | tf_op jit(solution)/shard_map/ppermute | solution.py:268
  26.3 4.7 %local.6 = (f32[8,1024,128]{2,1,0:T(8,128)S(1)}, f32[8,1024,128]{2,1,0:T(8,128)}, f32[8,1024,128]{2,1,0:T(8,128)}, f32[1,1024]{1,0:T(1,128)S(1)}) custom-call(f32[4,1024]{1,0:T(4,128)S(1)} %copy-done.8, bf16[8,1024,128]{2,1,0:T(8,128)(2,1)S(1)} %copy-done.4, bf16[8,1024,128]{2,1,0:T(8,128)(2,1)S(1)} %copy-done.2, bf16[8,1024,128]{2,1,0:T(8,128)(2,1)S(1)} %copy-done.3, ...), custom_call_target="tpu_custom_call" | custom-call | flops 2684354560 | bytes 5242880 | tf_op jit(solution)/shard_map/local/pallas_call | solution.py:135
  31.0 2.7 %local.7 = (f32[8,1024,128]{2,1,0:T(8,128)S(1)}, f32[8,1024,128]{2,1,0:T(8,128)}, f32[8,1024,128]{2,1,0:T(8,128)}, f32[1,1024]{1,0:T(1,128)S(1)}) custom-call(f32[4,1024]{1,0:T(4,128)S(1)} %copy-done.8, bf16[8,1024,128]{2,1,0:T(8,128)(2,1)S(1)} %copy-done.4, ...), custom_call_target="tpu_custom_call", output_to_operand_aliasing={{0}: (5, {}), {1}: (6, {}), {2}: (7, {})} | custom-call | flops 1342177280 | bytes 2621440 | tf_op jit(solution)/shard_map/local/pallas_call | solution.py:135
  33.7 2.7 %local.8 = (f32[8,1024,128]{2,1,0:T(8,128)S(1)}, f32[8,1024,128]{2,1,0:T(8,128)}, f32[8,1024,128]{2,1,0:T(8,128)}, f32[1,1024]{1,0:T(1,128)S(1)}) custom-call(f32[4,1024]{1,0:T(4,128)S(1)} %copy-done.8, bf16[8,1024,128]{2,1,0:T(8,128)(2,1)S(1)} %copy-done.4, ...), custom_call_target="tpu_custom_call", output_to_operand_aliasing={{0}: (5, {}), {1}: (6, {}), {2}: (7, {})} | custom-call | flops 1342177280 | bytes 2621440 | tf_op jit(solution)/shard_map/local/pallas_call | solution.py:135
  36.4 0.0 collective-permute-done.5.rest_4_
  36.4 4.6 %collective-permute-start.9 = (f32[4,128,128]{2,1,0:T(8,128)S(1)}, f32[4,128,128]{2,1,0:T(8,128)S(1)}, u32[]{:S(2)}, u32[]{:S(2)}) collective-permute-start(f32[4,128,128]{2,1,0:T(8,128)S(1)} %add.76), channel_id=1, source_target_pairs={{8,0},{12,4},{24,16},{28,20},{9,1},{13,5},{25,17},{29,21},{10,2},{... | collective-permute-start | bytes 786440 | tf_op jit(solution)/shard_map/ppermute | solution.py:295
  41.0 0.0 collective-permute-done.4.rest_3_.rest_1_
  41.1 0.7 collective-permute-start.8
  41.8 0.7 collective-permute-start.10
  42.5 0.0 collective-permute-done.7.rest_4_
  42.5 2.7 %collective-permute-start.13 = (f32[4,128,128]{2,1,0:T(8,128)S(1)}, f32[4,128,128]{2,1,0:T(8,128)S(1)}, u32[]{:S(2)}, u32[]{:S(2)}) collective-permute-start(f32[4,128,128]{2,1,0:T(8,128)S(1)} %add.78), channel_id=1, source_target_pairs={{8,0},{12,4},{24,16},{28,20},{9,1},{13,5},{25,17},{29,21},{10,2},{... | collective-permute-start | bytes 786440 | tf_op jit(solution)/shard_map/ppermute | solution.py:295
  45.2 4.7 %local.9 = (f32[8,1024,128]{2,1,0:T(8,128)S(1)}, f32[8,1024,128]{2,1,0:T(8,128)}, f32[8,1024,128]{2,1,0:T(8,128)}, f32[1,1024]{1,0:T(1,128)S(1)}) custom-call(f32[4,1024]{1,0:T(4,128)S(1)} %copy-done.8, bf16[8,1024,128]{2,1,0:T(8,128)(2,1)S(1)} %copy-done.4, ...), custom_call_target="tpu_custom_call", output_to_operand_aliasing={{0}: (5, {}), {1}: (6, {}), {2}: (7, {})} | custom-call | flops 2684354560 | bytes 5242880 | tf_op jit(solution)/shard_map/local/pallas_call | solution.py:135
  49.9 2.8 %local.10 = (f32[8,1024,128]{2,1,0:T(8,128)S(1)}, f32[8,1024,128]{2,1,0:T(8,128)}, f32[8,1024,128]{2,1,0:T(8,128)}, f32[1,1024]{1,0:T(1,128)S(1)}) custom-call(f32[4,1024]{1,0:T(4,128)S(1)} %copy-done.8, bf16[8,1024,128]{2,1,0:T(8,128)(2,1)S(1)} %copy-done.4, ...), custom_call_target="tpu_custom_call", output_to_operand_aliasing={{0}: (5, {}), {1}: (6, {}), {2}: (7, {})} | custom-call | flops 1342177280 | bytes 2621440 | tf_op jit(solution)/shard_map/local/pallas_call | solution.py:135
  52.7 0.0 collective-permute-done.9.rest_4_
  52.8 1.0 %collective-permute-start.15 = (f32[4,128,128]{2,1,0:T(8,128)S(1)}, f32[4,128,128]{2,1,0:T(8,128)S(1)}, u32[]{:S(2)}, u32[]{:S(2)}) collective-permute-start(f32[4,128,128]{2,1,0:T(8,128)S(1)} %get-tuple-element.80), channel_id=1, source_target_pairs={{0,4},{4,0},{8,12},{12,8},{16,20},{20,16},{24,28},{28,24},{1,5},{5... | collective-permute-start | bytes 786440 | tf_op jit(solution)/shard_map/ppermute | solution.py:295
  53.7 0.0 collective-permute-done.13
  53.8 1.2 %collective-permute-start.14 = (f32[4,128,128]{2,1,0:T(8,128)S(1)}, f32[4,128,128]{2,1,0:T(8,128)S(1)}, u32[]{:S(2)}, u32[]{:S(2)}) collective-permute-start(f32[4,128,128]{2,1,0:T(8,128)S(1)} %get-tuple-element.82), channel_id=1, source_target_pairs={{0,4},{4,0},{8,12},{12,8},{16,20},{20,16},{24,28},{28,24},{1,5},{5... | collective-permute-start | bytes 786440 | tf_op jit(solution)/shard_map/ppermute | solution.py:295
  55.0 1.3 %collective-permute-start.12 = (f32[4,128,128]{2,1,0:T(8,128)S(1)}, f32[4,128,128]{2,1,0:T(8,128)S(1)}, u32[]{:S(2)}, u32[]{:S(2)}) collective-permute-start(f32[4,128,128]{2,1,0:T(8,128)S(1)} %collective-permute-done.8.rest_3_.rest_2_), channel_id=1, source_target_pairs={{16,24},{20,28},{17,25},{21,29},{18,26},{22,30},{19,27},{23,31}} | collective-permute-start | bytes 786440 | tf_op jit(solution)/shard_map/ppermute | solution.py:260
  56.3 1.3 %collective-permute-start.11 = (f32[4,128,128]{2,1,0:T(8,128)S(1)}, f32[4,128,128]{2,1,0:T(8,128)S(1)}, u32[]{:S(2)}, u32[]{:S(2)}) collective-permute-start(f32[4,128,128]{2,1,0:T(8,128)S(1)} %collective-permute-done.10.rest_2_), channel_id=1, source_target_pairs={{16,24},{20,28},{17,25},{21,29},{18,26},{22,30},{19,27},{23,31}} | collective-permute-start | bytes 786440 | tf_op jit(solution)/shard_map/ppermute | solution.py:260
  57.6 2.8 %local.11 = (f32[8,1024,128]{2,1,0:T(8,128)S(1)}, f32[8,1024,128]{2,1,0:T(8,128)}, f32[8,1024,128]{2,1,0:T(8,128)}, f32[1,1024]{1,0:T(1,128)S(1)}) custom-call(f32[4,1024]{1,0:T(4,128)S(1)} %copy-done.8, bf16[8,1024,128]{2,1,0:T(8,128)(2,1)S(1)} %copy-done.4, ...), custom_call_target="tpu_custom_call", output_to_operand_aliasing={{0}: (5, {}), {1}: (6, {}), {2}: (7, {})} | custom-call | flops 1342177280 | bytes 2621440 | tf_op jit(solution)/shard_map/local/pallas_call | solution.py:135
  60.4 4.7 %collective-permute-done.12.rest_3_ = f32[4,128,128]{2,1,0:T(8,128)S(1)} collective-permute-done((f32[4,128,128]{2,1,0:T(8,128)S(1)}, f32[4,128,128]{2,1,0:T(8,128)S(1)}, u32[]{:S(2)}, u32[]{:S(2)}) %collective-permute-start.12) | collective-permute-done | bytes 262176 | tf_op jit(solution)/shard_map/ppermute | solution.py:260
  65.1 4.3 %query_side.2 = (bf16[8,1024,128]{2,1,0:T(8,128)(2,1)}, f32[3,1024]{1,0:T(4,128)S(1)}) custom-call(f32[3]{0:T(128)S(1)} %fusion.2.flag_ref, f32[4,1024]{1,0:T(4,128)S(1)} %copy-done.8, bf16[8,1024,128]{2,1,0:T(8,128)(2,1)S(1)} %copy-done.4, bf16[8,1024,128]{2,1,0:T(8,128)(2,1)S(1)} %copy-done.6, f32[8,1024,128]{2,1,0:T(8,128)S(1)} %get-tuple-element.60.sum_ref, ...), custom_call_target="tpu_custom_call" | custom-call | flops 1610612736 | bytes 6291456 | tf_op jit(solution)/shard_map/query_side/pallas_call | solution.py:193
  69.5 4.4 %query_side.3 = (bf16[8,1024,128]{2,1,0:T(8,128)(2,1)}, f32[3,1024]{1,0:T(4,128)S(1)}) custom-call(f32[3]{0:T(128)S(1)} %fusion.2.flag_ref, f32[4,1024]{1,0:T(4,128)S(1)} %copy-done.8, bf16[8,1024,128]{2,1,0:T(8,128)(2,1)S(1)} %copy-done.4, bf16[8,1024,128]{2,1,0:T(8,128)(2,1)S(1)} %copy-done.7, ...), custom_call_target="tpu_custom_call", output_to_operand_aliasing={{0}: (9, {})} | custom-call | flops 1610612736 | bytes 6291456 | tf_op jit(solution)/shard_map/query_side/pallas_call | solution.py:193
  73.9 0.1 collective-permute-start.16
  73.9 1.5 %collective-permute-start.17 = (f32[4,1024]{1,0:T(4,128)S(1)}, f32[4,1024]{1,0:T(4,128)S(1)}, u32[]{:S(2)}, u32[]{:S(2)}) collective-permute-start(f32[4,1024]{1,0:T(4,128)S(1)} %pad_maximum_fusion), channel_id=1, source_target_pairs={{0,2},{1,3},{2,0},{3,1},{4,6},{5,7},{6,4},{7,5},{8,10},{9,11},{10,... | collective-permute-start | bytes 49160 | tf_op jit(solution)/shard_map/ppermute | solution.py:364
  75.5 1.4 %collective-permute-start.18 = (f32[4,1024]{1,0:T(4,128)S(1)}, f32[4,1024]{1,0:T(4,128)S(1)}, u32[]{:S(2)}, u32[]{:S(2)}) collective-permute-start(f32[4,1024]{1,0:T(4,128)S(1)} %pad_maximum_fusion), channel_id=1, source_target_pairs={{0,3},{1,0},{2,1},{3,2},{4,7},{5,4},{6,5},{7,6},{8,11},{9,8},{10,9... | collective-permute-start | bytes 49160 | tf_op jit(solution)/shard_map/ppermute | solution.py:364
  76.9 2.5 %key_side.2 = (bf16[8,1024,128]{2,1,0:T(8,128)(2,1)}, bf16[8,1024,128]{2,1,0:T(8,128)(2,1)}) custom-call(bf16[8,1024,128]{2,1,0:T(8,128)(2,1)S(1)} %copy-done.2, bf16[8,1024,128]{2,1,0:T(8,128)(2,1)S(1)} %copy-done.3, f32[8,1024,128]{2,1,0:T(8,128)S(1)} %copy-done, f32[8,1024,128]{2,1,0:T(8,128)S(1)} %copy-done.1, ...), custom_call_target="tpu_custom_call" | custom-call | flops 1073741824 | bytes 8388608 | tf_op jit(solution)/shard_map/key_side/pallas_call | solution.py:232
  79.4 2.5 %key_side.3 = (bf16[8,1024,128]{2,1,0:T(8,128)(2,1)}, bf16[8,1024,128]{2,1,0:T(8,128)(2,1)}) custom-call(bf16[8,1024,128]{2,1,0:T(8,128)(2,1)S(1)} %copy-done.2, bf16[8,1024,128]{2,1,0:T(8,128)(2,1)S(1)} %copy-done.3, f32[8,1024,128]{2,1,0:T(8,128)S(1)} %copy-done, f32[8,1024,128]{2,1,0:T(8,128)S(1)} %copy-done.1, ...), custom_call_target="tpu_custom_call", output_to_operand_aliasing={{0}: (6, {}), {1}: (7, {})} | custom-call | flops 1073741824 | bytes 8388608 | tf_op jit(solution)/shard_map/key_side/pallas_call | solution.py:232
  81.9 0.6 add_add_fusion
  (37 shorter events, 0.4 us)
Async XLA Ops:
  0.6 9.0 %copy-start.2 = (bf16[8,1024,128]{2,1,0:T(8,128)(2,1)S(1)}, bf16[8,1024,128]{2,1,0:T(8,128)(2,1)}, u32[]{:S(2)}) copy-start(bf16[8,1024,128]{2,1,0:T(8,128)(2,1)} %k_ref.19) | copy-start | bytes 6291460
  0.6 9.0 %copy-start.3 = (bf16[8,1024,128]{2,1,0:T(8,128)(2,1)S(1)}, bf16[8,1024,128]{2,1,0:T(8,128)(2,1)}, u32[]{:S(2)}) copy-start(bf16[8,1024,128]{2,1,0:T(8,128)(2,1)} %v_ref.19) | copy-start | bytes 6291460
  0.8 1.7 %copy-start.4 = (bf16[8,1024,128]{2,1,0:T(8,128)(2,1)S(1)}, bf16[8,1024,128]{2,1,0:T(8,128)(2,1)}, u32[]{:S(2)}) copy-start(bf16[8,1024,128]{2,1,0:T(8,128)(2,1)} %q_ref.19) | copy-start | bytes 6291460
  2.5 1.6 %copy-start.5 = (bf16[8,1024,128]{2,1,0:T(8,128)(2,1)S(1)}, bf16[8,1024,128]{2,1,0:T(8,128)(2,1)}, u32[]{:S(2)}) copy-start(bf16[8,1024,128]{2,1,0:T(8,128)(2,1)} %g_ref.19) | copy-start | bytes 6291460
  4.1 0.7 copy-start.8
  4.9 7.6 %copy-start.6 = (bf16[8,1024,128]{2,1,0:T(8,128)(2,1)S(1)}, bf16[8,1024,128]{2,1,0:T(8,128)(2,1)}, u32[]{:S(2)}) copy-start(bf16[8,1024,128]{2,1,0:T(8,128)(2,1)} %g_ref.19) | copy-start | bytes 6291460
  7.3 10.7 %collective-permute-start.1 = (f32[4,128,128]{2,1,0:T(8,128)S(1)}, f32[4,128,128]{2,1,0:T(8,128)S(1)}, u32[]{:S(2)}, u32[]{:S(2)}) collective-permute-start(f32[4,128,128]{2,1,0:T(8,128)S(1)} %get-tuple-element.45), channel_id=1, source_target_pairs={{24,16},{28,20},{25,17},{29,21},{26,18},{30,22},{27,19},{31,23}} | collective-permute-start | bytes 786440 | tf_op jit(solution)/shard_map/ppermute | solution.py:284
  10.9 7.8 %collective-permute-start = (f32[4,128,128]{2,1,0:T(8,128)S(1)}, f32[4,128,128]{2,1,0:T(8,128)S(1)}, u32[]{:S(2)}, u32[]{:S(2)}) collective-permute-start(f32[4,128,128]{2,1,0:T(8,128)S(1)} %states.2), channel_id=1, source_target_pairs={{0,4},{4,0},{8,12},{12,8},{16,20},{20,16},{24,28},{28,24},{1,5},{5... | collective-permute-start | bytes 786440 | tf_op jit(solution)/shard_map/ppermute | solution.py:268
  14.9 6.6 %collective-permute-start.3 = (f32[4,128,128]{2,1,0:T(8,128)S(1)}, f32[4,128,128]{2,1,0:T(8,128)S(1)}, u32[]{:S(2)}, u32[]{:S(2)}) collective-permute-start(f32[4,128,128]{2,1,0:T(8,128)S(1)} %get-tuple-element.49), channel_id=1, source_target_pairs={{24,16},{28,20},{25,17},{29,21},{26,18},{30,22},{27,19},{31,23}} | collective-permute-start | bytes 786440 | tf_op jit(solution)/shard_map/ppermute | solution.py:284
  17.4 7.6 %collective-permute-start.2 = (f32[4,128,128]{2,1,0:T(8,128)S(1)}, f32[4,128,128]{2,1,0:T(8,128)S(1)}, u32[]{:S(2)}, u32[]{:S(2)}) collective-permute-start(f32[4,128,128]{2,1,0:T(8,128)S(1)} %states.3), channel_id=1, source_target_pairs={{0,4},{4,0},{8,12},{12,8},{16,20},{20,16},{24,28},{28,24},{1,5},{5... | collective-permute-start | bytes 786440 | tf_op jit(solution)/shard_map/ppermute | solution.py:268
  18.0 18.4 %collective-permute-start.5 = (f32[4,128,128]{2,1,0:T(8,128)S(1)}, f32[4,128,128]{2,1,0:T(8,128)S(1)}, u32[]{:S(2)}, u32[]{:S(2)}) collective-permute-start(f32[4,128,128]{2,1,0:T(8,128)S(1)} %add.72), channel_id=1, source_target_pairs={{16,8},{20,12},{17,9},{21,13},{18,10},{22,14},{19,11},{23,15}} | collective-permute-start | bytes 786440 | tf_op jit(solution)/shard_map/ppermute | solution.py:286
  18.7 22.3 %collective-permute-start.4 = (f32[4,128,128]{2,1,0:T(8,128)S(1)}, f32[4,128,128]{2,1,0:T(8,128)S(1)}, u32[]{:S(2)}, u32[]{:S(2)}) collective-permute-start(f32[4,128,128]{2,1,0:T(8,128)S(1)} %add.71), channel_id=1, source_target_pairs={{0,8},{4,12},{16,24},{20,28},{1,9},{5,13},{17,25},{21,29},{2,10},{... | collective-permute-start | bytes 786440 | tf_op jit(solution)/shard_map/ppermute | solution.py:268
  21.5 21.0 %collective-permute-start.7 = (f32[4,128,128]{2,1,0:T(8,128)S(1)}, f32[4,128,128]{2,1,0:T(8,128)S(1)}, u32[]{:S(2)}, u32[]{:S(2)}) collective-permute-start(f32[4,128,128]{2,1,0:T(8,128)S(1)} %add.74), channel_id=1, source_target_pairs={{16,8},{20,12},{17,9},{21,13},{18,10},{22,14},{19,11},{23,15}} | collective-permute-start | bytes 786440 | tf_op jit(solution)/shard_map/ppermute | solution.py:286
  25.0 16.8 %collective-permute-start.6 = (f32[4,128,128]{2,1,0:T(8,128)S(1)}, f32[4,128,128]{2,1,0:T(8,128)S(1)}, u32[]{:S(2)}, u32[]{:S(2)}) collective-permute-start(f32[4,128,128]{2,1,0:T(8,128)S(1)} %add.73), channel_id=1, source_target_pairs={{0,8},{4,12},{16,24},{20,28},{1,9},{5,13},{17,25},{21,29},{2,10},{... | collective-permute-start | bytes 786440 | tf_op jit(solution)/shard_map/ppermute | solution.py:268
  36.4 16.3 %collective-permute-start.9 = (f32[4,128,128]{2,1,0:T(8,128)S(1)}, f32[4,128,128]{2,1,0:T(8,128)S(1)}, u32[]{:S(2)}, u32[]{:S(2)}) collective-permute-start(f32[4,128,128]{2,1,0:T(8,128)S(1)} %add.76), channel_id=1, source_target_pairs={{8,0},{12,4},{24,16},{28,20},{9,1},{13,5},{25,17},{29,21},{10,2},{... | collective-permute-start | bytes 786440 | tf_op jit(solution)/shard_map/ppermute | solution.py:295
  41.1 13.9 %collective-permute-start.8 = (f32[4,128,128]{2,1,0:T(8,128)S(1)}, f32[4,128,128]{2,1,0:T(8,128)S(1)}, u32[]{:S(2)}, u32[]{:S(2)}) collective-permute-start(f32[4,128,128]{2,1,0:T(8,128)S(1)} %add.75), channel_id=1, source_target_pairs={{8,16},{12,20},{9,17},{13,21},{10,18},{14,22},{11,19},{15,23}} | collective-permute-start | bytes 786440 | tf_op jit(solution)/shard_map/ppermute | solution.py:258
  41.8 14.5 %collective-permute-start.10 = (f32[4,128,128]{2,1,0:T(8,128)S(1)}, f32[4,128,128]{2,1,0:T(8,128)S(1)}, u32[]{:S(2)}, u32[]{:S(2)}) collective-permute-start(f32[4,128,128]{2,1,0:T(8,128)S(1)} %add.77), channel_id=1, source_target_pairs={{8,16},{12,20},{9,17},{13,21},{10,18},{14,22},{11,19},{15,23}} | collective-permute-start | bytes 786440 | tf_op jit(solution)/shard_map/ppermute | solution.py:258
  42.5 11.2 %collective-permute-start.13 = (f32[4,128,128]{2,1,0:T(8,128)S(1)}, f32[4,128,128]{2,1,0:T(8,128)S(1)}, u32[]{:S(2)}, u32[]{:S(2)}) collective-permute-start(f32[4,128,128]{2,1,0:T(8,128)S(1)} %add.78), channel_id=1, source_target_pairs={{8,0},{12,4},{24,16},{28,20},{9,1},{13,5},{25,17},{29,21},{10,2},{... | collective-permute-start | bytes 786440 | tf_op jit(solution)/shard_map/ppermute | solution.py:295
  52.8 24.1 %collective-permute-start.15 = (f32[4,128,128]{2,1,0:T(8,128)S(1)}, f32[4,128,128]{2,1,0:T(8,128)S(1)}, u32[]{:S(2)}, u32[]{:S(2)}) collective-permute-start(f32[4,128,128]{2,1,0:T(8,128)S(1)} %get-tuple-element.80), channel_id=1, source_target_pairs={{0,4},{4,0},{8,12},{12,8},{16,20},{20,16},{24,28},{28,24},{1,5},{5... | collective-permute-start | bytes 786440 | tf_op jit(solution)/shard_map/ppermute | solution.py:295
  53.8 25.6 %collective-permute-start.14 = (f32[4,128,128]{2,1,0:T(8,128)S(1)}, f32[4,128,128]{2,1,0:T(8,128)S(1)}, u32[]{:S(2)}, u32[]{:S(2)}) collective-permute-start(f32[4,128,128]{2,1,0:T(8,128)S(1)} %get-tuple-element.82), channel_id=1, source_target_pairs={{0,4},{4,0},{8,12},{12,8},{16,20},{20,16},{24,28},{28,24},{1,5},{5... | collective-permute-start | bytes 786440 | tf_op jit(solution)/shard_map/ppermute | solution.py:295
  55.0 10.1 %collective-permute-start.12 = (f32[4,128,128]{2,1,0:T(8,128)S(1)}, f32[4,128,128]{2,1,0:T(8,128)S(1)}, u32[]{:S(2)}, u32[]{:S(2)}) collective-permute-start(f32[4,128,128]{2,1,0:T(8,128)S(1)} %collective-permute-done.8.rest_3_.rest_2_), channel_id=1, source_target_pairs={{16,24},{20,28},{17,25},{21,29},{18,26},{22,30},{19,27},{23,31}} | collective-permute-start | bytes 786440 | tf_op jit(solution)/shard_map/ppermute | solution.py:260
  56.3 13.2 %collective-permute-start.11 = (f32[4,128,128]{2,1,0:T(8,128)S(1)}, f32[4,128,128]{2,1,0:T(8,128)S(1)}, u32[]{:S(2)}, u32[]{:S(2)}) collective-permute-start(f32[4,128,128]{2,1,0:T(8,128)S(1)} %collective-permute-done.10.rest_2_), channel_id=1, source_target_pairs={{16,24},{20,28},{17,25},{21,29},{18,26},{22,30},{19,27},{23,31}} | collective-permute-start | bytes 786440 | tf_op jit(solution)/shard_map/ppermute | solution.py:260
  65.1 4.3 %copy-start.7 = (bf16[8,1024,128]{2,1,0:T(8,128)(2,1)S(1)}, bf16[8,1024,128]{2,1,0:T(8,128)(2,1)}, u32[]{:S(2)}) copy-start(bf16[8,1024,128]{2,1,0:T(8,128)(2,1)} %g_ref.19) | copy-start | bytes 6291460
  69.4 7.4 %copy-start = (f32[8,1024,128]{2,1,0:T(8,128)S(1)}, f32[8,1024,128]{2,1,0:T(8,128)}, u32[]{:S(2)}) copy-start(f32[8,1024,128]{2,1,0:T(8,128)} %get-tuple-element.63.ks_ref) | copy-start | bytes 12582916
  69.5 7.4 %copy-start.1 = (f32[8,1024,128]{2,1,0:T(8,128)S(1)}, f32[8,1024,128]{2,1,0:T(8,128)}, u32[]{:S(2)}) copy-start(f32[8,1024,128]{2,1,0:T(8,128)} %get-tuple-element.64.vs_ref) | copy-start | bytes 12582916
  73.9 8.0 %collective-permute-start.16 = (f32[4,1024]{1,0:T(4,128)S(1)}, f32[4,1024]{1,0:T(4,128)S(1)}, u32[]{:S(2)}, u32[]{:S(2)}) collective-permute-start(f32[4,1024]{1,0:T(4,128)S(1)} %pad_maximum_fusion), channel_id=1, source_target_pairs={{0,1},{1,2},{2,3},{3,0},{4,5},{5,6},{6,7},{7,4},{8,9},{9,10},{10,1... | collective-permute-start | bytes 49160 | tf_op jit(solution)/shard_map/ppermute | solution.py:364
  73.9 7.9 %collective-permute-start.17 = (f32[4,1024]{1,0:T(4,128)S(1)}, f32[4,1024]{1,0:T(4,128)S(1)}, u32[]{:S(2)}, u32[]{:S(2)}) collective-permute-start(f32[4,1024]{1,0:T(4,128)S(1)} %pad_maximum_fusion), channel_id=1, source_target_pairs={{0,2},{1,3},{2,0},{3,1},{4,6},{5,7},{6,4},{7,5},{8,10},{9,11},{10,... | collective-permute-start | bytes 49160 | tf_op jit(solution)/shard_map/ppermute | solution.py:364
  75.5 6.4 %collective-permute-start.18 = (f32[4,1024]{1,0:T(4,128)S(1)}, f32[4,1024]{1,0:T(4,128)S(1)}, u32[]{:S(2)}, u32[]{:S(2)}) collective-permute-start(f32[4,1024]{1,0:T(4,128)S(1)} %pad_maximum_fusion), channel_id=1, source_target_pairs={{0,3},{1,0},{2,1},{3,2},{4,7},{5,4},{6,5},{7,6},{8,11},{9,8},{10,9... | collective-permute-start | bytes 49160 | tf_op jit(solution)/shard_map/ppermute | solution.py:364

commit v2 on v0

v2 whole, which is shorter than its diff:
```python
import jax
import jax.numpy as jnp
from jax import lax
from jax.experimental import pallas as pl
from jax.experimental.pallas import tpu as pltpu
from jax.sharding import PartitionSpec as P

F32, BF16 = jnp.float32, jnp.bfloat16
NN = (((1,), (0,)), ((), ()))
NT = (((1,), (1,)), ((), ()))
TN = (((0,), (0,)), ((), ()))
VMEM_BYTES = 16 * 2**20
PARTS = (4, 4)
FILL = (1, 2, 1, 1, 1, 1, 1)

INSIDE = pl.BlockSpec(memory_space=pltpu.VMEM)
OUTSIDE = pl.BlockSpec(memory_space=pltpu.HBM)
SCALARS = pl.BlockSpec(memory_space=pltpu.SMEM)
ANYWHERE = pl.BlockSpec(memory_space=pl.ANY)


def dot(a, b, dims):
    return lax.dot_general(a, b, dims, preferred_element_type=F32)


def call(kernel, name, args, specs, outs, out_specs, deps=(), aliases=None, scratch=(), flops=0):
    deps = list(deps)
    count = len(args)

    def body(*refs):
        kernel(*refs[:count], *refs[count + len(deps) :])

    return pl.pallas_call(
        body,
        in_specs=list(specs) + [ANYWHERE] * len(deps),
        out_specs=list(out_specs),
        out_shape=list(outs),
        scratch_shapes=list(scratch),
        input_output_aliases=aliases or {},
        compiler_params=pltpu.CompilerParams(vmem_limit_bytes=VMEM_BYTES),
        cost_estimate=pl.CostEstimate(flops=1, bytes_accessed=1, transcendentals=0),
        name=name,
    )(*args, *deps)


def load_states(key_rows, value_rows, held, first, count, deps):
    shape = key_rows.shape
    depth = shape[2]

    def kernel(k_hbm, v_hbm, *rest):
        k_in, v_in, state, sems = rest[-4:]
        copies = []
        for i in range(count):
            at = first + i
            copies.append(
                (
                    pltpu.make_async_copy(k_hbm.at[at], k_in.at[at], sems.at[0, i]),
                    pltpu.make_async_copy(v_hbm.at[at], v_in.at[at], sems.at[1, i]),
                )
            )
        for pair in copies:
            for copy in pair:
                copy.start()
        for i in range(count):
            for copy in copies[i]:
                copy.wait()
            state[i] = dot(k_in[first + i], v_in[first + i], TN)

    kind = pltpu.VMEM(shape, BF16)
    return call(
        kernel,
        "load_states",
        [key_rows, value_rows, *held],
        [OUTSIDE, OUTSIDE] + [INSIDE] * len(held),
        [kind, kind, jax.ShapeDtypeStruct((count, depth, depth), F32)],
        [INSIDE] * 3,
        deps,
        {2 + i: i for i in range(len(held))},
        [pltpu.SemaphoreType.DMA((2, count))],
        count * shape[1] * depth * depth * 8,
    )


def state_grads(flags, queries, out_grad, level_weight, first, count, deps):
    _, length, depth = queries.shape
    levels = level_weight.shape[0] - 1

    def kernel(flag_ref, q_ref, g_ref, w_ref, *outs):
        for i in range(count):
            turned = g_ref[first + i].T.astype(F32)
            weighted = [
                (w_ref[level + 1 : level + 2, :] * flag_ref[level] * turned).astype(BF16)
                for level in range(levels)
            ]
            grads = dot(jnp.concatenate(weighted, axis=0), q_ref[first + i], NN)
            for level in range(levels):
                outs[level][i] = grads[level * depth : (level + 1) * depth]

    return call(
        kernel,
        "state_grads",
        [flags, queries, out_grad, level_weight],
        [SCALARS] + [INSIDE] * 3,
        [jax.ShapeDtypeStruct((count, depth, depth), F32)] * levels,
        [INSIDE] * levels,
        deps,
        flops=count * length * depth * depth * 16,
    )


def local_head(level_weight, queries, key_rows, value_rows, out_grad, held, at, deps):
    heads, length, depth = queries.shape
    tile = min(256, length)

    def kernel(w_ref, q_ref, k_ref, v_ref, g_ref, *rest):
        lq_ref, lk_ref, lv_ref, lw_ref = rest[-4:]
        k_turned = k_ref[at].T
        for i in range(length // tile):
            upto = (i + 1) * tile
            t = pl.ds(i * tile, tile)
            q, g, w = q_ref[at, t, :], g_ref[at, t, :], w_ref[0:1, t]
            raw = dot(k_ref[at, :upto, :], q, NT)
            d_attn = dot(v_ref[at, :upto, :], g, NT)
            rows = lax.broadcasted_iota(jnp.int32, (upto, tile), 0)
            columns = lax.broadcasted_iota(jnp.int32, (upto, tile), 1) + i * tile
            raw = jnp.where(rows <= columns, raw, 0.0)
            d_attn = jnp.where(rows <= columns, d_attn, 0.0)
            lw_ref[0:1, t] = jnp.sum(raw * d_attn, axis=0, keepdims=True)
            attn = (raw * w).astype(BF16)
            d_raw = (d_attn * w).astype(BF16)
            k_part, v_part = dot(d_raw, q, NN), dot(attn, g, NN)
            lk_ref[at, t, :] = k_part[i * tile :]
            lv_ref[at, t, :] = v_part[i * tile :]
            if i:
                lk_ref[at, : i * tile, :] += k_part[: i * tile]
                lv_ref[at, : i * tile, :] += v_part[: i * tile]
            lq_ref[at, :, t] = dot(k_turned[:, :upto], d_raw, NN)

    return call(
        kernel,
        "local",
        [level_weight, queries, key_rows, value_rows, out_grad, *held],
        [INSIDE] * (5 + len(held)),
        [
            pltpu.VMEM((heads, depth, length), F32),
            pltpu.VMEM(queries.shape, F32),
            pltpu.VMEM(queries.shape, F32),
            jax.ShapeDtypeStruct((1, length), F32),
        ],
        [INSIDE] * 4,
        deps,
        {5 + i: i for i in range(len(held))},
        flops=length * length * depth * 12,
    )


def mix(name, flags, arrays, rule, deps):
    def kernel(flag_ref, *refs):
        refs[-1][...] = rule(flag_ref, [ref[...] for ref in refs[:-1]])

    return call(
        kernel,
        name,
        [flags, *arrays],
        [SCALARS] + [INSIDE] * len(arrays),
        [jax.ShapeDtypeStruct(arrays[0].shape, F32)],
        [INSIDE],
        deps,
    )[0]


def keep(flag, array):
    return jnp.where(flag > 0.0, array, 0.0)


def query_side(flags, level_weight, queries, out_grad, query_sum, states, here, first, out, final, deps):
    shape = queries.shape
    _, length, depth = shape
    count = states[0][0].shape[0]
    flat = [part for parts in states for part in parts]
    levels = level_weight.shape[0] - 1
    number = len(here)

    def kernel(flag_ref, w_ref, q_ref, g_ref, sum_ref, *rest):
        if final:
            out_ref, row_ref, staged, sems = rest[-4:]
        else:
            out_ref, row_ref = rest[-2:]
        copies = []
        rows = [None] * number
        for i in range(count):
            parts, at = [], 0
            for j, level in enumerate(here):
                state = rest[at][i]
                if len(states[j]) > 1:
                    state = jnp.where(flag_ref[levels - 2] > 0.0, rest[at + 1][i], state)
                at += len(states[j])
                parts.append(keep(flag_ref[level], state).astype(BF16))
            z_all = dot(jnp.concatenate(parts, axis=0), g_ref[first + i], NT)
            turned = q_ref[first + i].T.astype(F32)
            total = sum_ref[first + i]
            for j, level in enumerate(here):
                z = z_all[j * depth : (j + 1) * depth]
                total = total + w_ref[level + 1 : level + 2, :] * z
                row = jnp.sum(turned * z, axis=0, keepdims=True)
                rows[j] = row if rows[j] is None else rows[j] + row
            if final:
                staged[i] = total.T.astype(BF16)
                copy = pltpu.make_async_copy(staged.at[i], out_ref.at[first + i], sems.at[i])
                copy.start()
                copies.append(copy)
            else:
                out_ref[first + i] = total
        for j in range(number):
            row_ref[j : j + 1, :] = rows[j]
        for copy in copies:
            copy.wait()

    args = [flags, level_weight, queries, out_grad, query_sum, *flat]
    specs = [SCALARS] + [INSIDE] * (len(args) - 1)
    if final:
        aliases = {len(args): 0} if out else {}
        args, specs = args + list(out), specs + [OUTSIDE] * len(out)
        target = jax.ShapeDtypeStruct(shape, BF16)
        scratch = [pltpu.VMEM((count, length, depth), BF16), pltpu.SemaphoreType.DMA((count,))]
    else:
        aliases = {4: 0}
        target = pltpu.VMEM(query_sum.shape, F32)
        scratch = []
    return call(
        kernel,
        "query_side",
        args,
        specs,
        [target, jax.ShapeDtypeStruct((number, length), F32)],
        [OUTSIDE if final else INSIDE, INSIDE],
        deps,
        aliases,
        scratch,
        number * count * length * depth * depth * 8,
    )


def key_side(flags, key_rows, value_rows, key_sum, value_sum, parts, first, out, deps):
    shape = key_rows.shape
    _, length, depth = shape
    count = parts[0].shape[0]
    levels = flags.shape[0]

    def kernel(flag_ref, k_ref, v_ref, ks_ref, vs_ref, *rest):
        k_out, v_out, staged, sems = rest[-4:]
        copies = []
        for i in range(count):
            grad = gathered(flag_ref, [rest[j][i] for j in range(len(parts))]).astype(BF16)
            at = first + i
            staged[0, i] = (ks_ref[at] + dot(v_ref[at], grad, NN)).astype(BF16)
            staged[1, i] = (vs_ref[at] + dot(k_ref[at], grad, NT)).astype(BF16)
            for j, ref in enumerate((k_out, v_out)):
                copy = pltpu.make_async_copy(staged.at[j, i], ref.at[at], sems.at[j, i])
                copy.start()
                copies.append(copy)
        for copy in copies:
            copy.wait()

    args = [flags, key_rows, value_rows, key_sum, value_sum, *parts]
    return call(
        kernel,
        "key_side",
        args + list(out),
        [SCALARS] + [INSIDE] * (len(args) - 1) + [OUTSIDE] * len(out),
        [jax.ShapeDtypeStruct(shape, BF16)] * 2,
        [OUTSIDE] * 2,
        deps,
        {len(args) + i: i for i in range(len(out))},
        [pltpu.VMEM((2, count, length, depth), BF16), pltpu.SemaphoreType.DMA((2, count))],
        count * length * depth * depth * 16,
    )


def bit(n, level):
    return n >> level & 1


def swaps(size):
    levels = size.bit_length() - 1
    top, low = levels - 1, levels - 2
    up = [[(n, n ^ 2**level) for n in range(size)] for level in range(low)]
    across = [(n, n ^ 2**low) for n in range(size)]
    middle = []
    for n in range(size):
        if bit(n, top) != bit(n, low):
            middle.append((n, n ^ 2**top ^ 2**low))
        else:
            middle.append((n, n ^ 1 if low else size - 1 - n))
    return up + [across, middle, across] + up[::-1]


def gathered(flags, terms):
    levels = flags.shape[0]
    top, low = flags[levels - 1], flags[levels - 2]
    total = jnp.where(low > 0.0, keep(1.0 - top, terms[0]), terms[1])
    for term in terms[2:]:
        total = total + term
    return total


def per_device(queries, key_rows, value_rows, level_weight, out_grad):
    size = lax.axis_size("ctx")
    levels = size.bit_length() - 1
    top, low = levels - 1, levels - 2
    heads, length, depth = queries.shape
    position = lax.axis_index("ctx")
    flags = (position // 2 ** jnp.arange(levels, dtype=jnp.int32) % 2).astype(F32)
    counts = PARTS if sum(PARTS) == heads else (heads,)
    parts = range(len(counts))
    firsts = [sum(counts[:part]) for part in parts]
    steps = swaps(size)

    def inside(array):
        return pltpu.with_memory_space_constraint(array, pltpu.VMEM)

    def outside(array):
        return pltpu.with_memory_space_constraint(array, pltpu.HBM)

    q_in, g_in = inside(queries), inside(out_grad)
    k_out, v_out = outside(key_rows), outside(value_rows)
    w_in = level_weight
    kv, got, grads = [], [[] for _ in parts], [None for _ in parts]
    ups = [None for _ in parts]
    dep = []
    for part in parts:
        *kv, state = load_states(k_out, v_out, kv, firsts[part], counts[part], dep)
        ups[part] = [state]
        dep = [state]
        if low:
            got[part].append(lax.ppermute(state, "ctx", steps[0]))
    k_in, v_in = kv

    held, rows, todo = [], [], list(range(heads))
    early, late = list(parts), list(parts)
    early_rows, late_rows = [], []
    query_out = []

    def make_grads(part, dep):
        grads[part] = state_grads(flags, q_in, g_in, w_in, firsts[part], counts[part], dep)
        return [grads[part][top]]

    def local(dep):
        nonlocal held
        if todo:
            *held, row = local_head(w_in, q_in, k_in, v_in, g_in, held, todo.pop(0), dep)
            rows.append(row)
            dep = [row]
        return dep

    def query(part, here, states, final, dep):
        out, row = query_side(
            flags, w_in, q_in, g_in, held[0], states, here, firsts[part], query_out, final, dep
        )
        if final:
            query_out[:] = [out]
        else:
            held[0] = out
        return row

    def early_query(dep):
        part = early.pop(0)
        row = query(part, list(range(top)), [[got[part][level]] for level in range(top)], False, dep)
        early_rows.append(row)
        return [row]

    def late_query(dep):
        part = late.pop(0)
        row = query(part, [top], [[got[part][top], got[part][top + 1]]], True, dep)
        late_rows.append(row)
        return [row]

    def advance(step, part, dep):
        have, grad = got[part], grads[part]
        if step < low:
            terms = ups[part] + have

            def rule(flag, terms):
                return sum(terms[1:], terms[0])

        elif step == low:
            terms = ups[part] + have + [grad[top]]

            def rule(flag, terms):
                return jnp.where(flag[low] > 0.0, terms[-1], sum(terms[1:-1], terms[0]))

        elif step == low + 1:
            terms = ups[part] + have[:low] + [grad[top], have[low]]

            def rule(flag, terms):
                up = sum(terms[1:-2], terms[0])
                return jnp.where(flag[top] > 0.0, terms[-2], up) + terms[-1]

        elif step == low + 2:
            terms = [grad[low], have[low + 1]]

            def rule(flag, terms):
                other = keep(1.0 - flag[low] * flag[top], terms[1])
                return keep(flag[low], terms[0]) + other

        else:
            level = 2 * low + 2 - step
            terms = [grad[level], *have[low + 1 :]]

            def rule(flag, terms):
                return terms[0] + gathered(flag, terms[1:])

        sent = mix("mix", flags, terms, rule, dep)
        have.append(lax.ppermute(sent, "ctx", steps[step]))
        return [sent]

    for part in parts:
        dep = make_grads(part, dep)
    fill = list(FILL)
    for step in range(1 if low else 0, len(steps)):
        for part in parts:
            for _ in range(fill.pop(0) if fill else 0):
                dep = local(dep)
            dep = advance(step, part, dep)
        if step == low + 2:
            for _ in todo[:]:
                dep = local(dep)
            for _ in parts:
                dep = early_query(dep)
        if step == low + 3:
            for _ in parts:
                dep = late_query(dep)
    while late:
        dep = late_query(dep)

    weight_grad = jnp.concatenate([sum(rows), sum(early_rows), sum(late_rows)], axis=0)
    ways = lax.axis_size("head")
    others = [
        lax.ppermute(weight_grad, "head", [(n, (n + shift) % ways) for n in range(ways)])
        for shift in range(1, ways)
    ]
    key_out = []
    for part in parts:
        key_out = key_side(
            flags, k_in, v_in, held[1], held[2], got[part][low + 1 :], firsts[part], key_out, dep
        )
        dep = []
    for other in others:
        weight_grad = weight_grad + other
    return query_out[0], key_out[0], key_out[1], weight_grad


def solution(mesh):
    placed = (
        P("head", "ctx", None),
        P("head", "ctx", None),
        P("head", "ctx", None),
        P(None, "ctx"),
        P("head", "ctx", None),
    )
    return jax.shard_map(
        per_device,
        mesh=mesh,
        in_specs=placed,
        out_specs=(
            P("head", "ctx", None),
            P("head", "ctx", None),
            P("head", "ctx", None),
            P(None, "ctx"),
        ),
        check_vma=False,
    )
```

time: 203 us -> 66.1 us (0.33)
  matrix products: 121 us -> 0 us
  Pallas kernels: 0 us -> 40 us
  waiting for transfers between devices: 23.5 us -> 3.27 us
  local copies, waits for them, and re-layouts: 22.4 us -> 4.24 us
  starting transfers between devices: 0.08 us -> 16.5 us
  blocking collectives: 13.4 us -> 0 us
  between operations: 14.3 us -> 1.1 us
  other arithmetic: 5.92 us -> 0.82 us
    dot_general x49 -> x0, matrix products: 121 us -> none  [the longest x8 30.8 us: local_block(): jnp.einsum('ts,td->sd', attn, out_grad, preferred_element_type=jnp.float32)]
    pallas_call x0 -> x26, Pallas kernels: none -> 40 us  [call(): pl.pallas_call(body, in_specs=list(specs) + [ANYWHERE] * len(deps), out_s...]
    reduce_scatter x1 -> x0, waiting for transfers between devices: 23.4 us -> none  [per_device(): lax.psum_scatter(total, 'ctx', scatter_dimension=0, tiled=True)[0]]
    unnamed x23 -> x16, local copies, waits for them, and re-layouts: 21.1 us -> 4.24 us
    ppermute x0 -> x13, starting transfers between devices: none -> 16.5 us  [the longest x8 11.4 us: advance(): have.append(lax.ppermute(sent, 'ctx', steps[step]))]
    psum x1 -> x0, blocking collectives: 13.4 us -> none  [per_device(): weight_grad = lax.psum(jnp.stack(weight_rows, axis=0), 'head')]
    ppermute x0 -> x13, waiting for transfers between devices: none -> 3.27 us  [the longest x3 2.66 us: per_device(): lax.ppermute(weight_grad, 'head', [(n, (n + shift) % ways) for n in range...]
    reduce_sum x2 -> x0, other arithmetic: 3.18 us -> none  [the longest x1 3.17 us: per_device(): sums.append(jnp.sum(column[:, None, None, None] * piece, axis=0))]
  transfers between devices with their start and end apart: 2 -> 13, of which waited for: 1 -> 3; matrix products, arithmetic and copies ran while one was open for 63% -> 1% of each run, Pallas kernels for 0% -> 54%
where the time goes in v2:
time: 66.1 us; the launch traced here: 65.9 us
  Pallas kernels  40 us (61%)
  starting transfers between devices  16.5 us (25%)
  local copies, waits for them, and re-layouts  4.24 us (6%)
  waiting for transfers between devices  3.27 us (5%)
  between operations  1.1 us (2%)
  other arithmetic  0.82 us (1%)
    pallas_call x26, Pallas kernels, call(): pl.pallas_call(body, in_specs=list(specs) + [ANYWHERE] * len(deps), out_s...  40 us
    ppermute x8, starting transfers between devices, advance(): have.append(lax.ppermute(sent, 'ctx', steps[step]))  11.4 us
    unnamed x16, local copies, waits for them, and re-layouts  4.24 us
    ppermute x2, starting transfers between devices, per_device(): got[part].append(lax.ppermute(state, 'ctx', steps[0]))  3.07 us
    ppermute x3, waiting for transfers between devices, per_device(): lax.ppermute(weight_grad, 'head', [(n, (n + shift) % ways) for n in range...  2.66 us
    ppermute x3, starting transfers between devices, per_device(): lax.ppermute(weight_grad, 'head', [(n, (n + shift) % ways) for n in range...  2.06 us
  transfers between devices with their start and end apart: 13, of which 3 were waited for; matrix products, arithmetic and copies ran while one was open for 1% of the time, Pallas kernels for 54%

profile of v2, /device:TPU:0, one launch (start us, length us, event | category | flops | bytes accessed | tf_op | source)
XLA Modules:
  0.0 65.9 jit_solution(12125450226027181073)
XLA Ops:
  0.6 2.2 %load_states.2 = (bf16[8,1024,128]{2,1,0:T(8,128)(2,1)S(1)}, bf16[8,1024,128]{2,1,0:T(8,128)(2,1)S(1)}, f32[4,128,128]{2,1,0:T(8,128)S(1)}) custom-call(bf16[8,1024,128]{2,1,0:T(8,128)(2,1)} %refs_0_.11, bf16[8,1024,128]{2,1,0:T(8,128)(2,1)} %refs_1_.17), custom_call_target="tpu_custom_call" | custom-call | flops 1 | bytes 1 | tf_op jit(solution)/shard_map/load_states/pallas_call | solution.py:33
  2.8 3.0 %collective-permute-start = (f32[4,128,128]{2,1,0:T(8,128)S(1)}, f32[4,128,128]{2,1,0:T(8,128)S(1)}, u32[]{:S(2)}, u32[]{:S(2)}) collective-permute-start(f32[4,128,128]{2,1,0:T(8,128)S(1)} %get-tuple-element.62.refs_4_.refs_1_), channel_id=1, source_target_pairs={{0,4},{4,0},{8,12},{12,8},{16,20},{20,16},{24,28},{28,24},{1,5},{5... | collective-permute-start | bytes 786440 | tf_op jit(solution)/shard_map/ppermute | solution.py:336
  5.9 2.3 %load_states.3 = (bf16[8,1024,128]{2,1,0:T(8,128)(2,1)S(1)}, bf16[8,1024,128]{2,1,0:T(8,128)(2,1)S(1)}, f32[4,128,128]{2,1,0:T(8,128)S(1)}) custom-call(bf16[8,1024,128]{2,1,0:T(8,128)(2,1)} %refs_0_.11, bf16[8,1024,128]{2,1,0:T(8,128)(2,1)} %refs_1_.17, ...), custom_call_target="tpu_custom_call", output_to_operand_aliasing={{0}: (2, {}), {1}: (3, {})} | custom-call | flops 1 | bytes 1 | tf_op jit(solution)/shard_map/load_states/pallas_call | solution.py:33
  8.2 0.0 copy-start.3
  8.2 1.3 %copy-done.3 = bf16[8,1024,128]{2,1,0:T(8,128)(2,1)} copy-done((bf16[8,1024,128]{2,1,0:T(8,128)(2,1)}, bf16[8,1024,128]{2,1,0:T(8,128)(2,1)S(1)}, u32[]{:S(2)}) %copy-start.3) | copy-done | bytes 2097176
  9.5 1.3 %copy-done.5 = bf16[8,1024,128]{2,1,0:T(8,128)(2,1)} copy-done((bf16[8,1024,128]{2,1,0:T(8,128)(2,1)}, bf16[8,1024,128]{2,1,0:T(8,128)(2,1)S(1)}, u32[]{:S(2)}) %copy-start.5) | copy-done | bytes 2097176
  10.9 0.0 collective-permute-start.1
  10.9 0.1 fusion.2.refs_0_
  11.1 0.0 copy-start.1
  11.1 1.6 %copy-done.1 = bf16[8,1024,128]{2,1,0:T(8,128)(2,1)S(1)} copy-done((bf16[8,1024,128]{2,1,0:T(8,128)(2,1)S(1)}, bf16[8,1024,128]{2,1,0:T(8,128)(2,1)}, u32[]{:S(2)}) %copy-start.1) | copy-done | bytes 2097176
  12.7 1.6 %state_grads.2 = (f32[4,128,128]{2,1,0:T(8,128)S(1)}, f32[4,128,128]{2,1,0:T(8,128)S(1)}, f32[4,128,128]{2,1,0:T(8,128)S(1)}) custom-call(f32[3]{0:T(128)S(1)} %fusion.2.refs_0_, bf16[8,1024,128]{2,1,0:T(8,128)(2,1)S(1)} %copy-done, bf16[8,1024,128]{2,1,0:T(8,128)(2,1)S(1)} %copy-done.1, f32[4,1024]{1,0:T(4,128)S(1)} %copy-done.7, ...), custom_call_target="tpu_custom_call" | custom-call | flops 1 | bytes 1 | tf_op jit(solution)/shard_map/state_grads/pallas_call | solution.py:33
  14.2 1.6 %state_grads.3 = (f32[4,128,128]{2,1,0:T(8,128)S(1)}, f32[4,128,128]{2,1,0:T(8,128)S(1)}, f32[4,128,128]{2,1,0:T(8,128)S(1)}) custom-call(f32[3]{0:T(128)S(1)} %fusion.2.refs_0_, bf16[8,1024,128]{2,1,0:T(8,128)(2,1)S(1)} %copy-done, bf16[8,1024,128]{2,1,0:T(8,128)(2,1)S(1)} %copy-done.1, f32[4,1024]{1,0:T(4,128)S(1)} %copy-done.7, ...), custom_call_target="tpu_custom_call" | custom-call | flops 1 | bytes 1 | tf_op jit(solution)/shard_map/state_grads/pallas_call | solution.py:33
  15.8 1.9 %local.8 = (f32[8,128,1024]{2,1,0:T(8,128)S(1)}, f32[8,1024,128]{2,1,0:T(8,128)S(1)}, f32[8,1024,128]{2,1,0:T(8,128)S(1)}, f32[1,1024]{1,0:T(1,128)S(1)}) custom-call(f32[4,1024]{1,0:T(4,128)S(1)} %copy-done.7, bf16[8,1024,128]{2,1,0:T(8,128)(2,1)S(1)} %copy-done, bf16[8,1024,128]{2,1,0:T(8,128)(2,1)S(1)} %copy-done.4, bf16[8,1024,128]{2,1,0:T(8,128)(2,1)S(1)} %copy-done.6, ...), custom_call_target="tpu_custom_call" | custom-call | flops 1 | bytes 1 | tf_op jit(solution)/shard_map/local/pallas_call | solution.py:33
  17.7 0.6 mix.8.refs_8_
  18.3 2.1 %collective-permute-start.2 = (f32[4,128,128]{2,1,0:T(8,128)S(1)}, f32[4,128,128]{2,1,0:T(8,128)S(1)}, u32[]{:S(2)}, u32[]{:S(2)}) collective-permute-start(f32[4,128,128]{2,1,0:T(8,128)S(1)} %mix.8.refs_8_), channel_id=1, source_target_pairs={{0,8},{4,12},{8,0},{12,4},{16,24},{20,28},{24,16},{28,20},{1,9},{5... | collective-permute-start | bytes 786440 | tf_op jit(solution)/shard_map/ppermute | solution.py:414
  20.5 1.9 %local.9 = (f32[8,128,1024]{2,1,0:T(8,128)S(1)}, f32[8,1024,128]{2,1,0:T(8,128)S(1)}, f32[8,1024,128]{2,1,0:T(8,128)S(1)}, f32[1,1024]{1,0:T(1,128)S(1)}) custom-call(f32[4,1024]{1,0:T(4,128)S(1)} %copy-done.7, bf16[8,1024,128]{2,1,0:T(8,128)(2,1)S(1)} %copy-done, ...), custom_call_target="tpu_custom_call", output_to_operand_aliasing={{0}: (5, {}), {1}: (6, {}), {2}: (7, {})} | custom-call | flops 1 | bytes 1 | tf_op jit(solution)/shard_map/local/pallas_call | solution.py:33
  22.4 1.9 %local.10 = (f32[8,128,1024]{2,1,0:T(8,128)S(1)}, f32[8,1024,128]{2,1,0:T(8,128)S(1)}, f32[8,1024,128]{2,1,0:T(8,128)S(1)}, f32[1,1024]{1,0:T(1,128)S(1)}) custom-call(f32[4,1024]{1,0:T(4,128)S(1)} %copy-done.7, bf16[8,1024,128]{2,1,0:T(8,128)(2,1)S(1)} %copy-done, ...), custom_call_target="tpu_custom_call", output_to_operand_aliasing={{0}: (5, {}), {1}: (6, {}), {2}: (7, {})} | custom-call | flops 1 | bytes 1 | tf_op jit(solution)/shard_map/local/pallas_call | solution.py:33
  24.2 0.6 mix.9.refs_8_
  24.8 0.1 collective-permute-start.3
  24.9 1.9 %local.11 = (f32[8,128,1024]{2,1,0:T(8,128)S(1)}, f32[8,1024,128]{2,1,0:T(8,128)S(1)}, f32[8,1024,128]{2,1,0:T(8,128)S(1)}, f32[1,1024]{1,0:T(1,128)S(1)}) custom-call(f32[4,1024]{1,0:T(4,128)S(1)} %copy-done.7, bf16[8,1024,128]{2,1,0:T(8,128)(2,1)S(1)} %copy-done, ...), custom_call_target="tpu_custom_call", output_to_operand_aliasing={{0}: (5, {}), {1}: (6, {}), {2}: (7, {})} | custom-call | flops 1 | bytes 1 | tf_op jit(solution)/shard_map/local/pallas_call | solution.py:33
  26.8 0.6 mix.10.refs_8_
  27.4 2.0 %collective-permute-start.4 = (f32[4,128,128]{2,1,0:T(8,128)S(1)}, f32[4,128,128]{2,1,0:T(8,128)S(1)}, u32[]{:S(2)}, u32[]{:S(2)}) collective-permute-start(f32[4,128,128]{2,1,0:T(8,128)S(1)} %mix.10.refs_8_), channel_id=1, source_target_pairs={{0,4},{4,0},{8,16},{12,20},{16,8},{20,12},{24,28},{28,24},{1,5},{5... | collective-permute-start | bytes 786440 | tf_op jit(solution)/shard_map/ppermute | solution.py:414
  29.4 2.1 %local.12 = (f32[8,128,1024]{2,1,0:T(8,128)S(1)}, f32[8,1024,128]{2,1,0:T(8,128)S(1)}, f32[8,1024,128]{2,1,0:T(8,128)S(1)}, f32[1,1024]{1,0:T(1,128)S(1)}) custom-call(f32[4,1024]{1,0:T(4,128)S(1)} %copy-done.7, bf16[8,1024,128]{2,1,0:T(8,128)(2,1)S(1)} %copy-done, ...), custom_call_target="tpu_custom_call", output_to_operand_aliasing={{0}: (5, {}), {1}: (6, {}), {2}: (7, {})} | custom-call | flops 1 | bytes 1 | tf_op jit(solution)/shard_map/local/pallas_call | solution.py:33
  31.5 0.6 collective-permute-done.3.refs_4_.refs_6_
  32.1 0.6 mix.11.refs_8_
  32.7 1.6 %collective-permute-start.5 = (f32[4,128,128]{2,1,0:T(8,128)S(1)}, f32[4,128,128]{2,1,0:T(8,128)S(1)}, u32[]{:S(2)}, u32[]{:S(2)}) collective-permute-start(f32[4,128,128]{2,1,0:T(8,128)S(1)} %mix.11.refs_8_), channel_id=1, source_target_pairs={{0,4},{4,0},{8,16},{12,20},{16,8},{20,12},{24,28},{28,24},{1,5},{5... | collective-permute-start | bytes 786440 | tf_op jit(solution)/shard_map/ppermute | solution.py:414
  34.3 1.9 %local.13 = (f32[8,128,1024]{2,1,0:T(8,128)S(1)}, f32[8,1024,128]{2,1,0:T(8,128)S(1)}, f32[8,1024,128]{2,1,0:T(8,128)S(1)}, f32[1,1024]{1,0:T(1,128)S(1)}) custom-call(f32[4,1024]{1,0:T(4,128)S(1)} %copy-done.7, bf16[8,1024,128]{2,1,0:T(8,128)(2,1)S(1)} %copy-done, ...), custom_call_target="tpu_custom_call", output_to_operand_aliasing={{0}: (5, {}), {1}: (6, {}), {2}: (7, {})} | custom-call | flops 1 | bytes 1 | tf_op jit(solution)/shard_map/local/pallas_call | solution.py:33
  36.2 0.6 mix.12.refs_8_
  36.8 1.7 %collective-permute-start.7 = (f32[4,128,128]{2,1,0:T(8,128)S(1)}, f32[4,128,128]{2,1,0:T(8,128)S(1)}, u32[]{:S(2)}, u32[]{:S(2)}) collective-permute-start(f32[4,128,128]{2,1,0:T(8,128)S(1)} %mix.12.refs_8_), channel_id=1, source_target_pairs={{0,8},{4,12},{8,0},{12,4},{16,24},{20,28},{24,16},{28,20},{1,9},{5... | collective-permute-start | bytes 786440 | tf_op jit(solution)/shard_map/ppermute | solution.py:414
  38.5 1.9 %local.14 = (f32[8,128,1024]{2,1,0:T(8,128)S(1)}, f32[8,1024,128]{2,1,0:T(8,128)S(1)}, f32[8,1024,128]{2,1,0:T(8,128)S(1)}, f32[1,1024]{1,0:T(1,128)S(1)}) custom-call(f32[4,1024]{1,0:T(4,128)S(1)} %copy-done.7, bf16[8,1024,128]{2,1,0:T(8,128)(2,1)S(1)} %copy-done, ...), custom_call_target="tpu_custom_call", output_to_operand_aliasing={{0}: (5, {}), {1}: (6, {}), {2}: (7, {})} | custom-call | flops 1 | bytes 1 | tf_op jit(solution)/shard_map/local/pallas_call | solution.py:33
  40.4 0.6 mix.13.refs_8_
  41.0 1.7 %collective-permute-start.6 = (f32[4,128,128]{2,1,0:T(8,128)S(1)}, f32[4,128,128]{2,1,0:T(8,128)S(1)}, u32[]{:S(2)}, u32[]{:S(2)}) collective-permute-start(f32[4,128,128]{2,1,0:T(8,128)S(1)} %mix.13.refs_8_), channel_id=1, source_target_pairs={{0,8},{4,12},{8,0},{12,4},{16,24},{20,28},{24,16},{28,20},{1,9},{5... | collective-permute-start | bytes 786440 | tf_op jit(solution)/shard_map/ppermute | solution.py:414
  42.7 1.9 %local.15 = (f32[8,128,1024]{2,1,0:T(8,128)S(1)}, f32[8,1024,128]{2,1,0:T(8,128)S(1)}, f32[8,1024,128]{2,1,0:T(8,128)S(1)}, f32[1,1024]{1,0:T(1,128)S(1)}) custom-call(f32[4,1024]{1,0:T(4,128)S(1)} %copy-done.7, bf16[8,1024,128]{2,1,0:T(8,128)(2,1)S(1)} %copy-done, ...), custom_call_target="tpu_custom_call", output_to_operand_aliasing={{0}: (5, {}), {1}: (6, {}), {2}: (7, {})} | custom-call | flops 1 | bytes 1 | tf_op jit(solution)/shard_map/local/pallas_call | solution.py:33
  44.6 1.7 %query_side.4 = (f32[8,128,1024]{2,1,0:T(8,128)S(1)}, f32[2,1024]{1,0:T(2,128)S(1)}) custom-call(f32[3]{0:T(128)S(1)} %fusion.2.refs_0_, f32[4,1024]{1,0:T(4,128)S(1)} %copy-done.7, bf16[8,1024,128]{2,1,0:T(8,128)(2,1)S(1)} %copy-done, bf16[8,1024,128]{2,1,0:T(8,128)(2,1)S(1)} %copy-done.2, ...), custom_call_target="tpu_custom_call", output_to_operand_aliasing={{0}: (4, {})} | custom-call | flops 1 | bytes 1 | tf_op jit(solution)/shard_map/query_side/pallas_call | solution.py:33
  46.3 1.7 %query_side.5 = (f32[8,128,1024]{2,1,0:T(8,128)S(1)}, f32[2,1024]{1,0:T(2,128)S(1)}) custom-call(f32[3]{0:T(128)S(1)} %fusion.2.refs_0_, f32[4,1024]{1,0:T(4,128)S(1)} %copy-done.7, bf16[8,1024,128]{2,1,0:T(8,128)(2,1)S(1)} %copy-done, bf16[8,1024,128]{2,1,0:T(8,128)(2,1)S(1)} %copy-done.2, ...), custom_call_target="tpu_custom_call", output_to_operand_aliasing={{0}: (4, {})} | custom-call | flops 1 | bytes 1 | tf_op jit(solution)/shard_map/query_side/pallas_call | solution.py:33
  48.1 0.6 mix.14.refs_4_
  48.7 1.6 %collective-permute-start.9 = (f32[4,128,128]{2,1,0:T(8,128)S(1)}, f32[4,128,128]{2,1,0:T(8,128)S(1)}, u32[]{:S(2)}, u32[]{:S(2)}) collective-permute-start(f32[4,128,128]{2,1,0:T(8,128)S(1)} %mix.14.refs_4_), channel_id=1, source_target_pairs={{0,4},{4,0},{8,12},{12,8},{16,20},{20,16},{24,28},{28,24},{1,5},{5... | collective-permute-start | bytes 786440 | tf_op jit(solution)/shard_map/ppermute | solution.py:414
  50.3 0.6 mix.15.refs_7_
  50.9 0.6 collective-permute-start.8
  51.4 2.2 %query_side.6 = (bf16[8,1024,128]{2,1,0:T(8,128)(2,1)}, f32[1,1024]{1,0:T(1,128)S(1)}) custom-call(f32[3]{0:T(128)S(1)} %fusion.2.refs_0_, f32[4,1024]{1,0:T(4,128)S(1)} %copy-done.7, bf16[8,1024,128]{2,1,0:T(8,128)(2,1)S(1)} %copy-done, bf16[8,1024,128]{2,1,0:T(8,128)(2,1)S(1)} %copy-done.2, f32[8,128,1024]{2,1,0:T(8,128)S(1)} %get-tuple-element.102.refs_4_, ...), custom_call_target="tpu_custom_call" | custom-call | flops 1 | bytes 1 | tf_op jit(solution)/shard_map/query_side/pallas_call | solution.py:33
  53.7 2.2 %query_side.7 = (bf16[8,1024,128]{2,1,0:T(8,128)(2,1)}, f32[1,1024]{1,0:T(1,128)S(1)}) custom-call(f32[3]{0:T(128)S(1)} %fusion.2.refs_0_, f32[4,1024]{1,0:T(4,128)S(1)} %copy-done.7, bf16[8,1024,128]{2,1,0:T(8,128)(2,1)S(1)} %copy-done, bf16[8,1024,128]{2,1,0:T(8,128)(2,1)S(1)} %copy-done.2, ...), custom_call_target="tpu_custom_call", output_to_operand_aliasing={{0}: (7, {})} | custom-call | flops 1 | bytes 1 | tf_op jit(solution)/shard_map/query_side/pallas_call | solution.py:33
  55.9 1.6 %collective-permute-start.11 = (f32[4,1024]{1,0:T(4,128)S(1)}, f32[4,1024]{1,0:T(4,128)S(1)}, u32[]{:S(2)}, u32[]{:S(2)}) collective-permute-start(f32[4,1024]{1,0:T(4,128)S(1)} %pad_maximum_fusion), channel_id=1, source_target_pairs={{0,2},{1,3},{2,0},{3,1},{4,6},{5,7},{6,4},{7,5},{8,10},{9,11},{10,... | collective-permute-start | bytes 49160 | tf_op jit(solution)/shard_map/ppermute | solution.py:439
  57.5 0.5 collective-permute-start.10
  58.0 1.7 %collective-permute-done.11 = f32[4,1024]{1,0:T(4,128)S(1)} collective-permute-done((f32[4,1024]{1,0:T(4,128)S(1)}, f32[4,1024]{1,0:T(4,128)S(1)}, u32[]{:S(2)}, u32[]{:S(2)}) %collective-permute-start.11) | collective-permute-done | bytes 16416 | tf_op jit(solution)/shard_map/ppermute | solution.py:439
  59.8 0.9 %collective-permute-done.10 = f32[4,1024]{1,0:T(4,128)S(1)} collective-permute-done((f32[4,1024]{1,0:T(4,128)S(1)}, f32[4,1024]{1,0:T(4,128)S(1)}, u32[]{:S(2)}, u32[]{:S(2)}) %collective-permute-start.10) | collective-permute-done | bytes 16416 | tf_op jit(solution)/shard_map/ppermute | solution.py:439
  60.7 0.6 add_add_fusion
  61.3 2.2 %key_side.2 = (bf16[8,1024,128]{2,1,0:T(8,128)(2,1)}, bf16[8,1024,128]{2,1,0:T(8,128)(2,1)}) custom-call(f32[3]{0:T(128)S(1)} %fusion.2.refs_0_, bf16[8,1024,128]{2,1,0:T(8,128)(2,1)S(1)} %copy-done.4, bf16[8,1024,128]{2,1,0:T(8,128)(2,1)S(1)} %copy-done.6, f32[8,1024,128]{2,1,0:T(8,128)S(1)} %get-tuple-element.109.refs_3_, ...), custom_call_target="tpu_custom_call" | custom-call | flops 1 | bytes 1 | tf_op jit(solution)/shard_map/key_side/pallas_call | solution.py:33
  63.5 2.2 %key_side.3 = (bf16[8,1024,128]{2,1,0:T(8,128)(2,1)}, bf16[8,1024,128]{2,1,0:T(8,128)(2,1)}) custom-call(f32[3]{0:T(128)S(1)} %fusion.2.refs_0_, bf16[8,1024,128]{2,1,0:T(8,128)(2,1)S(1)} %copy-done.4, bf16[8,1024,128]{2,1,0:T(8,128)(2,1)S(1)} %copy-done.6, ...), custom_call_target="tpu_custom_call", output_to_operand_aliasing={{0}: (8, {}), {1}: (9, {})} | custom-call | flops 1 | bytes 1 | tf_op jit(solution)/shard_map/key_side/pallas_call | solution.py:33
  (26 shorter events, 0.1 us)
Async XLA Ops:
  2.8 14.9 %collective-permute-start = (f32[4,128,128]{2,1,0:T(8,128)S(1)}, f32[4,128,128]{2,1,0:T(8,128)S(1)}, u32[]{:S(2)}, u32[]{:S(2)}) collective-permute-start(f32[4,128,128]{2,1,0:T(8,128)S(1)} %get-tuple-element.62.refs_4_.refs_1_), channel_id=1, source_target_pairs={{0,4},{4,0},{8,12},{12,8},{16,20},{20,16},{24,28},{28,24},{1,5},{5... | collective-permute-start | bytes 786440 | tf_op jit(solution)/shard_map/ppermute | solution.py:336
  5.9 5.2 %copy-start = (bf16[8,1024,128]{2,1,0:T(8,128)(2,1)S(1)}, bf16[8,1024,128]{2,1,0:T(8,128)(2,1)}, u32[]{:S(2)}) copy-start(bf16[8,1024,128]{2,1,0:T(8,128)(2,1)} %refs_2_.11) | copy-start | bytes 6291460
  5.9 5.2 %copy-start.7 = (f32[4,1024]{1,0:T(4,128)S(1)}, f32[4,1024]{1,0:T(4,128)}, u32[]{:S(2)}) copy-start(f32[4,1024]{1,0:T(4,128)} %refs_1_.31) | copy-start | bytes 49156
  8.2 1.3 %copy-start.3 = (bf16[8,1024,128]{2,1,0:T(8,128)(2,1)}, bf16[8,1024,128]{2,1,0:T(8,128)(2,1)S(1)}, u32[]{:S(2)}) copy-start(bf16[8,1024,128]{2,1,0:T(8,128)(2,1)S(1)} %get-tuple-element.63.refs_2_.refs_1_) | copy-start | bytes 6291460
  9.5 1.3 %copy-start.5 = (bf16[8,1024,128]{2,1,0:T(8,128)(2,1)}, bf16[8,1024,128]{2,1,0:T(8,128)(2,1)S(1)}, u32[]{:S(2)}) copy-start(bf16[8,1024,128]{2,1,0:T(8,128)(2,1)S(1)} %get-tuple-element.64.refs_3_.refs_2_) | copy-start | bytes 6291460
  10.9 13.4 %collective-permute-start.1 = (f32[4,128,128]{2,1,0:T(8,128)S(1)}, f32[4,128,128]{2,1,0:T(8,128)S(1)}, u32[]{:S(2)}, u32[]{:S(2)}) collective-permute-start(f32[4,128,128]{2,1,0:T(8,128)S(1)} %get-tuple-element.65.refs_4_.refs_1_), channel_id=1, source_target_pairs={{0,4},{4,0},{8,12},{12,8},{16,20},{20,16},{24,28},{28,24},{1,5},{5... | collective-permute-start | bytes 786440 | tf_op jit(solution)/shard_map/ppermute | solution.py:336
  11.1 1.6 %copy-start.1 = (bf16[8,1024,128]{2,1,0:T(8,128)(2,1)S(1)}, bf16[8,1024,128]{2,1,0:T(8,128)(2,1)}, u32[]{:S(2)}) copy-start(bf16[8,1024,128]{2,1,0:T(8,128)(2,1)} %refs_3_.11) | copy-start | bytes 6291460
  12.6 3.2 %copy-start.2 = (bf16[8,1024,128]{2,1,0:T(8,128)(2,1)S(1)}, bf16[8,1024,128]{2,1,0:T(8,128)(2,1)}, u32[]{:S(2)}) copy-start(bf16[8,1024,128]{2,1,0:T(8,128)(2,1)} %refs_3_.11) | copy-start | bytes 6291460
  12.6 3.2 %copy-start.4 = (bf16[8,1024,128]{2,1,0:T(8,128)(2,1)S(1)}, bf16[8,1024,128]{2,1,0:T(8,128)(2,1)}, u32[]{:S(2)}) copy-start(bf16[8,1024,128]{2,1,0:T(8,128)(2,1)} %copy-done.3) | copy-start | bytes 6291460
  12.6 3.2 %copy-start.6 = (bf16[8,1024,128]{2,1,0:T(8,128)(2,1)S(1)}, bf16[8,1024,128]{2,1,0:T(8,128)(2,1)}, u32[]{:S(2)}) copy-start(bf16[8,1024,128]{2,1,0:T(8,128)(2,1)} %copy-done.5) | copy-start | bytes 6291460
  18.3 8.5 %collective-permute-start.2 = (f32[4,128,128]{2,1,0:T(8,128)S(1)}, f32[4,128,128]{2,1,0:T(8,128)S(1)}, u32[]{:S(2)}, u32[]{:S(2)}) collective-permute-start(f32[4,128,128]{2,1,0:T(8,128)S(1)} %mix.8.refs_8_), channel_id=1, source_target_pairs={{0,8},{4,12},{8,0},{12,4},{16,24},{20,28},{24,16},{28,20},{1,9},{5... | collective-permute-start | bytes 786440 | tf_op jit(solution)/shard_map/ppermute | solution.py:414
  24.8 7.3 %collective-permute-start.3 = (f32[4,128,128]{2,1,0:T(8,128)S(1)}, f32[4,128,128]{2,1,0:T(8,128)S(1)}, u32[]{:S(2)}, u32[]{:S(2)}) collective-permute-start(f32[4,128,128]{2,1,0:T(8,128)S(1)} %mix.9.refs_8_), channel_id=1, source_target_pairs={{0,8},{4,12},{8,0},{12,4},{16,24},{20,28},{24,16},{28,20},{1,9},{5... | collective-permute-start | bytes 786440 | tf_op jit(solution)/shard_map/ppermute | solution.py:414
  27.4 8.8 %collective-permute-start.4 = (f32[4,128,128]{2,1,0:T(8,128)S(1)}, f32[4,128,128]{2,1,0:T(8,128)S(1)}, u32[]{:S(2)}, u32[]{:S(2)}) collective-permute-start(f32[4,128,128]{2,1,0:T(8,128)S(1)} %mix.10.refs_8_), channel_id=1, source_target_pairs={{0,4},{4,0},{8,16},{12,20},{16,8},{20,12},{24,28},{28,24},{1,5},{5... | collective-permute-start | bytes 786440 | tf_op jit(solution)/shard_map/ppermute | solution.py:414
  32.7 7.7 %collective-permute-start.5 = (f32[4,128,128]{2,1,0:T(8,128)S(1)}, f32[4,128,128]{2,1,0:T(8,128)S(1)}, u32[]{:S(2)}, u32[]{:S(2)}) collective-permute-start(f32[4,128,128]{2,1,0:T(8,128)S(1)} %mix.11.refs_8_), channel_id=1, source_target_pairs={{0,4},{4,0},{8,16},{12,20},{16,8},{20,12},{24,28},{28,24},{1,5},{5... | collective-permute-start | bytes 786440 | tf_op jit(solution)/shard_map/ppermute | solution.py:414
  36.8 11.2 %collective-permute-start.7 = (f32[4,128,128]{2,1,0:T(8,128)S(1)}, f32[4,128,128]{2,1,0:T(8,128)S(1)}, u32[]{:S(2)}, u32[]{:S(2)}) collective-permute-start(f32[4,128,128]{2,1,0:T(8,128)S(1)} %mix.12.refs_8_), channel_id=1, source_target_pairs={{0,8},{4,12},{8,0},{12,4},{16,24},{20,28},{24,16},{28,20},{1,9},{5... | collective-permute-start | bytes 786440 | tf_op jit(solution)/shard_map/ppermute | solution.py:414
  41.0 9.2 %collective-permute-start.6 = (f32[4,128,128]{2,1,0:T(8,128)S(1)}, f32[4,128,128]{2,1,0:T(8,128)S(1)}, u32[]{:S(2)}, u32[]{:S(2)}) collective-permute-start(f32[4,128,128]{2,1,0:T(8,128)S(1)} %mix.13.refs_8_), channel_id=1, source_target_pairs={{0,8},{4,12},{8,0},{12,4},{16,24},{20,28},{24,16},{28,20},{1,9},{5... | collective-permute-start | bytes 786440 | tf_op jit(solution)/shard_map/ppermute | solution.py:414
  48.7 12.6 %collective-permute-start.9 = (f32[4,128,128]{2,1,0:T(8,128)S(1)}, f32[4,128,128]{2,1,0:T(8,128)S(1)}, u32[]{:S(2)}, u32[]{:S(2)}) collective-permute-start(f32[4,128,128]{2,1,0:T(8,128)S(1)} %mix.14.refs_4_), channel_id=1, source_target_pairs={{0,4},{4,0},{8,12},{12,8},{16,20},{20,16},{24,28},{28,24},{1,5},{5... | collective-permute-start | bytes 786440 | tf_op jit(solution)/shard_map/ppermute | solution.py:414
  50.9 12.7 %collective-permute-start.8 = (f32[4,128,128]{2,1,0:T(8,128)S(1)}, f32[4,128,128]{2,1,0:T(8,128)S(1)}, u32[]{:S(2)}, u32[]{:S(2)}) collective-permute-start(f32[4,128,128]{2,1,0:T(8,128)S(1)} %mix.15.refs_7_), channel_id=1, source_target_pairs={{0,4},{4,0},{8,12},{12,8},{16,20},{20,16},{24,28},{28,24},{1,5},{5... | collective-permute-start | bytes 786440 | tf_op jit(solution)/shard_map/ppermute | solution.py:414
  55.9 3.8 %collective-permute-start.11 = (f32[4,1024]{1,0:T(4,128)S(1)}, f32[4,1024]{1,0:T(4,128)S(1)}, u32[]{:S(2)}, u32[]{:S(2)}) collective-permute-start(f32[4,1024]{1,0:T(4,128)S(1)} %pad_maximum_fusion), channel_id=1, source_target_pairs={{0,2},{1,3},{2,0},{3,1},{4,6},{5,7},{6,4},{7,5},{8,10},{9,11},{10,... | collective-permute-start | bytes 49160 | tf_op jit(solution)/shard_map/ppermute | solution.py:439
  57.5 2.3 %collective-permute-start.12 = (f32[4,1024]{1,0:T(4,128)S(1)}, f32[4,1024]{1,0:T(4,128)S(1)}, u32[]{:S(2)}, u32[]{:S(2)}) collective-permute-start(f32[4,1024]{1,0:T(4,128)S(1)} %pad_maximum_fusion), channel_id=1, source_target_pairs={{0,3},{1,0},{2,1},{3,2},{4,7},{5,4},{6,5},{7,6},{8,11},{9,8},{10,9... | collective-permute-start | bytes 49160 | tf_op jit(solution)/shard_map/ppermute | solution.py:439
  57.5 3.2 %collective-permute-start.10 = (f32[4,1024]{1,0:T(4,128)S(1)}, f32[4,1024]{1,0:T(4,128)S(1)}, u32[]{:S(2)}, u32[]{:S(2)}) collective-permute-start(f32[4,1024]{1,0:T(4,128)S(1)} %pad_maximum_fusion), channel_id=1, source_target_pairs={{0,1},{1,2},{2,3},{3,0},{4,5},{5,6},{6,7},{7,4},{8,9},{9,10},{10,1... | collective-permute-start | bytes 49160 | tf_op jit(solution)/shard_map/ppermute | solution.py:439

commit v3 on v2

v3 whole, which is shorter than its diff:
```python
import jax
import jax.numpy as jnp
from jax import lax
from jax.experimental import pallas as pl
from jax.experimental.pallas import tpu as pltpu
from jax.sharding import PartitionSpec as P

F32, BF16 = jnp.float32, jnp.bfloat16
NN = (((1,), (0,)), ((), ()))
NT = (((1,), (1,)), ((), ()))
TN = (((0,), (0,)), ((), ()))
VMEM_BYTES = 16 * 2**20
PARTS = (4, 4)
FILL = (0, 1, 1, 1, 2, 1, 2, 0)

INSIDE = pl.BlockSpec(memory_space=pltpu.VMEM)
OUTSIDE = pl.BlockSpec(memory_space=pltpu.HBM)
ANYWHERE = pl.BlockSpec(memory_space=pl.ANY)


def dot(a, b, dims):
    return lax.dot_general(a, b, dims, preferred_element_type=F32)


def block_bits(levels):
    position = lax.axis_index("ctx")
    return [(position >> level & 1) == 1 for level in range(levels)]


def inside(array):
    return pltpu.with_memory_space_constraint(array, pltpu.VMEM)


def outside(array):
    return pltpu.with_memory_space_constraint(array, pltpu.HBM)


def call(kernel, name, args, specs, outs, out_specs, deps=(), aliases=None, scratch=()):
    deps = list(deps)
    count = len(args)
    args = [
        inside(arg) if spec is INSIDE else outside(arg) if spec is OUTSIDE else arg
        for arg, spec in zip(args, specs, strict=True)
    ]

    def body(*refs):
        kernel(*refs[:count], *refs[count + len(deps) :])

    return pl.pallas_call(
        body,
        in_specs=list(specs) + [ANYWHERE] * len(deps),
        out_specs=list(out_specs),
        out_shape=list(outs),
        scratch_shapes=list(scratch),
        input_output_aliases=aliases or {},
        compiler_params=pltpu.CompilerParams(vmem_limit_bytes=VMEM_BYTES),
        cost_estimate=pl.CostEstimate(flops=1, bytes_accessed=1, transcendentals=0),
        name=name,
    )(*args, *deps)


def load_states(pairs, held, first, count, deps):
    shape = pairs[0].shape
    depth = shape[2]
    number = len(pairs)

    def kernel(*refs):
        sems = refs[-1]
        state = refs[-2]
        inner = refs[-2 - number : -2]
        halves = [(0, count // 2), (count // 2, count)] if count > 1 else [(0, 1)]
        copies = []
        for half, (start, stop) in enumerate(halves):
            at = pl.ds(first + start, stop - start)
            for j in range(2):
                copies.append(
                    pltpu.make_async_copy(refs[j].at[at], inner[j].at[at], sems.at[j, half])
                )
        for j in range(2, number):
            copies.append(pltpu.make_async_copy(refs[j], inner[j], sems.at[j, 0]))
        for copy in copies:
            copy.start()
        for half, (start, stop) in enumerate(halves):
            copies[2 * half].wait()
            copies[2 * half + 1].wait()
            for i in range(start, stop):
                state[i] = dot(inner[0][first + i], inner[1][first + i], TN)
        for copy in copies[2 * len(halves) :]:
            copy.wait()

    kind = pltpu.VMEM(shape, BF16)
    return call(
        kernel,
        "load_states",
        [*pairs, *held],
        [OUTSIDE] * number + [INSIDE] * len(held),
        [kind] * number + [jax.ShapeDtypeStruct((count, depth, depth), F32)],
        [INSIDE] * (number + 1),
        deps,
        {number + i: i for i in range(len(held))},
        [pltpu.SemaphoreType.DMA((number, 2))],
    )


def state_grads(queries, out_grad, level_weight, first, count, deps):
    _, length, depth = queries.shape
    levels = level_weight.shape[0] - 1

    def kernel(q_ref, g_ref, w_ref, *outs):
        bits = block_bits(levels)
        for i in range(count):
            turned = g_ref[first + i].T.astype(F32)
            weighted = [
                (keep(bits[level], w_ref[level + 1 : level + 2, :]) * turned).astype(BF16)
                for level in range(levels)
            ]
            grads = dot(jnp.concatenate(weighted, axis=0), q_ref[first + i], NN)
            for level in range(levels):
                outs[level][i] = grads[level * depth : (level + 1) * depth]

    return call(
        kernel,
        "state_grads",
        [queries, out_grad, level_weight],
        [INSIDE] * 3,
        [jax.ShapeDtypeStruct((count, depth, depth), F32)] * levels,
        [INSIDE] * levels,
        deps,
    )


def local_head(level_weight, queries, key_rows, value_rows, out_grad, held, at, deps):
    heads, length, depth = queries.shape
    tile = min(256, length)

    def kernel(w_ref, q_ref, k_ref, v_ref, g_ref, *rest):
        lq_ref, lk_ref, lv_ref, lw_ref = rest[-4:]
        k_turned = k_ref[at].T
        for i in range(length // tile):
            upto = (i + 1) * tile
            t = pl.ds(i * tile, tile)
            q, g, w = q_ref[at, t, :], g_ref[at, t, :], w_ref[0:1, t]
            raw = dot(k_ref[at, :upto, :], q, NT)
            d_attn = dot(v_ref[at, :upto, :], g, NT)
            rows = lax.broadcasted_iota(jnp.int32, (upto, tile), 0)
            columns = lax.broadcasted_iota(jnp.int32, (upto, tile), 1) + i * tile
            raw = jnp.where(rows <= columns, raw, 0.0)
            d_attn = jnp.where(rows <= columns, d_attn, 0.0)
            lw_ref[0:1, t] = jnp.sum(raw * d_attn, axis=0, keepdims=True)
            attn = (raw * w).astype(BF16)
            d_raw = (d_attn * w).astype(BF16)
            k_part, v_part = dot(d_raw, q, NN), dot(attn, g, NN)
            lk_ref[at, t, :] = k_part[i * tile :]
            lv_ref[at, t, :] = v_part[i * tile :]
            if i:
                lk_ref[at, : i * tile, :] += k_part[: i * tile]
                lv_ref[at, : i * tile, :] += v_part[: i * tile]
            lq_ref[at, :, t] = dot(k_turned[:, :upto], d_raw, NN)

    return call(
        kernel,
        "local",
        [level_weight, queries, key_rows, value_rows, out_grad, *held],
        [INSIDE] * (5 + len(held)),
        [
            pltpu.VMEM((heads, depth, length), F32),
            pltpu.VMEM(queries.shape, F32),
            pltpu.VMEM(queries.shape, F32),
            jax.ShapeDtypeStruct((1, length), F32),
        ],
        [INSIDE] * 4,
        deps,
        {5 + i: i for i in range(len(held))},
    )


def mix(levels, arrays, rule, deps):
    def kernel(*refs):
        refs[-1][...] = rule(block_bits(levels), [ref[...] for ref in refs[:-1]])

    return call(
        kernel,
        "mix",
        arrays,
        [INSIDE] * len(arrays),
        [jax.ShapeDtypeStruct(arrays[0].shape, F32)],
        [INSIDE],
        deps,
    )[0]


def keep(flag, array):
    return jnp.where(flag, array, 0.0)


def query_side(level_weight, queries, out_grad, query_sum, states, rows, first, out, deps):
    shape = queries.shape
    _, length, depth = shape
    count = states[0].shape[0]
    levels = len(states) - 1
    single, whole = rows

    def kernel(w_ref, q_ref, g_ref, sum_ref, *rest):
        state_refs = rest[: levels + 1]
        singles = rest[levels + 1 : levels + 1 + len(single)]
        wholes = rest[levels + 1 + len(single) : levels + 1 + len(single) + len(whole)]
        out_ref, row_ref, staged, sems = rest[-4:]
        bits = block_bits(levels)
        copies = []
        totals = [None] * levels

        def product(i):
            parts = [state_refs[level][i] for level in range(levels)]
            parts[-1] = jnp.where(bits[levels - 2], state_refs[levels][i], parts[-1])
            parts = [keep(bit_here, part).astype(BF16) for bit_here, part in zip(bits, parts, strict=True)]
            return dot(jnp.concatenate(parts, axis=0), g_ref[first + i], NT)

        later = product(0)
        for i in range(count):
            z_all = later
            if i + 1 < count:
                later = product(i + 1)
            turned = q_ref[first + i].T.astype(F32)
            total = sum_ref[first + i]
            for level in range(levels):
                z = z_all[level * depth : (level + 1) * depth]
                total = total + w_ref[level + 1 : level + 2, :] * z
                row = jnp.sum(turned * z, axis=0, keepdims=True)
                totals[level] = row if totals[level] is None else totals[level] + row
            staged[i] = total.T.astype(BF16)
            copy = pltpu.make_async_copy(staged.at[i], out_ref.at[first + i], sems.at[i])
            copy.start()
            copies.append(copy)
        own = None
        for ref in singles:
            own = ref[...] if own is None else own + ref[...]
        for ref in wholes:
            own = ref[0:1, :] if own is None else own + ref[0:1, :]
            for level in range(levels):
                totals[level] += ref[level + 1 : level + 2, :]
        row_ref[0:1, :] = own
        for level in range(levels):
            row_ref[level + 1 : level + 2, :] = totals[level]
        for copy in copies:
            copy.wait()

    args = [level_weight, queries, out_grad, query_sum, *states, *single, *whole]
    return call(
        kernel,
        "query_side",
        args + list(out),
        [INSIDE] * len(args) + [OUTSIDE] * len(out),
        [jax.ShapeDtypeStruct(shape, BF16), jax.ShapeDtypeStruct((levels + 1, length), F32)],
        [OUTSIDE, INSIDE],
        deps,
        {len(args): 0} if out else {},
        [pltpu.VMEM((count, length, depth), BF16), pltpu.SemaphoreType.DMA((count,))],
    )


def key_side(key_rows, value_rows, key_sum, value_sum, parts, levels, rows, first, out, deps):
    shape = key_rows.shape
    _, length, depth = shape
    count = parts[0].shape[0]
    summed = [jax.ShapeDtypeStruct(rows[0].shape, F32)] if rows else []

    def kernel(k_ref, v_ref, ks_ref, vs_ref, *rest):
        k_out, v_out = rest[len(parts) + len(rows) + len(out) :][:2]
        staged, sems = rest[-2 - 2 * len(summed) :][:2]
        bits = block_bits(levels)
        copies = []
        if rows:
            total = rest[len(parts)][...]
            for ref in rest[len(parts) + 1 : len(parts) + len(rows)]:
                total = total + ref[...]
            rest[-2][...] = total
            copies.append(pltpu.make_async_copy(rest[-2], rest[-5], rest[-1]))
            copies[0].start()

        def products(i):
            grad = gathered(bits, [rest[j][i] for j in range(len(parts))]).astype(BF16)
            return dot(v_ref[first + i], grad, NN), dot(k_ref[first + i], grad, NT)

        later = products(0)
        for i in range(count):
            added = later
            if i + 1 < count:
                later = products(i + 1)
            at = first + i
            for j, (ref, sum_ref) in enumerate(((k_out, ks_ref), (v_out, vs_ref))):
                staged[j, i] = (sum_ref[at] + added[j]).astype(BF16)
                copy = pltpu.make_async_copy(staged.at[j, i], ref.at[at], sems.at[j, i])
                copy.start()
                copies.append(copy)
        for copy in copies:
            copy.wait()

    args = [key_rows, value_rows, key_sum, value_sum, *parts, *rows]
    return call(
        kernel,
        "key_side",
        args + list(out),
        [INSIDE] * len(args) + [OUTSIDE] * len(out),
        [jax.ShapeDtypeStruct(shape, BF16)] * 2 + summed,
        [OUTSIDE] * (2 + len(summed)),
        deps,
        {len(args) + i: i for i in range(len(out))},
        [pltpu.VMEM((2, count, length, depth), BF16), pltpu.SemaphoreType.DMA((2, count))]
        + ([pltpu.VMEM(rows[0].shape, F32), pltpu.SemaphoreType.DMA] if rows else []),
    )


def bit(n, level):
    return n >> level & 1


def swaps(size):
    levels = size.bit_length() - 1
    top, low = levels - 1, levels - 2
    up = [[(n, n ^ 2**level) for n in range(size)] for level in range(low)]
    across = [(n, n ^ 2**low) for n in range(size)]
    middle = []
    for n in range(size):
        if bit(n, top) != bit(n, low):
            middle.append((n, n ^ 2**top ^ 2**low))
        else:
            middle.append((n, n ^ 1 if low else size - 1 - n))
    return up + [across, middle, across] + up[::-1]


def gathered(bits, terms):
    top, low = bits[-1], bits[-2]
    total = jnp.where(low, keep(~top, terms[0]), terms[1])
    for term in terms[2:]:
        total = total + term
    return total


def per_device(queries, key_rows, value_rows, level_weight, out_grad):
    size = lax.axis_size("ctx")
    levels = size.bit_length() - 1
    top, low = levels - 1, levels - 2
    heads = queries.shape[0]
    counts = PARTS if sum(PARTS) == heads else (heads,)
    parts = range(len(counts))
    firsts = [sum(counts[:part]) for part in parts]
    steps = swaps(size)
    w_in = level_weight
    got, grads, ups = [[] for _ in parts], [None for _ in parts], [None for _ in parts]
    inner, dep = [], []
    for part in parts:
        more = part == parts[-1]
        pairs = [key_rows, value_rows] + ([queries, out_grad] if more else [])
        *inner, state = load_states(pairs, inner, firsts[part], counts[part], dep)
        ups[part] = [state]
        dep = [state]
        if low:
            got[part].append(lax.ppermute(state, "ctx", steps[0]))
    k_in, v_in, q_in, g_in = inner

    held, rows, todo = [], [], list(range(heads))

    def local(dep):
        nonlocal held
        if todo:
            *held, row = local_head(w_in, q_in, k_in, v_in, g_in, held, todo.pop(0), dep)
            rows.append(row)
            dep = [row]
        return dep

    def advance(step, part, dep):
        have, grad = got[part], grads[part]
        if step < low:
            terms = ups[part] + have

            def rule(bits, terms):
                return sum(terms[1:], terms[0])

        elif step == low:
            terms = ups[part] + have + [grad[top]]

            def rule(bits, terms):
                return jnp.where(bits[low], terms[-1], sum(terms[1:-1], terms[0]))

        elif step == low + 1:
            terms = ups[part] + have[:low] + [grad[top], have[low]]

            def rule(bits, terms):
                up = sum(terms[1:-2], terms[0])
                return jnp.where(bits[top], terms[-2], up) + terms[-1]

        elif step == low + 2:
            terms = [grad[low], have[low + 1]]

            def rule(bits, terms):
                other = jnp.where(bits[low], keep(~bits[top], terms[1]), terms[1])
                return keep(bits[low], terms[0]) + other

        else:
            terms = [grad[2 * low + 2 - step], *have[low + 1 :]]

            def rule(bits, terms):
                return terms[0] + gathered(bits, terms[1:])

        sent = mix(levels, terms, rule, dep)
        have.append(lax.ppermute(sent, "ctx", steps[step]))
        return [sent]

    for part in parts:
        grads[part] = state_grads(q_in, g_in, w_in, firsts[part], counts[part], dep)
        dep = [grads[part][top]]

    query_out, weight_rows, asked = [], [], list(parts)

    def query(dep):
        part = asked.pop(0)
        grad, row = query_side(
            w_in,
            q_in,
            g_in,
            held[0],
            got[part][: levels + 1],
            ([] if weight_rows else rows, weight_rows),
            firsts[part],
            query_out,
            dep,
        )
        query_out[:], weight_rows[:] = [grad], [row]
        return [row]

    fill = list(FILL)
    for step in range(1 if low else 0, len(steps)):
        for part in parts:
            if step == low + 3 and part:
                dep = query(dep)
            for _ in range(fill.pop(0) if fill else 0):
                dep = local(dep)
            dep = advance(step, part, dep)
    while todo:
        dep = local(dep)
    while asked:
        dep = query(dep)
    ways = lax.axis_size("head")
    weight_rows += [
        lax.ppermute(weight_rows[0], "head", [(n, (n + shift) % ways) for n in range(ways)])
        for shift in range(1, ways)
    ]
    key_out, weight_grad = [], None
    for part in parts:
        *key_out, weight_grad = [
            *key_side(
                k_in,
                v_in,
                held[1],
                held[2],
                got[part][low + 1 :],
                levels,
                weight_rows if part == parts[-1] else [],
                firsts[part],
                key_out,
                dep,
            ),
            *([] if part == parts[-1] else [None]),
        ]
        dep = []
    return query_out[0], key_out[0], key_out[1], weight_grad


def solution(mesh):
    placed = (
        P("head", "ctx", None),
        P("head", "ctx", None),
        P("head", "ctx", None),
        P(None, "ctx"),
        P("head", "ctx", None),
    )
    return jax.shard_map(
        per_device,
        mesh=mesh,
        in_specs=placed,
        out_specs=(
            P("head", "ctx", None),
            P("head", "ctx", None),
            P("head", "ctx", None),
            P(None, "ctx"),
        ),
        check_vma=False,
    )
```

time: 66.1 us -> 53.9 us (0.82)
  Pallas kernels: 40 us -> 30.7 us
  local copies, waits for them, and re-layouts: 4.24 us -> 0.01 us
  waiting for transfers between devices: 3.27 us -> 4.9 us
  other arithmetic: 0.82 us -> 0 us
    pallas_call x26 -> x24, Pallas kernels: 40 us -> 30.7 us  [call(): pl.pallas_call(body, in_specs=list(specs) + [ANYWHERE] * len(deps), out_s...]
    unnamed x16 -> x2, local copies, waits for them, and re-layouts: 4.24 us -> 0.01 us
    ppermute x2, waiting for transfers between devices: 0.01 us -> 2.7 us  [per_device(): got[part].append(lax.ppermute(state, 'ctx', steps[0]))]
    ppermute x3, waiting for transfers between devices: 2.66 us -> 1.27 us  [per_device(): lax.ppermute(weight_rows[0], 'head', [(n, (n + shift) % ways) for n in ra...]
    ppermute x8, starting transfers between devices: 11.4 us -> 12.2 us  [advance(): have.append(lax.ppermute(sent, 'ctx', steps[step]))]
    add x4 -> x0, other arithmetic: 0.66 us -> none  [the longest x1 0.63 us: per_device(): weight_grad = weight_grad + other]
  transfers between devices with their start and end apart: 13 -> 13, of which waited for: 3 -> 7; matrix products, arithmetic and copies ran while one was open for 1% -> 0% of each run, Pallas kernels for 54% -> 50%
where the time goes in v3:
time: 53.9 us; the launch traced here: 53.7 us
  Pallas kernels  30.7 us (57%)
  starting transfers between devices  17.1 us (32%)
  waiting for transfers between devices  4.9 us (9%)
  between operations  1 us (2%)
    pallas_call x24, Pallas kernels, call(): pl.pallas_call(body, in_specs=list(specs) + [ANYWHERE] * len(deps), out_s...  30.7 us
    ppermute x8, starting transfers between devices, advance(): have.append(lax.ppermute(sent, 'ctx', steps[step]))  12.2 us
    ppermute x2, starting transfers between devices, per_device(): got[part].append(lax.ppermute(state, 'ctx', steps[0]))  3.12 us
    ppermute x2, waiting for transfers between devices, per_device(): got[part].append(lax.ppermute(state, 'ctx', steps[0]))  2.7 us
    ppermute x3, starting transfers between devices, per_device(): lax.ppermute(weight_rows[0], 'head', [(n, (n + shift) % ways) for n in ra...  1.79 us
    ppermute x3, waiting for transfers between devices, per_device(): lax.ppermute(weight_rows[0], 'head', [(n, (n + shift) % ways) for n in ra...  1.27 us
  transfers between devices with their start and end apart: 13, of which 7 were waited for; matrix products, arithmetic and copies ran while one was open for 0% of the time, Pallas kernels for 50%

profile of v3, /device:TPU:0, one launch (start us, length us, event | category | flops | bytes accessed | tf_op | source)
XLA Modules:
  0.0 53.7 jit_solution(9494106009851471039)
XLA Ops:
  0.6 1.9 %load_states.2 = (bf16[8,1024,128]{2,1,0:T(8,128)(2,1)S(1)}, bf16[8,1024,128]{2,1,0:T(8,128)(2,1)S(1)}, f32[4,128,128]{2,1,0:T(8,128)S(1)}) custom-call(bf16[8,1024,128]{2,1,0:T(8,128)(2,1)} %refs_0_.13, bf16[8,1024,128]{2,1,0:T(8,128)(2,1)} %refs_1_.3), custom_call_target="tpu_custom_call" | custom-call | flops 1 | bytes 1 | tf_op jit(solution)/shard_map/load_states/pallas_call | solution.py:49
  2.6 3.0 %collective-permute-start = (f32[4,128,128]{2,1,0:T(8,128)S(1)}, f32[4,128,128]{2,1,0:T(8,128)S(1)}, u32[]{:S(2)}, u32[]{:S(2)}) collective-permute-start(f32[4,128,128]{2,1,0:T(8,128)S(1)} %get-tuple-element.61.refs_6_.refs_0_), channel_id=1, source_target_pairs={{0,4},{4,0},{8,12},{12,8},{16,20},{20,16},{24,28},{28,24},{1,5},{5... | collective-permute-start | bytes 786440 | tf_op jit(solution)/shard_map/ppermute | solution.py:358
  5.6 3.0 %load_states.3 = (bf16[8,1024,128]{2,1,0:T(8,128)(2,1)S(1)}, bf16[8,1024,128]{2,1,0:T(8,128)(2,1)S(1)}, bf16[8,1024,128]{2,1,0:T(8,128)(2,1)S(1)}, bf16[8,1024,128]{2,1,0:T(8,128)(2,1)S(1)}, f32[4,128,128]{2,1,0:T(8,128)S(1)}) custom-call(bf16[8,1024,128]{2,1,0:T(8,128)(2,1)} %refs_0_.13, ...), custom_call_target="tpu_custom_call", output_to_operand_aliasing={{0}: (4, {}), {1}: (5, {})} | custom-call | flops 1 | bytes 1 | tf_op jit(solution)/shard_map/load_states/pallas_call | solution.py:49
  8.6 0.1 collective-permute-start.1
  8.6 0.0 copy-done
  8.7 1.0 %state_grads.2 = (f32[4,128,128]{2,1,0:T(8,128)S(1)}, f32[4,128,128]{2,1,0:T(8,128)S(1)}, f32[4,128,128]{2,1,0:T(8,128)S(1)}) custom-call(bf16[8,1024,128]{2,1,0:T(8,128)(2,1)S(1)} %get-tuple-element.62.refs_0_.refs_1_, bf16[8,1024,128]{2,1,0:T(8,128)(2,1)S(1)} %get-tuple-element.63.refs_1_.refs_4_.refs_2_, f32[4,1024]{1,0:T(4,128)S(1)} %copy-done, ...), custom_call_target="tpu_custom_call" | custom-call | flops 1 | bytes 1 | tf_op jit(solution)/shard_map/state_grads/pallas_call | solution.py:49
  9.7 1.0 %state_grads.3 = (f32[4,128,128]{2,1,0:T(8,128)S(1)}, f32[4,128,128]{2,1,0:T(8,128)S(1)}, f32[4,128,128]{2,1,0:T(8,128)S(1)}) custom-call(bf16[8,1024,128]{2,1,0:T(8,128)(2,1)S(1)} %get-tuple-element.62.refs_0_.refs_1_, bf16[8,1024,128]{2,1,0:T(8,128)(2,1)S(1)} %get-tuple-element.63.refs_1_.refs_4_.refs_2_, f32[4,1024]{1,0:T(4,128)S(1)} %copy-done, ...), custom_call_target="tpu_custom_call" | custom-call | flops 1 | bytes 1 | tf_op jit(solution)/shard_map/state_grads/pallas_call | solution.py:49
  10.7 2.0 %collective-permute-done.refs_1_.refs_4_ = f32[4,128,128]{2,1,0:T(8,128)S(1)} collective-permute-done((f32[4,128,128]{2,1,0:T(8,128)S(1)}, f32[4,128,128]{2,1,0:T(8,128)S(1)}, u32[]{:S(2)}, u32[]{:S(2)}) %collective-permute-start) | collective-permute-done | bytes 262176 | tf_op jit(solution)/shard_map/ppermute | solution.py:358
  12.8 2.2 %collective-permute-start.2 = (f32[4,128,128]{2,1,0:T(8,128)S(1)}, f32[4,128,128]{2,1,0:T(8,128)S(1)}, u32[]{:S(2)}, u32[]{:S(2)}) collective-permute-start(f32[4,128,128]{2,1,0:T(8,128)S(1)} %mix.8.refs_5_), channel_id=1, source_target_pairs={{0,8},{4,12},{8,0},{12,4},{16,24},{20,28},{24,16},{28,20},{1,9},{5... | collective-permute-start | bytes 786440 | tf_op jit(solution)/shard_map/ppermute | solution.py:406
  15.0 1.9 %local.8 = (f32[8,128,1024]{2,1,0:T(8,128)S(1)}, f32[8,1024,128]{2,1,0:T(8,128)S(1)}, f32[8,1024,128]{2,1,0:T(8,128)S(1)}, f32[1,1024]{1,0:T(1,128)S(1)}) custom-call(f32[4,1024]{1,0:T(4,128)S(1)} %copy-done, bf16[8,1024,128]{2,1,0:T(8,128)(2,1)S(1)} %get-tuple-element.62.refs_0_.refs_1_, bf16[8,1024,128]{2,1,0:T(8,128)(2,1)S(1)} %get-tuple-element.64.refs_2_.refs_0_, ...), custom_call_target="tpu_custom_call" | custom-call | flops 1 | bytes 1 | tf_op jit(solution)/shard_map/local/pallas_call | solution.py:49
  16.8 0.7 %collective-permute-done.1.refs_1_.refs_4_ = f32[4,128,128]{2,1,0:T(8,128)S(1)} collective-permute-done((f32[4,128,128]{2,1,0:T(8,128)S(1)}, f32[4,128,128]{2,1,0:T(8,128)S(1)}, u32[]{:S(2)}, u32[]{:S(2)}) %collective-permute-start.1) | collective-permute-done | bytes 262176 | tf_op jit(solution)/shard_map/ppermute | solution.py:358
  17.6 1.9 %collective-permute-start.3 = (f32[4,128,128]{2,1,0:T(8,128)S(1)}, f32[4,128,128]{2,1,0:T(8,128)S(1)}, u32[]{:S(2)}, u32[]{:S(2)}) collective-permute-start(f32[4,128,128]{2,1,0:T(8,128)S(1)} %mix.9.refs_8_), channel_id=1, source_target_pairs={{0,8},{4,12},{8,0},{12,4},{16,24},{20,28},{24,16},{28,20},{1,9},{5... | collective-permute-start | bytes 786440 | tf_op jit(solution)/shard_map/ppermute | solution.py:406
  19.4 1.9 %local.9 = (f32[8,128,1024]{2,1,0:T(8,128)S(1)}, f32[8,1024,128]{2,1,0:T(8,128)S(1)}, f32[8,1024,128]{2,1,0:T(8,128)S(1)}, f32[1,1024]{1,0:T(1,128)S(1)}) custom-call(f32[4,1024]{1,0:T(4,128)S(1)} %copy-done, bf16[8,1024,128]{2,1,0:T(8,128)(2,1)S(1)} %get-tuple-element.62.refs_0_.refs_1_, ...), custom_call_target="tpu_custom_call", output_to_operand_aliasing={{0}: (5, {}), {1}: (6, {}), {2}: (7, {})} | custom-call | flops 1 | bytes 1 | tf_op jit(solution)/shard_map/local/pallas_call | solution.py:49
  21.3 0.0 collective-permute-done.2.refs_3_.refs_5_
  21.3 0.1 mix.10.refs_8_
  21.4 1.6 %collective-permute-start.4 = (f32[4,128,128]{2,1,0:T(8,128)S(1)}, f32[4,128,128]{2,1,0:T(8,128)S(1)}, u32[]{:S(2)}, u32[]{:S(2)}) collective-permute-start(f32[4,128,128]{2,1,0:T(8,128)S(1)} %mix.10.refs_8_), channel_id=1, source_target_pairs={{0,4},{4,0},{8,16},{12,20},{16,8},{20,12},{24,28},{28,24},{1,5},{5... | collective-permute-start | bytes 786440 | tf_op jit(solution)/shard_map/ppermute | solution.py:406
  23.0 1.9 %local.10 = (f32[8,128,1024]{2,1,0:T(8,128)S(1)}, f32[8,1024,128]{2,1,0:T(8,128)S(1)}, f32[8,1024,128]{2,1,0:T(8,128)S(1)}, f32[1,1024]{1,0:T(1,128)S(1)}) custom-call(f32[4,1024]{1,0:T(4,128)S(1)} %copy-done, bf16[8,1024,128]{2,1,0:T(8,128)(2,1)S(1)} %get-tuple-element.62.refs_0_.refs_1_, ...), custom_call_target="tpu_custom_call", output_to_operand_aliasing={{0}: (5, {}), {1}: (6, {}), {2}: (7, {})} | custom-call | flops 1 | bytes 1 | tf_op jit(solution)/shard_map/local/pallas_call | solution.py:49
  24.8 0.3 collective-permute-done.3.refs_3_.refs_5_
  25.2 1.8 %collective-permute-start.5 = (f32[4,128,128]{2,1,0:T(8,128)S(1)}, f32[4,128,128]{2,1,0:T(8,128)S(1)}, u32[]{:S(2)}, u32[]{:S(2)}) collective-permute-start(f32[4,128,128]{2,1,0:T(8,128)S(1)} %mix.11.refs_8_), channel_id=1, source_target_pairs={{0,4},{4,0},{8,16},{12,20},{16,8},{20,12},{24,28},{28,24},{1,5},{5... | collective-permute-start | bytes 786440 | tf_op jit(solution)/shard_map/ppermute | solution.py:406
  27.0 1.9 %local.11 = (f32[8,128,1024]{2,1,0:T(8,128)S(1)}, f32[8,1024,128]{2,1,0:T(8,128)S(1)}, f32[8,1024,128]{2,1,0:T(8,128)S(1)}, f32[1,1024]{1,0:T(1,128)S(1)}) custom-call(f32[4,1024]{1,0:T(4,128)S(1)} %copy-done, bf16[8,1024,128]{2,1,0:T(8,128)(2,1)S(1)} %get-tuple-element.62.refs_0_.refs_1_, ...), custom_call_target="tpu_custom_call", output_to_operand_aliasing={{0}: (5, {}), {1}: (6, {}), {2}: (7, {})} | custom-call | flops 1 | bytes 1 | tf_op jit(solution)/shard_map/local/pallas_call | solution.py:49
  28.9 2.0 %local.12 = (f32[8,128,1024]{2,1,0:T(8,128)S(1)}, f32[8,1024,128]{2,1,0:T(8,128)S(1)}, f32[8,1024,128]{2,1,0:T(8,128)S(1)}, f32[1,1024]{1,0:T(1,128)S(1)}) custom-call(f32[4,1024]{1,0:T(4,128)S(1)} %copy-done, bf16[8,1024,128]{2,1,0:T(8,128)(2,1)S(1)} %get-tuple-element.62.refs_0_.refs_1_, ...), custom_call_target="tpu_custom_call", output_to_operand_aliasing={{0}: (5, {}), {1}: (6, {}), {2}: (7, {})} | custom-call | flops 1 | bytes 1 | tf_op jit(solution)/shard_map/local/pallas_call | solution.py:49
  30.9 0.0 collective-permute-done.4.refs_1_.refs_6_.refs_4_
  30.9 0.1 mix.12.refs_8_
  30.9 1.7 %collective-permute-start.7 = (f32[4,128,128]{2,1,0:T(8,128)S(1)}, f32[4,128,128]{2,1,0:T(8,128)S(1)}, u32[]{:S(2)}, u32[]{:S(2)}) collective-permute-start(f32[4,128,128]{2,1,0:T(8,128)S(1)} %mix.12.refs_8_), channel_id=1, source_target_pairs={{0,8},{4,12},{8,0},{12,4},{16,24},{20,28},{24,16},{28,20},{1,9},{5... | collective-permute-start | bytes 786440 | tf_op jit(solution)/shard_map/ppermute | solution.py:406
  32.6 1.9 %local.13 = (f32[8,128,1024]{2,1,0:T(8,128)S(1)}, f32[8,1024,128]{2,1,0:T(8,128)S(1)}, f32[8,1024,128]{2,1,0:T(8,128)S(1)}, f32[1,1024]{1,0:T(1,128)S(1)}) custom-call(f32[4,1024]{1,0:T(4,128)S(1)} %copy-done, bf16[8,1024,128]{2,1,0:T(8,128)(2,1)S(1)} %get-tuple-element.62.refs_0_.refs_1_, ...), custom_call_target="tpu_custom_call", output_to_operand_aliasing={{0}: (5, {}), {1}: (6, {}), {2}: (7, {})} | custom-call | flops 1 | bytes 1 | tf_op jit(solution)/shard_map/local/pallas_call | solution.py:49
  34.5 0.0 collective-permute-done.5.refs_1_.refs_6_.refs_4_
  34.5 0.1 mix.13.refs_8_
  34.6 0.9 %collective-permute-start.6 = (f32[4,128,128]{2,1,0:T(8,128)S(1)}, f32[4,128,128]{2,1,0:T(8,128)S(1)}, u32[]{:S(2)}, u32[]{:S(2)}) collective-permute-start(f32[4,128,128]{2,1,0:T(8,128)S(1)} %mix.13.refs_8_), channel_id=1, source_target_pairs={{0,8},{4,12},{8,0},{12,4},{16,24},{20,28},{24,16},{28,20},{1,9},{5... | collective-permute-start | bytes 786440 | tf_op jit(solution)/shard_map/ppermute | solution.py:406
  35.5 1.9 %local.14 = (f32[8,128,1024]{2,1,0:T(8,128)S(1)}, f32[8,1024,128]{2,1,0:T(8,128)S(1)}, f32[8,1024,128]{2,1,0:T(8,128)S(1)}, f32[1,1024]{1,0:T(1,128)S(1)}) custom-call(f32[4,1024]{1,0:T(4,128)S(1)} %copy-done, bf16[8,1024,128]{2,1,0:T(8,128)(2,1)S(1)} %get-tuple-element.62.refs_0_.refs_1_, ...), custom_call_target="tpu_custom_call", output_to_operand_aliasing={{0}: (5, {}), {1}: (6, {}), {2}: (7, {})} | custom-call | flops 1 | bytes 1 | tf_op jit(solution)/shard_map/local/pallas_call | solution.py:49
  37.4 1.9 %local.15 = (f32[8,128,1024]{2,1,0:T(8,128)S(1)}, f32[8,1024,128]{2,1,0:T(8,128)S(1)}, f32[8,1024,128]{2,1,0:T(8,128)S(1)}, f32[1,1024]{1,0:T(1,128)S(1)}) custom-call(f32[4,1024]{1,0:T(4,128)S(1)} %copy-done, bf16[8,1024,128]{2,1,0:T(8,128)(2,1)S(1)} %get-tuple-element.62.refs_0_.refs_1_, ...), custom_call_target="tpu_custom_call", output_to_operand_aliasing={{0}: (5, {}), {1}: (6, {}), {2}: (7, {})} | custom-call | flops 1 | bytes 1 | tf_op jit(solution)/shard_map/local/pallas_call | solution.py:49
  39.2 0.5 collective-permute-done.7.refs_2_.refs_7_.refs_5_
  39.7 0.1 mix.14.refs_16_
  39.8 1.2 %collective-permute-start.12 = (f32[4,128,128]{2,1,0:T(8,128)S(1)}, f32[4,128,128]{2,1,0:T(8,128)S(1)}, u32[]{:S(2)}, u32[]{:S(2)}) collective-permute-start(f32[4,128,128]{2,1,0:T(8,128)S(1)} %mix.14.refs_16_), channel_id=1, source_target_pairs={{0,4},{4,0},{8,12},{12,8},{16,20},{20,16},{24,28},{28,24},{1,5},{5... | collective-permute-start | bytes 786440 | tf_op jit(solution)/shard_map/ppermute | solution.py:406
  41.0 2.4 %query_side.2 = (bf16[8,1024,128]{2,1,0:T(8,128)(2,1)}, f32[4,1024]{1,0:T(4,128)S(1)}) custom-call(f32[4,1024]{1,0:T(4,128)S(1)} %copy-done, bf16[8,1024,128]{2,1,0:T(8,128)(2,1)S(1)} %get-tuple-element.62.refs_0_.refs_1_, bf16[8,1024,128]{2,1,0:T(8,128)(2,1)S(1)} %get-tuple-element.63.refs_1_.refs_4_.refs_2_, ...), custom_call_target="tpu_custom_call" | custom-call | flops 1 | bytes 1 | tf_op jit(solution)/shard_map/query_side/pallas_call | solution.py:49
  43.5 0.0 collective-permute-done.6.refs_2_.refs_7_.refs_5_
  43.5 0.1 mix.15.refs_10_
  43.6 0.9 %collective-permute-start.8 = (f32[4,128,128]{2,1,0:T(8,128)S(1)}, f32[4,128,128]{2,1,0:T(8,128)S(1)}, u32[]{:S(2)}, u32[]{:S(2)}) collective-permute-start(f32[4,128,128]{2,1,0:T(8,128)S(1)} %mix.15.refs_10_), channel_id=1, source_target_pairs={{0,4},{4,0},{8,12},{12,8},{16,20},{20,16},{24,28},{28,24},{1,5},{5... | collective-permute-start | bytes 786440 | tf_op jit(solution)/shard_map/ppermute | solution.py:406
  44.5 2.4 %query_side.3 = (bf16[8,1024,128]{2,1,0:T(8,128)(2,1)}, f32[4,1024]{1,0:T(4,128)S(1)}) custom-call(f32[4,1024]{1,0:T(4,128)S(1)} %copy-done, bf16[8,1024,128]{2,1,0:T(8,128)(2,1)S(1)} %get-tuple-element.62.refs_0_.refs_1_, bf16[8,1024,128]{2,1,0:T(8,128)(2,1)S(1)} %get-tuple-element.63.refs_1_.refs_4_.refs_2_, ...), custom_call_target="tpu_custom_call", output_to_operand_aliasing={{0}: (9, {})} | custom-call | flops 1 | bytes 1 | tf_op jit(solution)/shard_map/query_side/pallas_call | solution.py:49
  46.9 0.1 collective-permute-start.11
  47.0 1.6 %collective-permute-start.10 = (f32[4,1024]{1,0:T(4,128)S(1)}, f32[4,1024]{1,0:T(4,128)S(1)}, u32[]{:S(2)}, u32[]{:S(2)}) collective-permute-start(f32[4,1024]{1,0:T(4,128)S(1)} %get-tuple-element.108.refs_7_), channel_id=1, source_target_pairs={{0,2},{1,3},{2,0},{3,1},{4,6},{5,7},{6,4},{7,5},{8,10},{9,11},{10,... | collective-permute-start | bytes 49160 | tf_op jit(solution)/shard_map/ppermute | solution.py:445
  48.6 0.2 collective-permute-start.9
  48.7 0.0 collective-permute-done.12.refs_6_
  48.7 1.7 %key_side.2 = (bf16[8,1024,128]{2,1,0:T(8,128)(2,1)}, bf16[8,1024,128]{2,1,0:T(8,128)(2,1)}) custom-call(bf16[8,1024,128]{2,1,0:T(8,128)(2,1)S(1)} %get-tuple-element.64.refs_2_.refs_0_, bf16[8,1024,128]{2,1,0:T(8,128)(2,1)S(1)} %get-tuple-element.65.refs_3_.refs_1_, f32[8,1024,128]{2,1,0:T(8,128)S(1)} %get-tuple-element.106.refs_2_, ...), custom_call_target="tpu_custom_call" | custom-call | flops 1 | bytes 1 | tf_op jit(solution)/shard_map/key_side/pallas_call | solution.py:49
  50.5 0.0 collective-permute-done.11.refs_10_
  50.5 0.3 collective-permute-done.10.refs_9_
  50.8 0.9 %collective-permute-done.9.refs_8_ = f32[4,1024]{1,0:T(4,128)S(1)} collective-permute-done((f32[4,1024]{1,0:T(4,128)S(1)}, f32[4,1024]{1,0:T(4,128)S(1)}, u32[]{:S(2)}, u32[]{:S(2)}) %collective-permute-start.9) | collective-permute-done | bytes 16416 | tf_op jit(solution)/shard_map/ppermute | solution.py:445
  51.7 0.1 collective-permute-done.8.refs_6_
  51.9 1.7 %key_side.3 = (bf16[8,1024,128]{2,1,0:T(8,128)(2,1)}, bf16[8,1024,128]{2,1,0:T(8,128)(2,1)}, f32[4,1024]{1,0:T(4,128)}) custom-call(bf16[8,1024,128]{2,1,0:T(8,128)(2,1)S(1)} %get-tuple-element.64.refs_2_.refs_0_, bf16[8,1024,128]{2,1,0:T(8,128)(2,1)S(1)} %get-tuple-element.65.refs_3_.refs_1_, ...), custom_call_target="tpu_custom_call", output_to_operand_aliasing={{0}: (11, {}), {1}: (12, {})} | custom-call | flops 1 | bytes 1 | tf_op jit(solution)/shard_map/key_side/pallas_call | solution.py:49
  (4 shorter events, 0.1 us)
Async XLA Ops:
  2.6 10.2 %collective-permute-start = (f32[4,128,128]{2,1,0:T(8,128)S(1)}, f32[4,128,128]{2,1,0:T(8,128)S(1)}, u32[]{:S(2)}, u32[]{:S(2)}) collective-permute-start(f32[4,128,128]{2,1,0:T(8,128)S(1)} %get-tuple-element.61.refs_6_.refs_0_), channel_id=1, source_target_pairs={{0,4},{4,0},{8,12},{12,8},{16,20},{20,16},{24,28},{28,24},{1,5},{5... | collective-permute-start | bytes 786440 | tf_op jit(solution)/shard_map/ppermute | solution.py:358
  5.6 3.1 %copy-start = (f32[4,1024]{1,0:T(4,128)S(1)}, f32[4,1024]{1,0:T(4,128)}, u32[]{:S(2)}) copy-start(f32[4,1024]{1,0:T(4,128)} %refs_0_.23) | copy-start | bytes 49156
  8.6 9.0 %collective-permute-start.1 = (f32[4,128,128]{2,1,0:T(8,128)S(1)}, f32[4,128,128]{2,1,0:T(8,128)S(1)}, u32[]{:S(2)}, u32[]{:S(2)}) collective-permute-start(f32[4,128,128]{2,1,0:T(8,128)S(1)} %get-tuple-element.66.refs_3_.refs_0_), channel_id=1, source_target_pairs={{0,4},{4,0},{8,12},{12,8},{16,20},{20,16},{24,28},{28,24},{1,5},{5... | collective-permute-start | bytes 786440 | tf_op jit(solution)/shard_map/ppermute | solution.py:358
  12.8 8.5 %collective-permute-start.2 = (f32[4,128,128]{2,1,0:T(8,128)S(1)}, f32[4,128,128]{2,1,0:T(8,128)S(1)}, u32[]{:S(2)}, u32[]{:S(2)}) collective-permute-start(f32[4,128,128]{2,1,0:T(8,128)S(1)} %mix.8.refs_5_), channel_id=1, source_target_pairs={{0,8},{4,12},{8,0},{12,4},{16,24},{20,28},{24,16},{28,20},{1,9},{5... | collective-permute-start | bytes 786440 | tf_op jit(solution)/shard_map/ppermute | solution.py:406
  17.6 7.6 %collective-permute-start.3 = (f32[4,128,128]{2,1,0:T(8,128)S(1)}, f32[4,128,128]{2,1,0:T(8,128)S(1)}, u32[]{:S(2)}, u32[]{:S(2)}) collective-permute-start(f32[4,128,128]{2,1,0:T(8,128)S(1)} %mix.9.refs_8_), channel_id=1, source_target_pairs={{0,8},{4,12},{8,0},{12,4},{16,24},{20,28},{24,16},{28,20},{1,9},{5... | collective-permute-start | bytes 786440 | tf_op jit(solution)/shard_map/ppermute | solution.py:406
  21.4 9.5 %collective-permute-start.4 = (f32[4,128,128]{2,1,0:T(8,128)S(1)}, f32[4,128,128]{2,1,0:T(8,128)S(1)}, u32[]{:S(2)}, u32[]{:S(2)}) collective-permute-start(f32[4,128,128]{2,1,0:T(8,128)S(1)} %mix.10.refs_8_), channel_id=1, source_target_pairs={{0,4},{4,0},{8,16},{12,20},{16,8},{20,12},{24,28},{28,24},{1,5},{5... | collective-permute-start | bytes 786440 | tf_op jit(solution)/shard_map/ppermute | solution.py:406
  25.2 9.3 %collective-permute-start.5 = (f32[4,128,128]{2,1,0:T(8,128)S(1)}, f32[4,128,128]{2,1,0:T(8,128)S(1)}, u32[]{:S(2)}, u32[]{:S(2)}) collective-permute-start(f32[4,128,128]{2,1,0:T(8,128)S(1)} %mix.11.refs_8_), channel_id=1, source_target_pairs={{0,4},{4,0},{8,16},{12,20},{16,8},{20,12},{24,28},{28,24},{1,5},{5... | collective-permute-start | bytes 786440 | tf_op jit(solution)/shard_map/ppermute | solution.py:406
  30.9 8.8 %collective-permute-start.7 = (f32[4,128,128]{2,1,0:T(8,128)S(1)}, f32[4,128,128]{2,1,0:T(8,128)S(1)}, u32[]{:S(2)}, u32[]{:S(2)}) collective-permute-start(f32[4,128,128]{2,1,0:T(8,128)S(1)} %mix.12.refs_8_), channel_id=1, source_target_pairs={{0,8},{4,12},{8,0},{12,4},{16,24},{20,28},{24,16},{28,20},{1,9},{5... | collective-permute-start | bytes 786440 | tf_op jit(solution)/shard_map/ppermute | solution.py:406
  34.6 8.9 %collective-permute-start.6 = (f32[4,128,128]{2,1,0:T(8,128)S(1)}, f32[4,128,128]{2,1,0:T(8,128)S(1)}, u32[]{:S(2)}, u32[]{:S(2)}) collective-permute-start(f32[4,128,128]{2,1,0:T(8,128)S(1)} %mix.13.refs_8_), channel_id=1, source_target_pairs={{0,8},{4,12},{8,0},{12,4},{16,24},{20,28},{24,16},{28,20},{1,9},{5... | collective-permute-start | bytes 786440 | tf_op jit(solution)/shard_map/ppermute | solution.py:406
  39.8 8.9 %collective-permute-start.12 = (f32[4,128,128]{2,1,0:T(8,128)S(1)}, f32[4,128,128]{2,1,0:T(8,128)S(1)}, u32[]{:S(2)}, u32[]{:S(2)}) collective-permute-start(f32[4,128,128]{2,1,0:T(8,128)S(1)} %mix.14.refs_16_), channel_id=1, source_target_pairs={{0,4},{4,0},{8,12},{12,8},{16,20},{20,16},{24,28},{28,24},{1,5},{5... | collective-permute-start | bytes 786440 | tf_op jit(solution)/shard_map/ppermute | solution.py:406
  43.6 8.3 %collective-permute-start.8 = (f32[4,128,128]{2,1,0:T(8,128)S(1)}, f32[4,128,128]{2,1,0:T(8,128)S(1)}, u32[]{:S(2)}, u32[]{:S(2)}) collective-permute-start(f32[4,128,128]{2,1,0:T(8,128)S(1)} %mix.15.refs_10_), channel_id=1, source_target_pairs={{0,4},{4,0},{8,12},{12,8},{16,20},{20,16},{24,28},{28,24},{1,5},{5... | collective-permute-start | bytes 786440 | tf_op jit(solution)/shard_map/ppermute | solution.py:406
  46.9 3.5 %collective-permute-start.11 = (f32[4,1024]{1,0:T(4,128)S(1)}, f32[4,1024]{1,0:T(4,128)S(1)}, u32[]{:S(2)}, u32[]{:S(2)}) collective-permute-start(f32[4,1024]{1,0:T(4,128)S(1)} %get-tuple-element.108.refs_7_), channel_id=1, source_target_pairs={{0,3},{1,0},{2,1},{3,2},{4,7},{5,4},{6,5},{7,6},{8,11},{9,8},{10,9... | collective-permute-start | bytes 49160 | tf_op jit(solution)/shard_map/ppermute | solution.py:445
  47.0 3.8 %collective-permute-start.10 = (f32[4,1024]{1,0:T(4,128)S(1)}, f32[4,1024]{1,0:T(4,128)S(1)}, u32[]{:S(2)}, u32[]{:S(2)}) collective-permute-start(f32[4,1024]{1,0:T(4,128)S(1)} %get-tuple-element.108.refs_7_), channel_id=1, source_target_pairs={{0,2},{1,3},{2,0},{3,1},{4,6},{5,7},{6,4},{7,5},{8,10},{9,11},{10,... | collective-permute-start | bytes 49160 | tf_op jit(solution)/shard_map/ppermute | solution.py:445
  48.6 3.2 %collective-permute-start.9 = (f32[4,1024]{1,0:T(4,128)S(1)}, f32[4,1024]{1,0:T(4,128)S(1)}, u32[]{:S(2)}, u32[]{:S(2)}) collective-permute-start(f32[4,1024]{1,0:T(4,128)S(1)} %get-tuple-element.108.refs_7_), channel_id=1, source_target_pairs={{0,1},{1,2},{2,3},{3,0},{4,5},{5,6},{6,7},{7,4},{8,9},{9,10},{10,1... | collective-permute-start | bytes 49160 | tf_op jit(solution)/shard_map/ppermute | solution.py:445

commit v4 on v3

--- a/solution.py
+++ b/solution.py
@@ -11,7 +11,7 @@
 TN = (((0,), (0,)), ((), ()))
 VMEM_BYTES = 16 * 2**20
 PARTS = (4, 4)
-FILL = (0, 1, 1, 1, 2, 1, 2, 0)
+FILL = (1, 2, 1, 1, 1, 1, 1, 0)
 
 INSIDE = pl.BlockSpec(memory_space=pltpu.VMEM)
 OUTSIDE = pl.BlockSpec(memory_space=pltpu.HBM)
@@ -136,12 +136,22 @@
     def kernel(w_ref, q_ref, k_ref, v_ref, g_ref, *rest):
         lq_ref, lk_ref, lv_ref, lw_ref = rest[-4:]
         k_turned = k_ref[at].T
-        for i in range(length // tile):
+        tiles = length // tile
+
+        def products(i):
             upto = (i + 1) * tile
             t = pl.ds(i * tile, tile)
-            q, g, w = q_ref[at, t, :], g_ref[at, t, :], w_ref[0:1, t]
-            raw = dot(k_ref[at, :upto, :], q, NT)
-            d_attn = dot(v_ref[at, :upto, :], g, NT)
+            raw = dot(k_ref[at, :upto, :], q_ref[at, t, :], NT)
+            return raw, dot(v_ref[at, :upto, :], g_ref[at, t, :], NT)
+
+        later = products(0)
+        for i in range(tiles):
+            raw, d_attn = later
+            if i + 1 < tiles:
+                later = products(i + 1)
+            upto = (i + 1) * tile
+            t = pl.ds(i * tile, tile)
+            w = w_ref[0:1, t]
             rows = lax.broadcasted_iota(jnp.int32, (upto, tile), 0)
             columns = lax.broadcasted_iota(jnp.int32, (upto, tile), 1) + i * tile
             raw = jnp.where(rows <= columns, raw, 0.0)
@@ -149,7 +159,8 @@
             lw_ref[0:1, t] = jnp.sum(raw * d_attn, axis=0, keepdims=True)
             attn = (raw * w).astype(BF16)
             d_raw = (d_attn * w).astype(BF16)
-            k_part, v_part = dot(d_raw, q, NN), dot(attn, g, NN)
+            k_part = dot(d_raw, q_ref[at, t, :], NN)
+            v_part = dot(attn, g_ref[at, t, :], NN)
             lk_ref[at, t, :] = k_part[i * tile :]
             lv_ref[at, t, :] = v_part[i * tile :]
             if i:
@@ -204,9 +215,8 @@
         state_refs = rest[: levels + 1]
         singles = rest[levels + 1 : levels + 1 + len(single)]
         wholes = rest[levels + 1 + len(single) : levels + 1 + len(single) + len(whole)]
-        out_ref, row_ref, staged, sems = rest[-4:]
+        out_ref, row_ref = rest[-2:]
         bits = block_bits(levels)
-        copies = []
         totals = [None] * levels
 
         def product(i):
@@ -227,10 +237,7 @@
                 total = total + w_ref[level + 1 : level + 2, :] * z
                 row = jnp.sum(turned * z, axis=0, keepdims=True)
                 totals[level] = row if totals[level] is None else totals[level] + row
-            staged[i] = total.T.astype(BF16)
-            copy = pltpu.make_async_copy(staged.at[i], out_ref.at[first + i], sems.at[i])
-            copy.start()
-            copies.append(copy)
+            out_ref[first + i] = total.T.astype(BF16)
         own = None
         for ref in singles:
             own = ref[...] if own is None else own + ref[...]
@@ -241,20 +248,17 @@
         row_ref[0:1, :] = own
         for level in range(levels):
             row_ref[level + 1 : level + 2, :] = totals[level]
-        for copy in copies:
-            copy.wait()
 
     args = [level_weight, queries, out_grad, query_sum, *states, *single, *whole]
     return call(
         kernel,
         "query_side",
         args + list(out),
-        [INSIDE] * len(args) + [OUTSIDE] * len(out),
-        [jax.ShapeDtypeStruct(shape, BF16), jax.ShapeDtypeStruct((levels + 1, length), F32)],
-        [OUTSIDE, INSIDE],
+        [INSIDE] * (len(args) + len(out)),
+        [pltpu.VMEM(shape, BF16), jax.ShapeDtypeStruct((levels + 1, length), F32)],
+        [INSIDE] * 2,
         deps,
         {len(args): 0} if out else {},
-        [pltpu.VMEM((count, length, depth), BF16), pltpu.SemaphoreType.DMA((count,))],
     )
 
 

time: 53.9 us -> 52 us (0.965)
  Pallas kernels: 30.7 us -> 27.9 us
  local copies, waits for them, and re-layouts: 0.01 us -> 1.32 us
  waiting for transfers between devices: 4.9 us -> 3.82 us
  starting transfers between devices: 17.1 us -> 17.8 us
    pallas_call x24, Pallas kernels: 30.7 us -> 27.9 us  [call(): pl.pallas_call(body, in_specs=list(specs) + [ANYWHERE] * len(deps), out_s...]
    ppermute x8, waiting for transfers between devices: 0.93 us -> 3.51 us  [advance(): have.append(lax.ppermute(sent, 'ctx', steps[step]))]
    ppermute x2, waiting for transfers between devices: 2.7 us -> 0.3 us  [per_device(): got[part].append(lax.ppermute(state, 'ctx', steps[0]))]
    unnamed x2 -> x3, local copies, waits for them, and re-layouts: 0.01 us -> 1.32 us
    ppermute x3, waiting for transfers between devices: 1.27 us -> 0.01 us  [per_device(): lax.ppermute(weight_rows[0], 'head', [(n, (n + shift) % ways) for n in ra...]
    ppermute x8, starting transfers between devices: 12.2 us -> 12.9 us  [advance(): have.append(lax.ppermute(sent, 'ctx', steps[step]))]
  transfers between devices with their start and end apart: 13 -> 13, of which waited for: 7 -> 5; matrix products, arithmetic and copies ran while one was open for 0% -> 3% of each run, Pallas kernels for 50% -> 47%
where the time goes in v4:
time: 52 us; the launch traced here: 51.9 us
  Pallas kernels  27.9 us (54%)
  starting transfers between devices  17.8 us (34%)
  waiting for transfers between devices  3.82 us (7%)
  local copies, waits for them, and re-layouts  1.32 us (3%)
  between operations  1.02 us (2%)
    pallas_call x24, Pallas kernels, call(): pl.pallas_call(body, in_specs=list(specs) + [ANYWHERE] * len(deps), out_s...  27.9 us
    ppermute x8, starting transfers between devices, advance(): have.append(lax.ppermute(sent, 'ctx', steps[step]))  12.9 us
    ppermute x8, waiting for transfers between devices, advance(): have.append(lax.ppermute(sent, 'ctx', steps[step]))  3.51 us
    ppermute x2, starting transfers between devices, per_device(): got[part].append(lax.ppermute(state, 'ctx', steps[0]))  3.12 us
    ppermute x3, starting transfers between devices, per_device(): lax.ppermute(weight_rows[0], 'head', [(n, (n + shift) % ways) for n in ra...  1.79 us
    unnamed x3, local copies, waits for them, and re-layouts  1.32 us
  transfers between devices with their start and end apart: 13, of which 5 were waited for; matrix products, arithmetic and copies ran while one was open for 3% of the time, Pallas kernels for 47%

profile of v4, /device:TPU:0, one launch (start us, length us, event | category | flops | bytes accessed | tf_op | source)
XLA Modules:
  0.0 51.9 jit_solution(9261703113569538023)
XLA Ops:
  0.6 1.9 %load_states.2 = (bf16[8,1024,128]{2,1,0:T(8,128)(2,1)S(1)}, bf16[8,1024,128]{2,1,0:T(8,128)(2,1)S(1)}, f32[4,128,128]{2,1,0:T(8,128)S(1)}) custom-call(bf16[8,1024,128]{2,1,0:T(8,128)(2,1)} %refs_0_.13, bf16[8,1024,128]{2,1,0:T(8,128)(2,1)} %refs_1_.3), custom_call_target="tpu_custom_call" | custom-call | flops 1 | bytes 1 | tf_op jit(solution)/shard_map/load_states/pallas_call | solution.py:49
  2.6 3.0 %collective-permute-start = (f32[4,128,128]{2,1,0:T(8,128)S(1)}, f32[4,128,128]{2,1,0:T(8,128)S(1)}, u32[]{:S(2)}, u32[]{:S(2)}) collective-permute-start(f32[4,128,128]{2,1,0:T(8,128)S(1)} %get-tuple-element.61.refs_6_.refs_0_), channel_id=1, source_target_pairs={{0,4},{4,0},{8,12},{12,8},{16,20},{20,16},{24,28},{28,24},{1,5},{5... | collective-permute-start | bytes 786440 | tf_op jit(solution)/shard_map/ppermute | solution.py:362
  5.6 0.0 copy-start
  5.6 3.0 %load_states.3 = (bf16[8,1024,128]{2,1,0:T(8,128)(2,1)S(1)}, bf16[8,1024,128]{2,1,0:T(8,128)(2,1)S(1)}, bf16[8,1024,128]{2,1,0:T(8,128)(2,1)S(1)}, bf16[8,1024,128]{2,1,0:T(8,128)(2,1)S(1)}, f32[4,128,128]{2,1,0:T(8,128)S(1)}) custom-call(bf16[8,1024,128]{2,1,0:T(8,128)(2,1)} %refs_0_.13, ...), custom_call_target="tpu_custom_call", output_to_operand_aliasing={{0}: (4, {}), {1}: (5, {})} | custom-call | flops 1 | bytes 1 | tf_op jit(solution)/shard_map/load_states/pallas_call | solution.py:49
  8.6 0.1 collective-permute-start.1
  8.6 0.0 copy-done
  8.7 1.0 %state_grads.2 = (f32[4,128,128]{2,1,0:T(8,128)S(1)}, f32[4,128,128]{2,1,0:T(8,128)S(1)}, f32[4,128,128]{2,1,0:T(8,128)S(1)}) custom-call(bf16[8,1024,128]{2,1,0:T(8,128)(2,1)S(1)} %get-tuple-element.62.refs_0_.refs_1_, bf16[8,1024,128]{2,1,0:T(8,128)(2,1)S(1)} %get-tuple-element.63.refs_1_.refs_4_.refs_2_, f32[4,1024]{1,0:T(4,128)S(1)} %copy-done, ...), custom_call_target="tpu_custom_call" | custom-call | flops 1 | bytes 1 | tf_op jit(solution)/shard_map/state_grads/pallas_call | solution.py:49
  9.7 1.0 %state_grads.3 = (f32[4,128,128]{2,1,0:T(8,128)S(1)}, f32[4,128,128]{2,1,0:T(8,128)S(1)}, f32[4,128,128]{2,1,0:T(8,128)S(1)}) custom-call(bf16[8,1024,128]{2,1,0:T(8,128)(2,1)S(1)} %get-tuple-element.62.refs_0_.refs_1_, bf16[8,1024,128]{2,1,0:T(8,128)(2,1)S(1)} %get-tuple-element.63.refs_1_.refs_4_.refs_2_, f32[4,1024]{1,0:T(4,128)S(1)} %copy-done, ...), custom_call_target="tpu_custom_call" | custom-call | flops 1 | bytes 1 | tf_op jit(solution)/shard_map/state_grads/pallas_call | solution.py:49
  10.7 1.7 %local.8 = (f32[8,128,1024]{2,1,0:T(8,128)S(1)}, f32[8,1024,128]{2,1,0:T(8,128)S(1)}, f32[8,1024,128]{2,1,0:T(8,128)S(1)}, f32[1,1024]{1,0:T(1,128)S(1)}) custom-call(f32[4,1024]{1,0:T(4,128)S(1)} %copy-done, bf16[8,1024,128]{2,1,0:T(8,128)(2,1)S(1)} %get-tuple-element.62.refs_0_.refs_1_, bf16[8,1024,128]{2,1,0:T(8,128)(2,1)S(1)} %get-tuple-element.64.refs_2_.refs_0_, ...), custom_call_target="tpu_custom_call" | custom-call | flops 1 | bytes 1 | tf_op jit(solution)/shard_map/local/pallas_call | solution.py:49
  12.4 0.3 collective-permute-done.refs_1_.refs_4_
  12.8 2.2 %collective-permute-start.2 = (f32[4,128,128]{2,1,0:T(8,128)S(1)}, f32[4,128,128]{2,1,0:T(8,128)S(1)}, u32[]{:S(2)}, u32[]{:S(2)}) collective-permute-start(f32[4,128,128]{2,1,0:T(8,128)S(1)} %mix.8.refs_8_), channel_id=1, source_target_pairs={{0,8},{4,12},{8,0},{12,4},{16,24},{20,28},{24,16},{28,20},{1,9},{5... | collective-permute-start | bytes 786440 | tf_op jit(solution)/shard_map/ppermute | solution.py:410
  15.0 1.7 %local.9 = (f32[8,128,1024]{2,1,0:T(8,128)S(1)}, f32[8,1024,128]{2,1,0:T(8,128)S(1)}, f32[8,1024,128]{2,1,0:T(8,128)S(1)}, f32[1,1024]{1,0:T(1,128)S(1)}) custom-call(f32[4,1024]{1,0:T(4,128)S(1)} %copy-done, bf16[8,1024,128]{2,1,0:T(8,128)(2,1)S(1)} %get-tuple-element.62.refs_0_.refs_1_, ...), custom_call_target="tpu_custom_call", output_to_operand_aliasing={{0}: (5, {}), {1}: (6, {}), {2}: (7, {})} | custom-call | flops 1 | bytes 1 | tf_op jit(solution)/shard_map/local/pallas_call | solution.py:49
  16.7 1.7 %local.10 = (f32[8,128,1024]{2,1,0:T(8,128)S(1)}, f32[8,1024,128]{2,1,0:T(8,128)S(1)}, f32[8,1024,128]{2,1,0:T(8,128)S(1)}, f32[1,1024]{1,0:T(1,128)S(1)}) custom-call(f32[4,1024]{1,0:T(4,128)S(1)} %copy-done, bf16[8,1024,128]{2,1,0:T(8,128)(2,1)S(1)} %get-tuple-element.62.refs_0_.refs_1_, ...), custom_call_target="tpu_custom_call", output_to_operand_aliasing={{0}: (5, {}), {1}: (6, {}), {2}: (7, {})} | custom-call | flops 1 | bytes 1 | tf_op jit(solution)/shard_map/local/pallas_call | solution.py:49
  18.4 0.0 collective-permute-done.1.refs_1_.refs_4_
  18.4 1.0 %collective-permute-start.3 = (f32[4,128,128]{2,1,0:T(8,128)S(1)}, f32[4,128,128]{2,1,0:T(8,128)S(1)}, u32[]{:S(2)}, u32[]{:S(2)}) collective-permute-start(f32[4,128,128]{2,1,0:T(8,128)S(1)} %mix.9.refs_8_), channel_id=1, source_target_pairs={{0,8},{4,12},{8,0},{12,4},{16,24},{20,28},{24,16},{28,20},{1,9},{5... | collective-permute-start | bytes 786440 | tf_op jit(solution)/shard_map/ppermute | solution.py:410
  19.4 1.7 %local.11 = (f32[8,128,1024]{2,1,0:T(8,128)S(1)}, f32[8,1024,128]{2,1,0:T(8,128)S(1)}, f32[8,1024,128]{2,1,0:T(8,128)S(1)}, f32[1,1024]{1,0:T(1,128)S(1)}) custom-call(f32[4,1024]{1,0:T(4,128)S(1)} %copy-done, bf16[8,1024,128]{2,1,0:T(8,128)(2,1)S(1)} %get-tuple-element.62.refs_0_.refs_1_, ...), custom_call_target="tpu_custom_call", output_to_operand_aliasing={{0}: (5, {}), {1}: (6, {}), {2}: (7, {})} | custom-call | flops 1 | bytes 1 | tf_op jit(solution)/shard_map/local/pallas_call | solution.py:49
  21.1 0.0 collective-permute-done.2.refs_3_.refs_5_
  21.1 0.1 mix.10.refs_8_
  21.2 1.7 %collective-permute-start.4 = (f32[4,128,128]{2,1,0:T(8,128)S(1)}, f32[4,128,128]{2,1,0:T(8,128)S(1)}, u32[]{:S(2)}, u32[]{:S(2)}) collective-permute-start(f32[4,128,128]{2,1,0:T(8,128)S(1)} %mix.10.refs_8_), channel_id=1, source_target_pairs={{0,4},{4,0},{8,16},{12,20},{16,8},{20,12},{24,28},{28,24},{1,5},{5... | collective-permute-start | bytes 786440 | tf_op jit(solution)/shard_map/ppermute | solution.py:410
  22.9 1.7 %local.12 = (f32[8,128,1024]{2,1,0:T(8,128)S(1)}, f32[8,1024,128]{2,1,0:T(8,128)S(1)}, f32[8,1024,128]{2,1,0:T(8,128)S(1)}, f32[1,1024]{1,0:T(1,128)S(1)}) custom-call(f32[4,1024]{1,0:T(4,128)S(1)} %copy-done, bf16[8,1024,128]{2,1,0:T(8,128)(2,1)S(1)} %get-tuple-element.62.refs_0_.refs_1_, ...), custom_call_target="tpu_custom_call", output_to_operand_aliasing={{0}: (5, {}), {1}: (6, {}), {2}: (7, {})} | custom-call | flops 1 | bytes 1 | tf_op jit(solution)/shard_map/local/pallas_call | solution.py:49
  24.6 1.4 %collective-permute-done.3.refs_3_.refs_5_ = f32[4,128,128]{2,1,0:T(8,128)S(1)} collective-permute-done((f32[4,128,128]{2,1,0:T(8,128)S(1)}, f32[4,128,128]{2,1,0:T(8,128)S(1)}, u32[]{:S(2)}, u32[]{:S(2)}) %collective-permute-start.3) | collective-permute-done | bytes 262176 | tf_op jit(solution)/shard_map/ppermute | solution.py:410
  26.0 1.8 %collective-permute-start.5 = (f32[4,128,128]{2,1,0:T(8,128)S(1)}, f32[4,128,128]{2,1,0:T(8,128)S(1)}, u32[]{:S(2)}, u32[]{:S(2)}) collective-permute-start(f32[4,128,128]{2,1,0:T(8,128)S(1)} %mix.11.refs_8_), channel_id=1, source_target_pairs={{0,4},{4,0},{8,16},{12,20},{16,8},{20,12},{24,28},{28,24},{1,5},{5... | collective-permute-start | bytes 786440 | tf_op jit(solution)/shard_map/ppermute | solution.py:410
  27.8 1.9 %local.13 = (f32[8,128,1024]{2,1,0:T(8,128)S(1)}, f32[8,1024,128]{2,1,0:T(8,128)S(1)}, f32[8,1024,128]{2,1,0:T(8,128)S(1)}, f32[1,1024]{1,0:T(1,128)S(1)}) custom-call(f32[4,1024]{1,0:T(4,128)S(1)} %copy-done, bf16[8,1024,128]{2,1,0:T(8,128)(2,1)S(1)} %get-tuple-element.62.refs_0_.refs_1_, ...), custom_call_target="tpu_custom_call", output_to_operand_aliasing={{0}: (5, {}), {1}: (6, {}), {2}: (7, {})} | custom-call | flops 1 | bytes 1 | tf_op jit(solution)/shard_map/local/pallas_call | solution.py:49
  29.7 0.0 collective-permute-done.4.refs_1_.refs_6_.refs_4_
  29.7 0.1 mix.12.refs_8_
  29.8 1.7 %collective-permute-start.7 = (f32[4,128,128]{2,1,0:T(8,128)S(1)}, f32[4,128,128]{2,1,0:T(8,128)S(1)}, u32[]{:S(2)}, u32[]{:S(2)}) collective-permute-start(f32[4,128,128]{2,1,0:T(8,128)S(1)} %mix.12.refs_8_), channel_id=1, source_target_pairs={{0,8},{4,12},{8,0},{12,4},{16,24},{20,28},{24,16},{28,20},{1,9},{5... | collective-permute-start | bytes 786440 | tf_op jit(solution)/shard_map/ppermute | solution.py:410
  31.5 1.7 %local.14 = (f32[8,128,1024]{2,1,0:T(8,128)S(1)}, f32[8,1024,128]{2,1,0:T(8,128)S(1)}, f32[8,1024,128]{2,1,0:T(8,128)S(1)}, f32[1,1024]{1,0:T(1,128)S(1)}) custom-call(f32[4,1024]{1,0:T(4,128)S(1)} %copy-done, bf16[8,1024,128]{2,1,0:T(8,128)(2,1)S(1)} %get-tuple-element.62.refs_0_.refs_1_, ...), custom_call_target="tpu_custom_call", output_to_operand_aliasing={{0}: (5, {}), {1}: (6, {}), {2}: (7, {})} | custom-call | flops 1 | bytes 1 | tf_op jit(solution)/shard_map/local/pallas_call | solution.py:49
  33.2 0.6 %collective-permute-done.5.refs_1_.refs_6_.refs_4_ = f32[4,128,128]{2,1,0:T(8,128)S(1)} collective-permute-done((f32[4,128,128]{2,1,0:T(8,128)S(1)}, f32[4,128,128]{2,1,0:T(8,128)S(1)}, u32[]{:S(2)}, u32[]{:S(2)}) %collective-permute-start.5) | collective-permute-done | bytes 262176 | tf_op jit(solution)/shard_map/ppermute | solution.py:410
  33.8 1.6 %collective-permute-start.6 = (f32[4,128,128]{2,1,0:T(8,128)S(1)}, f32[4,128,128]{2,1,0:T(8,128)S(1)}, u32[]{:S(2)}, u32[]{:S(2)}) collective-permute-start(f32[4,128,128]{2,1,0:T(8,128)S(1)} %mix.13.refs_8_), channel_id=1, source_target_pairs={{0,8},{4,12},{8,0},{12,4},{16,24},{20,28},{24,16},{28,20},{1,9},{5... | collective-permute-start | bytes 786440 | tf_op jit(solution)/shard_map/ppermute | solution.py:410
  35.4 1.7 %local.15 = (f32[8,128,1024]{2,1,0:T(8,128)S(1)}, f32[8,1024,128]{2,1,0:T(8,128)S(1)}, f32[8,1024,128]{2,1,0:T(8,128)S(1)}, f32[1,1024]{1,0:T(1,128)S(1)}) custom-call(f32[4,1024]{1,0:T(4,128)S(1)} %copy-done, bf16[8,1024,128]{2,1,0:T(8,128)(2,1)S(1)} %get-tuple-element.62.refs_0_.refs_1_, ...), custom_call_target="tpu_custom_call", output_to_operand_aliasing={{0}: (5, {}), {1}: (6, {}), {2}: (7, {})} | custom-call | flops 1 | bytes 1 | tf_op jit(solution)/shard_map/local/pallas_call | solution.py:49
  37.1 0.4 collective-permute-done.7.refs_2_.refs_7_.refs_5_
  37.5 1.5 %collective-permute-start.12 = (f32[4,128,128]{2,1,0:T(8,128)S(1)}, f32[4,128,128]{2,1,0:T(8,128)S(1)}, u32[]{:S(2)}, u32[]{:S(2)}) collective-permute-start(f32[4,128,128]{2,1,0:T(8,128)S(1)} %mix.14.refs_16_), channel_id=1, source_target_pairs={{0,4},{4,0},{8,12},{12,8},{16,20},{20,16},{24,28},{28,24},{1,5},{5... | collective-permute-start | bytes 786440 | tf_op jit(solution)/shard_map/ppermute | solution.py:410
  39.0 1.7 %query_side.2 = (bf16[8,1024,128]{2,1,0:T(8,128)(2,1)S(1)}, f32[4,1024]{1,0:T(4,128)S(1)}) custom-call(f32[4,1024]{1,0:T(4,128)S(1)} %copy-done, bf16[8,1024,128]{2,1,0:T(8,128)(2,1)S(1)} %get-tuple-element.62.refs_0_.refs_1_, bf16[8,1024,128]{2,1,0:T(8,128)(2,1)S(1)} %get-tuple-element.63.refs_1_.refs_4_.refs_2_, ...), custom_call_target="tpu_custom_call" | custom-call | flops 1 | bytes 1 | tf_op jit(solution)/shard_map/query_side/pallas_call | solution.py:49
  40.7 1.2 %collective-permute-done.6.refs_2_.refs_7_.refs_5_ = f32[4,128,128]{2,1,0:T(8,128)S(1)} collective-permute-done((f32[4,128,128]{2,1,0:T(8,128)S(1)}, f32[4,128,128]{2,1,0:T(8,128)S(1)}, u32[]{:S(2)}, u32[]{:S(2)}) %collective-permute-start.6) | collective-permute-done | bytes 262176 | tf_op jit(solution)/shard_map/ppermute | solution.py:410
  41.9 1.5 %collective-permute-start.8 = (f32[4,128,128]{2,1,0:T(8,128)S(1)}, f32[4,128,128]{2,1,0:T(8,128)S(1)}, u32[]{:S(2)}, u32[]{:S(2)}) collective-permute-start(f32[4,128,128]{2,1,0:T(8,128)S(1)} %mix.15.refs_10_), channel_id=1, source_target_pairs={{0,4},{4,0},{8,12},{12,8},{16,20},{20,16},{24,28},{28,24},{1,5},{5... | collective-permute-start | bytes 786440 | tf_op jit(solution)/shard_map/ppermute | solution.py:410
  43.4 1.7 %query_side.3 = (bf16[8,1024,128]{2,1,0:T(8,128)(2,1)S(1)}, f32[4,1024]{1,0:T(4,128)S(1)}) custom-call(f32[4,1024]{1,0:T(4,128)S(1)} %copy-done, bf16[8,1024,128]{2,1,0:T(8,128)(2,1)S(1)} %get-tuple-element.62.refs_0_.refs_1_, bf16[8,1024,128]{2,1,0:T(8,128)(2,1)S(1)} %get-tuple-element.63.refs_1_.refs_4_.refs_2_, ...), custom_call_target="tpu_custom_call", output_to_operand_aliasing={{0}: (9, {})} | custom-call | flops 1 | bytes 1 | tf_op jit(solution)/shard_map/query_side/pallas_call | solution.py:49
  45.1 0.1 collective-permute-start.11
  45.2 1.6 %collective-permute-start.10 = (f32[4,1024]{1,0:T(4,128)S(1)}, f32[4,1024]{1,0:T(4,128)S(1)}, u32[]{:S(2)}, u32[]{:S(2)}) collective-permute-start(f32[4,1024]{1,0:T(4,128)S(1)} %get-tuple-element.108.refs_7_), channel_id=1, source_target_pairs={{0,2},{1,3},{2,0},{3,1},{4,6},{5,7},{6,4},{7,5},{8,10},{9,11},{10,... | collective-permute-start | bytes 49160 | tf_op jit(solution)/shard_map/ppermute | solution.py:449
  46.7 0.2 collective-permute-start.9
  46.9 1.3 %copy.61 = bf16[8,1024,128]{2,1,0:T(8,128)(2,1)} copy(bf16[8,1024,128]{2,1,0:T(8,128)(2,1)S(1)} %get-tuple-element.114) | data formatting | bytes 4194304
  48.2 0.0 collective-permute-done.12.refs_6_
  48.2 1.7 %key_side.2 = (bf16[8,1024,128]{2,1,0:T(8,128)(2,1)}, bf16[8,1024,128]{2,1,0:T(8,128)(2,1)}) custom-call(bf16[8,1024,128]{2,1,0:T(8,128)(2,1)S(1)} %get-tuple-element.64.refs_2_.refs_0_, bf16[8,1024,128]{2,1,0:T(8,128)(2,1)S(1)} %get-tuple-element.65.refs_3_.refs_1_, f32[8,1024,128]{2,1,0:T(8,128)S(1)} %get-tuple-element.106.refs_2_, ...), custom_call_target="tpu_custom_call" | custom-call | flops 1 | bytes 1 | tf_op jit(solution)/shard_map/key_side/pallas_call | solution.py:49
  49.9 0.0 collective-permute-done.11.refs_10_
  49.9 0.0 collective-permute-done.10.refs_9_
  49.9 0.0 collective-permute-done.9.refs_8_
  50.0 0.0 collective-permute-done.8.refs_6_
  50.0 1.7 %key_side.3 = (bf16[8,1024,128]{2,1,0:T(8,128)(2,1)}, bf16[8,1024,128]{2,1,0:T(8,128)(2,1)}, f32[4,1024]{1,0:T(4,128)}) custom-call(bf16[8,1024,128]{2,1,0:T(8,128)(2,1)S(1)} %get-tuple-element.64.refs_2_.refs_0_, bf16[8,1024,128]{2,1,0:T(8,128)(2,1)S(1)} %get-tuple-element.65.refs_3_.refs_1_, ...), custom_call_target="tpu_custom_call", output_to_operand_aliasing={{0}: (11, {}), {1}: (12, {})} | custom-call | flops 1 | bytes 1 | tf_op jit(solution)/shard_map/key_side/pallas_call | solution.py:49
  (6 shorter events, 0.3 us)
Async XLA Ops:
  2.6 10.2 %collective-permute-start = (f32[4,128,128]{2,1,0:T(8,128)S(1)}, f32[4,128,128]{2,1,0:T(8,128)S(1)}, u32[]{:S(2)}, u32[]{:S(2)}) collective-permute-start(f32[4,128,128]{2,1,0:T(8,128)S(1)} %get-tuple-element.61.refs_6_.refs_0_), channel_id=1, source_target_pairs={{0,4},{4,0},{8,12},{12,8},{16,20},{20,16},{24,28},{28,24},{1,5},{5... | collective-permute-start | bytes 786440 | tf_op jit(solution)/shard_map/ppermute | solution.py:362
  5.6 3.1 %copy-start = (f32[4,1024]{1,0:T(4,128)S(1)}, f32[4,1024]{1,0:T(4,128)}, u32[]{:S(2)}) copy-start(f32[4,1024]{1,0:T(4,128)} %refs_0_.23) | copy-start | bytes 49156
  8.6 9.8 %collective-permute-start.1 = (f32[4,128,128]{2,1,0:T(8,128)S(1)}, f32[4,128,128]{2,1,0:T(8,128)S(1)}, u32[]{:S(2)}, u32[]{:S(2)}) collective-permute-start(f32[4,128,128]{2,1,0:T(8,128)S(1)} %get-tuple-element.66.refs_3_.refs_0_), channel_id=1, source_target_pairs={{0,4},{4,0},{8,12},{12,8},{16,20},{20,16},{24,28},{28,24},{1,5},{5... | collective-permute-start | bytes 786440 | tf_op jit(solution)/shard_map/ppermute | solution.py:362
  12.8 8.4 %collective-permute-start.2 = (f32[4,128,128]{2,1,0:T(8,128)S(1)}, f32[4,128,128]{2,1,0:T(8,128)S(1)}, u32[]{:S(2)}, u32[]{:S(2)}) collective-permute-start(f32[4,128,128]{2,1,0:T(8,128)S(1)} %mix.8.refs_8_), channel_id=1, source_target_pairs={{0,8},{4,12},{8,0},{12,4},{16,24},{20,28},{24,16},{28,20},{1,9},{5... | collective-permute-start | bytes 786440 | tf_op jit(solution)/shard_map/ppermute | solution.py:410
  18.4 7.5 %collective-permute-start.3 = (f32[4,128,128]{2,1,0:T(8,128)S(1)}, f32[4,128,128]{2,1,0:T(8,128)S(1)}, u32[]{:S(2)}, u32[]{:S(2)}) collective-permute-start(f32[4,128,128]{2,1,0:T(8,128)S(1)} %mix.9.refs_8_), channel_id=1, source_target_pairs={{0,8},{4,12},{8,0},{12,4},{16,24},{20,28},{24,16},{28,20},{1,9},{5... | collective-permute-start | bytes 786440 | tf_op jit(solution)/shard_map/ppermute | solution.py:410
  21.2 8.5 %collective-permute-start.4 = (f32[4,128,128]{2,1,0:T(8,128)S(1)}, f32[4,128,128]{2,1,0:T(8,128)S(1)}, u32[]{:S(2)}, u32[]{:S(2)}) collective-permute-start(f32[4,128,128]{2,1,0:T(8,128)S(1)} %mix.10.refs_8_), channel_id=1, source_target_pairs={{0,4},{4,0},{8,16},{12,20},{16,8},{20,12},{24,28},{28,24},{1,5},{5... | collective-permute-start | bytes 786440 | tf_op jit(solution)/shard_map/ppermute | solution.py:410
  26.0 7.7 %collective-permute-start.5 = (f32[4,128,128]{2,1,0:T(8,128)S(1)}, f32[4,128,128]{2,1,0:T(8,128)S(1)}, u32[]{:S(2)}, u32[]{:S(2)}) collective-permute-start(f32[4,128,128]{2,1,0:T(8,128)S(1)} %mix.11.refs_8_), channel_id=1, source_target_pairs={{0,4},{4,0},{8,16},{12,20},{16,8},{20,12},{24,28},{28,24},{1,5},{5... | collective-permute-start | bytes 786440 | tf_op jit(solution)/shard_map/ppermute | solution.py:410
  29.8 7.7 %collective-permute-start.7 = (f32[4,128,128]{2,1,0:T(8,128)S(1)}, f32[4,128,128]{2,1,0:T(8,128)S(1)}, u32[]{:S(2)}, u32[]{:S(2)}) collective-permute-start(f32[4,128,128]{2,1,0:T(8,128)S(1)} %mix.12.refs_8_), channel_id=1, source_target_pairs={{0,8},{4,12},{8,0},{12,4},{16,24},{20,28},{24,16},{28,20},{1,9},{5... | collective-permute-start | bytes 786440 | tf_op jit(solution)/shard_map/ppermute | solution.py:410
  33.8 8.1 %collective-permute-start.6 = (f32[4,128,128]{2,1,0:T(8,128)S(1)}, f32[4,128,128]{2,1,0:T(8,128)S(1)}, u32[]{:S(2)}, u32[]{:S(2)}) collective-permute-start(f32[4,128,128]{2,1,0:T(8,128)S(1)} %mix.13.refs_8_), channel_id=1, source_target_pairs={{0,8},{4,12},{8,0},{12,4},{16,24},{20,28},{24,16},{28,20},{1,9},{5... | collective-permute-start | bytes 786440 | tf_op jit(solution)/shard_map/ppermute | solution.py:410
  37.5 10.7 %collective-permute-start.12 = (f32[4,128,128]{2,1,0:T(8,128)S(1)}, f32[4,128,128]{2,1,0:T(8,128)S(1)}, u32[]{:S(2)}, u32[]{:S(2)}) collective-permute-start(f32[4,128,128]{2,1,0:T(8,128)S(1)} %mix.14.refs_16_), channel_id=1, source_target_pairs={{0,4},{4,0},{8,12},{12,8},{16,20},{20,16},{24,28},{28,24},{1,5},{5... | collective-permute-start | bytes 786440 | tf_op jit(solution)/shard_map/ppermute | solution.py:410
  41.9 8.0 %collective-permute-start.8 = (f32[4,128,128]{2,1,0:T(8,128)S(1)}, f32[4,128,128]{2,1,0:T(8,128)S(1)}, u32[]{:S(2)}, u32[]{:S(2)}) collective-permute-start(f32[4,128,128]{2,1,0:T(8,128)S(1)} %mix.15.refs_10_), channel_id=1, source_target_pairs={{0,4},{4,0},{8,12},{12,8},{16,20},{20,16},{24,28},{28,24},{1,5},{5... | collective-permute-start | bytes 786440 | tf_op jit(solution)/shard_map/ppermute | solution.py:410
  45.1 4.8 %collective-permute-start.11 = (f32[4,1024]{1,0:T(4,128)S(1)}, f32[4,1024]{1,0:T(4,128)S(1)}, u32[]{:S(2)}, u32[]{:S(2)}) collective-permute-start(f32[4,1024]{1,0:T(4,128)S(1)} %get-tuple-element.108.refs_7_), channel_id=1, source_target_pairs={{0,3},{1,0},{2,1},{3,2},{4,7},{5,4},{6,5},{7,6},{8,11},{9,8},{10,9... | collective-permute-start | bytes 49160 | tf_op jit(solution)/shard_map/ppermute | solution.py:449
  45.2 4.8 %collective-permute-start.10 = (f32[4,1024]{1,0:T(4,128)S(1)}, f32[4,1024]{1,0:T(4,128)S(1)}, u32[]{:S(2)}, u32[]{:S(2)}) collective-permute-start(f32[4,1024]{1,0:T(4,128)S(1)} %get-tuple-element.108.refs_7_), channel_id=1, source_target_pairs={{0,2},{1,3},{2,0},{3,1},{4,6},{5,7},{6,4},{7,5},{8,10},{9,11},{10,... | collective-permute-start | bytes 49160 | tf_op jit(solution)/shard_map/ppermute | solution.py:449
  46.7 3.2 %collective-permute-start.9 = (f32[4,1024]{1,0:T(4,128)S(1)}, f32[4,1024]{1,0:T(4,128)S(1)}, u32[]{:S(2)}, u32[]{:S(2)}) collective-permute-start(f32[4,1024]{1,0:T(4,128)S(1)} %get-tuple-element.108.refs_7_), channel_id=1, source_target_pairs={{0,1},{1,2},{2,3},{3,0},{4,5},{5,6},{6,7},{7,4},{8,9},{9,10},{10,1... | collective-permute-start | bytes 49160 | tf_op jit(solution)/shard_map/ppermute | solution.py:449

commit v5 on v4

--- a/solution.py
+++ b/solution.py
@@ -11,7 +11,7 @@
 TN = (((0,), (0,)), ((), ()))
 VMEM_BYTES = 16 * 2**20
 PARTS = (4, 4)
-FILL = (1, 2, 1, 1, 1, 1, 1, 0)
+FILL = (1, 2, 0, 2, 0, 2, 0, 1)
 
 INSIDE = pl.BlockSpec(memory_space=pltpu.VMEM)
 OUTSIDE = pl.BlockSpec(memory_space=pltpu.HBM)
@@ -204,7 +204,7 @@
     return jnp.where(flag, array, 0.0)
 
 
-def query_side(level_weight, queries, out_grad, query_sum, states, rows, first, out, deps):
+def query_side(level_weight, queries, out_grad, query_sum, states, rows, first, out, done, deps):
     shape = queries.shape
     _, length, depth = shape
     count = states[0].shape[0]
@@ -215,7 +215,12 @@
         state_refs = rest[: levels + 1]
         singles = rest[levels + 1 : levels + 1 + len(single)]
         wholes = rest[levels + 1 + len(single) : levels + 1 + len(single) + len(whole)]
-        out_ref, row_ref = rest[-2:]
+        if done:
+            out_ref, row_ref, far_ref, sem = rest[-4:]
+            leave = pltpu.make_async_copy(out_ref.at[:done], far_ref.at[:done], sem)
+            leave.start()
+        else:
+            out_ref, row_ref = rest[-2:]
         bits = block_bits(levels)
         totals = [None] * levels
 
@@ -238,16 +243,18 @@
                 row = jnp.sum(turned * z, axis=0, keepdims=True)
                 totals[level] = row if totals[level] is None else totals[level] + row
             out_ref[first + i] = total.T.astype(BF16)
-        own = None
+        own = jnp.zeros((1, length), F32)
         for ref in singles:
-            own = ref[...] if own is None else own + ref[...]
+            own = own + ref[...]
         for ref in wholes:
-            own = ref[0:1, :] if own is None else own + ref[0:1, :]
+            own = own + ref[0:1, :]
             for level in range(levels):
                 totals[level] += ref[level + 1 : level + 2, :]
         row_ref[0:1, :] = own
         for level in range(levels):
             row_ref[level + 1 : level + 2, :] = totals[level]
+        if done:
+            leave.wait()
 
     args = [level_weight, queries, out_grad, query_sum, *states, *single, *whole]
     return call(
@@ -255,22 +262,26 @@
         "query_side",
         args + list(out),
         [INSIDE] * (len(args) + len(out)),
-        [pltpu.VMEM(shape, BF16), jax.ShapeDtypeStruct((levels + 1, length), F32)],
-        [INSIDE] * 2,
+        [pltpu.VMEM(shape, BF16), jax.ShapeDtypeStruct((levels + 1, length), F32)]
+        + ([jax.ShapeDtypeStruct(shape, BF16)] if done else []),
+        [INSIDE] * 2 + ([OUTSIDE] if done else []),
         deps,
         {len(args): 0} if out else {},
-    )
-
-
-def key_side(key_rows, value_rows, key_sum, value_sum, parts, levels, rows, first, out, deps):
+        [pltpu.SemaphoreType.DMA] if done else [],
+    )
+
+
+def key_side(key_rows, value_rows, key_sum, value_sum, parts, levels, rows, first, out, inner, deps):
     shape = key_rows.shape
     _, length, depth = shape
     count = parts[0].shape[0]
     summed = [jax.ShapeDtypeStruct(rows[0].shape, F32)] if rows else []
+    moved = list(inner[:2])
+    outs = 2 + len(summed) + len(moved) // 2
 
     def kernel(k_ref, v_ref, ks_ref, vs_ref, *rest):
-        k_out, v_out = rest[len(parts) + len(rows) + len(out) :][:2]
-        staged, sems = rest[-2 - 2 * len(summed) :][:2]
+        k_out, v_out = rest[len(parts) + len(rows) + len(moved) + len(out) :][:2]
+        staged, sems = rest[len(parts) + len(rows) + len(moved) + len(out) + outs :][:2]
         bits = block_bits(levels)
         copies = []
         if rows:
@@ -278,8 +289,15 @@
             for ref in rest[len(parts) + 1 : len(parts) + len(rows)]:
                 total = total + ref[...]
             rest[-2][...] = total
-            copies.append(pltpu.make_async_copy(rest[-2], rest[-5], rest[-1]))
+            far_ref = rest[len(parts) + len(rows) + len(moved) + len(out) + 2]
+            copies.append(pltpu.make_async_copy(rest[-2], far_ref, rest[-1]))
             copies[0].start()
+        if moved:
+            span = pl.ds(inner[2], shape[0] - inner[2])
+            near_ref = rest[len(parts) + len(rows)]
+            far_ref = rest[len(parts) + len(rows) + 2 + len(out) + 2 + len(summed)]
+            copies.append(pltpu.make_async_copy(near_ref.at[span], far_ref.at[span], rest[-1]))
+            copies[-1].start()
 
         def products(i):
             grad = gathered(bits, [rest[j][i] for j in range(len(parts))]).astype(BF16)
@@ -300,17 +318,26 @@
             copy.wait()
 
     args = [key_rows, value_rows, key_sum, value_sum, *parts, *rows]
+    scratch = [pltpu.VMEM((2, count, length, depth), BF16), pltpu.SemaphoreType.DMA((2, count))]
+    if rows:
+        scratch.append(pltpu.VMEM(rows[0].shape, F32))
+    if rows or moved:
+        scratch.append(pltpu.SemaphoreType.DMA)
+    aliases = {len(args) + len(moved) + i: i for i in range(len(out))}
+    if moved:
+        aliases[len(args) + 1] = outs - 1
     return call(
         kernel,
         "key_side",
-        args + list(out),
-        [INSIDE] * len(args) + [OUTSIDE] * len(out),
-        [jax.ShapeDtypeStruct(shape, BF16)] * 2 + summed,
-        [OUTSIDE] * (2 + len(summed)),
+        args + moved + list(out),
+        [INSIDE] * len(args) + ([INSIDE, OUTSIDE] if moved else []) + [OUTSIDE] * len(out),
+        [jax.ShapeDtypeStruct(shape, BF16)] * 2
+        + summed
+        + ([jax.ShapeDtypeStruct(shape, BF16)] if moved else []),
+        [OUTSIDE] * outs,
         deps,
-        {len(args) + i: i for i in range(len(out))},
-        [pltpu.VMEM((2, count, length, depth), BF16), pltpu.SemaphoreType.DMA((2, count))]
-        + ([pltpu.VMEM(rows[0].shape, F32), pltpu.SemaphoreType.DMA] if rows else []),
+        aliases,
+        scratch,
     )
 
 
@@ -345,7 +372,7 @@
     levels = size.bit_length() - 1
     top, low = levels - 1, levels - 2
     heads = queries.shape[0]
-    counts = PARTS if sum(PARTS) == heads else (heads,)
+    counts = PARTS if sum(PARTS) == heads else (heads - heads // 2, heads // 2)
     parts = range(len(counts))
     firsts = [sum(counts[:part]) for part in parts]
     steps = swaps(size)
@@ -414,19 +441,20 @@
         grads[part] = state_grads(q_in, g_in, w_in, firsts[part], counts[part], dep)
         dep = [grads[part][top]]
 
-    query_out, weight_rows, asked = [], [], list(parts)
+    query_out, weight_rows, far, asked = [], [], [], list(parts)
 
     def query(dep):
         part = asked.pop(0)
-        grad, row = query_side(
+        grad, row, *far[:] = query_side(
             w_in,
             q_in,
             g_in,
             held[0],
             got[part][: levels + 1],
-            ([] if weight_rows else rows, weight_rows),
+            ([] if asked else rows, weight_rows),
             firsts[part],
             query_out,
+            firsts[part],
             dep,
         )
         query_out[:], weight_rows[:] = [grad], [row]
@@ -449,25 +477,27 @@
         lax.ppermute(weight_rows[0], "head", [(n, (n + shift) % ways) for n in range(ways)])
         for shift in range(1, ways)
     ]
-    key_out, weight_grad = [], None
+    key_out, query_grad, weight_grad = [], None, None
     for part in parts:
-        *key_out, weight_grad = [
-            *key_side(
-                k_in,
-                v_in,
-                held[1],
-                held[2],
-                got[part][low + 1 :],
-                levels,
-                weight_rows if part == parts[-1] else [],
-                firsts[part],
-                key_out,
-                dep,
-            ),
-            *([] if part == parts[-1] else [None]),
-        ]
-        dep = []
-    return query_out[0], key_out[0], key_out[1], weight_grad
+        key_grad, value_grad, *more = key_side(
+            k_in,
+            v_in,
+            held[1],
+            held[2],
+            got[part][low + 1 :],
+            levels,
+            weight_rows if part == parts[-1] else [],
+            firsts[part],
+            key_out,
+            (query_out[0], far[0], firsts[-1]) if part == parts[0] else (),
+            dep,
+        )
+        if part == parts[0]:
+            query_grad = more.pop()
+        if part == parts[-1]:
+            weight_grad = more.pop()
+        key_out, dep = [key_grad, value_grad], []
+    return query_grad, key_out[0], key_out[1], weight_grad
 
 
 def solution(mesh):

time: 52 us -> 50.3 us (0.967)
  local copies, waits for them, and re-layouts: 1.32 us -> 0.01 us
  waiting for transfers between devices: 3.82 us -> 2.71 us
    ppermute x8, waiting for transfers between devices: 3.51 us -> 1.49 us  [advance(): have.append(lax.ppermute(sent, 'ctx', steps[step]))]
    unnamed x3 -> x2, local copies, waits for them, and re-layouts: 1.32 us -> 0.01 us
    ppermute x3, waiting for transfers between devices: 0.01 us -> 0.91 us  [per_device(): lax.ppermute(weight_rows[0], 'head', [(n, (n + shift) % ways) for n in ra...]
  transfers between devices with their start and end apart: 13 -> 13, of which waited for: 5 -> 3; matrix products, arithmetic and copies ran while one was open for 3% -> 0% of each run, Pallas kernels for 47% -> 49%
where the time goes in v5:
time: 50.3 us; the launch traced here: 50.1 us
  Pallas kernels  28.3 us (56%)
  starting transfers between devices  18.1 us (36%)
  waiting for transfers between devices  2.71 us (5%)
  between operations  1.02 us (2%)
    pallas_call x24, Pallas kernels, call(): pl.pallas_call(body, in_specs=list(specs) + [ANYWHERE] * len(deps), out_s...  28.3 us
    ppermute x8, starting transfers between devices, advance(): have.append(lax.ppermute(sent, 'ctx', steps[step]))  13.2 us
    ppermute x2, starting transfers between devices, per_device(): got[part].append(lax.ppermute(state, 'ctx', steps[0]))  3.12 us
    ppermute x3, starting transfers between devices, per_device(): lax.ppermute(weight_rows[0], 'head', [(n, (n + shift) % ways) for n in ra...  1.81 us
    ppermute x8, waiting for transfers between devices, advance(): have.append(lax.ppermute(sent, 'ctx', steps[step]))  1.49 us
  transfers between devices with their start and end apart: 13, of which 3 were waited for; matrix products, arithmetic and copies ran while one was open for 0% of the time, Pallas kernels for 49%

profile of v5, /device:TPU:0, one launch (start us, length us, event | category | flops | bytes accessed | tf_op | source)
XLA Modules:
  0.0 50.1 jit_solution(13482542856393294879)
XLA Ops:
  0.6 1.9 %load_states.2 = (bf16[8,1024,128]{2,1,0:T(8,128)(2,1)S(1)}, bf16[8,1024,128]{2,1,0:T(8,128)(2,1)S(1)}, f32[4,128,128]{2,1,0:T(8,128)S(1)}) custom-call(bf16[8,1024,128]{2,1,0:T(8,128)(2,1)} %refs_0_.13, bf16[8,1024,128]{2,1,0:T(8,128)(2,1)} %refs_1_.3), custom_call_target="tpu_custom_call" | custom-call | flops 1 | bytes 1 | tf_op jit(solution)/shard_map/load_states/pallas_call | solution.py:49
  2.6 3.0 %collective-permute-start = (f32[4,128,128]{2,1,0:T(8,128)S(1)}, f32[4,128,128]{2,1,0:T(8,128)S(1)}, u32[]{:S(2)}, u32[]{:S(2)}) collective-permute-start(f32[4,128,128]{2,1,0:T(8,128)S(1)} %get-tuple-element.63.refs_6_.refs_0_), channel_id=1, source_target_pairs={{0,4},{4,0},{8,12},{12,8},{16,20},{20,16},{24,28},{28,24},{1,5},{5... | collective-permute-start | bytes 786440 | tf_op jit(solution)/shard_map/ppermute | solution.py:389
  5.6 0.0 copy-start
  5.6 3.0 %load_states.3 = (bf16[8,1024,128]{2,1,0:T(8,128)(2,1)S(1)}, bf16[8,1024,128]{2,1,0:T(8,128)(2,1)S(1)}, bf16[8,1024,128]{2,1,0:T(8,128)(2,1)S(1)}, bf16[8,1024,128]{2,1,0:T(8,128)(2,1)S(1)}, f32[4,128,128]{2,1,0:T(8,128)S(1)}) custom-call(bf16[8,1024,128]{2,1,0:T(8,128)(2,1)} %refs_0_.13, ...), custom_call_target="tpu_custom_call", output_to_operand_aliasing={{0}: (4, {}), {1}: (5, {})} | custom-call | flops 1 | bytes 1 | tf_op jit(solution)/shard_map/load_states/pallas_call | solution.py:49
  8.6 0.1 collective-permute-start.2
  8.6 0.0 copy-done
  8.7 1.0 %state_grads.2 = (f32[4,128,128]{2,1,0:T(8,128)S(1)}, f32[4,128,128]{2,1,0:T(8,128)S(1)}, f32[4,128,128]{2,1,0:T(8,128)S(1)}) custom-call(bf16[8,1024,128]{2,1,0:T(8,128)(2,1)S(1)} %get-tuple-element.66.refs_0_.refs_1_, bf16[8,1024,128]{2,1,0:T(8,128)(2,1)S(1)} %get-tuple-element.67.refs_1_.refs_4_.refs_2_, f32[4,1024]{1,0:T(4,128)S(1)} %copy-done, ...), custom_call_target="tpu_custom_call" | custom-call | flops 1 | bytes 1 | tf_op jit(solution)/shard_map/state_grads/pallas_call | solution.py:49
  9.7 1.0 %state_grads.3 = (f32[4,128,128]{2,1,0:T(8,128)S(1)}, f32[4,128,128]{2,1,0:T(8,128)S(1)}, f32[4,128,128]{2,1,0:T(8,128)S(1)}) custom-call(bf16[8,1024,128]{2,1,0:T(8,128)(2,1)S(1)} %get-tuple-element.66.refs_0_.refs_1_, bf16[8,1024,128]{2,1,0:T(8,128)(2,1)S(1)} %get-tuple-element.67.refs_1_.refs_4_.refs_2_, f32[4,1024]{1,0:T(4,128)S(1)} %copy-done, ...), custom_call_target="tpu_custom_call" | custom-call | flops 1 | bytes 1 | tf_op jit(solution)/shard_map/state_grads/pallas_call | solution.py:49
  10.7 1.7 %local.8 = (f32[8,128,1024]{2,1,0:T(8,128)S(1)}, f32[8,1024,128]{2,1,0:T(8,128)S(1)}, f32[8,1024,128]{2,1,0:T(8,128)S(1)}, f32[1,1024]{1,0:T(1,128)S(1)}) custom-call(f32[4,1024]{1,0:T(4,128)S(1)} %copy-done, bf16[8,1024,128]{2,1,0:T(8,128)(2,1)S(1)} %get-tuple-element.66.refs_0_.refs_1_, bf16[8,1024,128]{2,1,0:T(8,128)(2,1)S(1)} %get-tuple-element.64.refs_2_.refs_0_, ...), custom_call_target="tpu_custom_call" | custom-call | flops 1 | bytes 1 | tf_op jit(solution)/shard_map/local/pallas_call | solution.py:49
  12.4 0.3 collective-permute-done.refs_1_.refs_4_
  12.8 2.2 %collective-permute-start.1 = (f32[4,128,128]{2,1,0:T(8,128)S(1)}, f32[4,128,128]{2,1,0:T(8,128)S(1)}, u32[]{:S(2)}, u32[]{:S(2)}) collective-permute-start(f32[4,128,128]{2,1,0:T(8,128)S(1)} %mix.8.refs_8_), channel_id=1, source_target_pairs={{0,8},{4,12},{8,0},{12,4},{16,24},{20,28},{24,16},{28,20},{1,9},{5... | collective-permute-start | bytes 786440 | tf_op jit(solution)/shard_map/ppermute | solution.py:437
  15.0 1.7 %local.9 = (f32[8,128,1024]{2,1,0:T(8,128)S(1)}, f32[8,1024,128]{2,1,0:T(8,128)S(1)}, f32[8,1024,128]{2,1,0:T(8,128)S(1)}, f32[1,1024]{1,0:T(1,128)S(1)}) custom-call(f32[4,1024]{1,0:T(4,128)S(1)} %copy-done, bf16[8,1024,128]{2,1,0:T(8,128)(2,1)S(1)} %get-tuple-element.66.refs_0_.refs_1_, ...), custom_call_target="tpu_custom_call", output_to_operand_aliasing={{0}: (5, {}), {1}: (6, {}), {2}: (7, {})} | custom-call | flops 1 | bytes 1 | tf_op jit(solution)/shard_map/local/pallas_call | solution.py:49
  16.7 1.7 %local.10 = (f32[8,128,1024]{2,1,0:T(8,128)S(1)}, f32[8,1024,128]{2,1,0:T(8,128)S(1)}, f32[8,1024,128]{2,1,0:T(8,128)S(1)}, f32[1,1024]{1,0:T(1,128)S(1)}) custom-call(f32[4,1024]{1,0:T(4,128)S(1)} %copy-done, bf16[8,1024,128]{2,1,0:T(8,128)(2,1)S(1)} %get-tuple-element.66.refs_0_.refs_1_, ...), custom_call_target="tpu_custom_call", output_to_operand_aliasing={{0}: (5, {}), {1}: (6, {}), {2}: (7, {})} | custom-call | flops 1 | bytes 1 | tf_op jit(solution)/shard_map/local/pallas_call | solution.py:49
  18.4 0.0 collective-permute-done.2.refs_1_.refs_4_
  18.4 1.0 %collective-permute-start.4 = (f32[4,128,128]{2,1,0:T(8,128)S(1)}, f32[4,128,128]{2,1,0:T(8,128)S(1)}, u32[]{:S(2)}, u32[]{:S(2)}) collective-permute-start(f32[4,128,128]{2,1,0:T(8,128)S(1)} %mix.9.refs_4_), channel_id=1, source_target_pairs={{0,8},{4,12},{8,0},{12,4},{16,24},{20,28},{24,16},{28,20},{1,9},{5... | collective-permute-start | bytes 786440 | tf_op jit(solution)/shard_map/ppermute | solution.py:437
  19.4 1.5 %collective-permute-done.1.refs_3_.refs_5_ = f32[4,128,128]{2,1,0:T(8,128)S(1)} collective-permute-done((f32[4,128,128]{2,1,0:T(8,128)S(1)}, f32[4,128,128]{2,1,0:T(8,128)S(1)}, u32[]{:S(2)}, u32[]{:S(2)}) %collective-permute-start.1) | collective-permute-done | bytes 262176 | tf_op jit(solution)/shard_map/ppermute | solution.py:437
  21.0 1.9 %collective-permute-start.3 = (f32[4,128,128]{2,1,0:T(8,128)S(1)}, f32[4,128,128]{2,1,0:T(8,128)S(1)}, u32[]{:S(2)}, u32[]{:S(2)}) collective-permute-start(f32[4,128,128]{2,1,0:T(8,128)S(1)} %mix.10.refs_8_), channel_id=1, source_target_pairs={{0,4},{4,0},{8,16},{12,20},{16,8},{20,12},{24,28},{28,24},{1,5},{5... | collective-permute-start | bytes 786440 | tf_op jit(solution)/shard_map/ppermute | solution.py:437
  22.9 1.7 %local.11 = (f32[8,128,1024]{2,1,0:T(8,128)S(1)}, f32[8,1024,128]{2,1,0:T(8,128)S(1)}, f32[8,1024,128]{2,1,0:T(8,128)S(1)}, f32[1,1024]{1,0:T(1,128)S(1)}) custom-call(f32[4,1024]{1,0:T(4,128)S(1)} %copy-done, bf16[8,1024,128]{2,1,0:T(8,128)(2,1)S(1)} %get-tuple-element.66.refs_0_.refs_1_, ...), custom_call_target="tpu_custom_call", output_to_operand_aliasing={{0}: (5, {}), {1}: (6, {}), {2}: (7, {})} | custom-call | flops 1 | bytes 1 | tf_op jit(solution)/shard_map/local/pallas_call | solution.py:49
  24.6 1.7 %local.12 = (f32[8,128,1024]{2,1,0:T(8,128)S(1)}, f32[8,1024,128]{2,1,0:T(8,128)S(1)}, f32[8,1024,128]{2,1,0:T(8,128)S(1)}, f32[1,1024]{1,0:T(1,128)S(1)}) custom-call(f32[4,1024]{1,0:T(4,128)S(1)} %copy-done, bf16[8,1024,128]{2,1,0:T(8,128)(2,1)S(1)} %get-tuple-element.66.refs_0_.refs_1_, ...), custom_call_target="tpu_custom_call", output_to_operand_aliasing={{0}: (5, {}), {1}: (6, {}), {2}: (7, {})} | custom-call | flops 1 | bytes 1 | tf_op jit(solution)/shard_map/local/pallas_call | solution.py:49
  26.3 0.0 collective-permute-done.4.refs_3_.refs_5_
  26.3 0.1 mix.11.refs_2_
  26.3 1.4 %collective-permute-start.6 = (f32[4,128,128]{2,1,0:T(8,128)S(1)}, f32[4,128,128]{2,1,0:T(8,128)S(1)}, u32[]{:S(2)}, u32[]{:S(2)}) collective-permute-start(f32[4,128,128]{2,1,0:T(8,128)S(1)} %mix.11.refs_2_), channel_id=1, source_target_pairs={{0,4},{4,0},{8,16},{12,20},{16,8},{20,12},{24,28},{28,24},{1,5},{5... | collective-permute-start | bytes 786440 | tf_op jit(solution)/shard_map/ppermute | solution.py:437
  27.8 0.0 collective-permute-done.3.refs_1_.refs_6_.refs_4_
  27.8 2.0 %collective-permute-start.5 = (f32[4,128,128]{2,1,0:T(8,128)S(1)}, f32[4,128,128]{2,1,0:T(8,128)S(1)}, u32[]{:S(2)}, u32[]{:S(2)}) collective-permute-start(f32[4,128,128]{2,1,0:T(8,128)S(1)} %mix.12.refs_8_), channel_id=1, source_target_pairs={{0,8},{4,12},{8,0},{12,4},{16,24},{20,28},{24,16},{28,20},{1,9},{5... | collective-permute-start | bytes 786440 | tf_op jit(solution)/shard_map/ppermute | solution.py:437
  29.8 1.9 %local.13 = (f32[8,128,1024]{2,1,0:T(8,128)S(1)}, f32[8,1024,128]{2,1,0:T(8,128)S(1)}, f32[8,1024,128]{2,1,0:T(8,128)S(1)}, f32[1,1024]{1,0:T(1,128)S(1)}) custom-call(f32[4,1024]{1,0:T(4,128)S(1)} %copy-done, bf16[8,1024,128]{2,1,0:T(8,128)(2,1)S(1)} %get-tuple-element.66.refs_0_.refs_1_, ...), custom_call_target="tpu_custom_call", output_to_operand_aliasing={{0}: (5, {}), {1}: (6, {}), {2}: (7, {})} | custom-call | flops 1 | bytes 1 | tf_op jit(solution)/shard_map/local/pallas_call | solution.py:49
  31.7 1.7 %local.14 = (f32[8,128,1024]{2,1,0:T(8,128)S(1)}, f32[8,1024,128]{2,1,0:T(8,128)S(1)}, f32[8,1024,128]{2,1,0:T(8,128)S(1)}, f32[1,1024]{1,0:T(1,128)S(1)}) custom-call(f32[4,1024]{1,0:T(4,128)S(1)} %copy-done, bf16[8,1024,128]{2,1,0:T(8,128)(2,1)S(1)} %get-tuple-element.66.refs_0_.refs_1_, ...), custom_call_target="tpu_custom_call", output_to_operand_aliasing={{0}: (5, {}), {1}: (6, {}), {2}: (7, {})} | custom-call | flops 1 | bytes 1 | tf_op jit(solution)/shard_map/local/pallas_call | solution.py:49
  33.5 0.0 collective-permute-done.6.refs_1_.refs_6_.refs_4_
  33.5 0.1 mix.13.refs_3_
  33.5 1.8 %collective-permute-start.8 = (f32[4,128,128]{2,1,0:T(8,128)S(1)}, f32[4,128,128]{2,1,0:T(8,128)S(1)}, u32[]{:S(2)}, u32[]{:S(2)}) collective-permute-start(f32[4,128,128]{2,1,0:T(8,128)S(1)} %mix.13.refs_3_), channel_id=1, source_target_pairs={{0,8},{4,12},{8,0},{12,4},{16,24},{20,28},{24,16},{28,20},{1,9},{5... | collective-permute-start | bytes 786440 | tf_op jit(solution)/shard_map/ppermute | solution.py:437
  35.4 0.0 collective-permute-done.5.refs_2_.refs_7_.refs_5_
  35.4 0.1 mix.14.refs_8_
  35.4 1.6 %collective-permute-start.7 = (f32[4,128,128]{2,1,0:T(8,128)S(1)}, f32[4,128,128]{2,1,0:T(8,128)S(1)}, u32[]{:S(2)}, u32[]{:S(2)}) collective-permute-start(f32[4,128,128]{2,1,0:T(8,128)S(1)} %mix.14.refs_8_), channel_id=1, source_target_pairs={{0,4},{4,0},{8,12},{12,8},{16,20},{20,16},{24,28},{28,24},{1,5},{5... | collective-permute-start | bytes 786440 | tf_op jit(solution)/shard_map/ppermute | solution.py:437
  37.0 1.7 %query_side.2 = (bf16[8,1024,128]{2,1,0:T(8,128)(2,1)S(1)}, f32[4,1024]{1,0:T(4,128)S(1)}) custom-call(f32[4,1024]{1,0:T(4,128)S(1)} %copy-done, bf16[8,1024,128]{2,1,0:T(8,128)(2,1)S(1)} %get-tuple-element.66.refs_0_.refs_1_, bf16[8,1024,128]{2,1,0:T(8,128)(2,1)S(1)} %get-tuple-element.67.refs_1_.refs_4_.refs_2_, ...), custom_call_target="tpu_custom_call" | custom-call | flops 1 | bytes 1 | tf_op jit(solution)/shard_map/query_side/pallas_call | solution.py:49
  38.7 1.7 %local.15 = (f32[8,128,1024]{2,1,0:T(8,128)S(1)}, f32[8,1024,128]{2,1,0:T(8,128)S(1)}, f32[8,1024,128]{2,1,0:T(8,128)S(1)}, f32[1,1024]{1,0:T(1,128)S(1)}) custom-call(f32[4,1024]{1,0:T(4,128)S(1)} %copy-done, bf16[8,1024,128]{2,1,0:T(8,128)(2,1)S(1)} %get-tuple-element.66.refs_0_.refs_1_, ...), custom_call_target="tpu_custom_call", output_to_operand_aliasing={{0}: (5, {}), {1}: (6, {}), {2}: (7, {})} | custom-call | flops 1 | bytes 1 | tf_op jit(solution)/shard_map/local/pallas_call | solution.py:49
  40.4 0.0 collective-permute-done.8.refs_2_.refs_7_.refs_5_
  40.4 0.1 mix.15.refs_18_
  40.5 1.2 %collective-permute-start.9 = (f32[4,128,128]{2,1,0:T(8,128)S(1)}, f32[4,128,128]{2,1,0:T(8,128)S(1)}, u32[]{:S(2)}, u32[]{:S(2)}) collective-permute-start(f32[4,128,128]{2,1,0:T(8,128)S(1)} %mix.15.refs_18_), channel_id=1, source_target_pairs={{0,4},{4,0},{8,12},{12,8},{16,20},{20,16},{24,28},{28,24},{1,5},{5... | collective-permute-start | bytes 786440 | tf_op jit(solution)/shard_map/ppermute | solution.py:437
  41.7 1.7 %query_side.3 = (bf16[8,1024,128]{2,1,0:T(8,128)(2,1)S(1)}, f32[4,1024]{1,0:T(4,128)S(1)}, bf16[8,1024,128]{2,1,0:T(8,128)(2,1)}) custom-call(f32[4,1024]{1,0:T(4,128)S(1)} %copy-done, bf16[8,1024,128]{2,1,0:T(8,128)(2,1)S(1)} %get-tuple-element.66.refs_0_.refs_1_, ...), custom_call_target="tpu_custom_call", output_to_operand_aliasing={{0}: (17, {})} | custom-call | flops 1 | bytes 1 | tf_op jit(solution)/shard_map/query_side/pallas_call | solution.py:49
  43.4 0.1 collective-permute-start.12
  43.5 1.6 %collective-permute-start.11 = (f32[4,1024]{1,0:T(4,128)S(1)}, f32[4,1024]{1,0:T(4,128)S(1)}, u32[]{:S(2)}, u32[]{:S(2)}) collective-permute-start(f32[4,1024]{1,0:T(4,128)S(1)} %get-tuple-element.111.refs_9_.refs_7_), channel_id=1, source_target_pairs={{0,2},{1,3},{2,0},{3,1},{4,6},{5,7},{6,4},{7,5},{8,10},{9,11},{10,... | collective-permute-start | bytes 49160 | tf_op jit(solution)/shard_map/ppermute | solution.py:477
  45.1 0.2 collective-permute-start.10
  45.3 0.0 collective-permute-done.7.refs_6_
  45.3 2.1 %key_side.2 = (bf16[8,1024,128]{2,1,0:T(8,128)(2,1)}, bf16[8,1024,128]{2,1,0:T(8,128)(2,1)}, bf16[8,1024,128]{2,1,0:T(8,128)(2,1)}) custom-call(bf16[8,1024,128]{2,1,0:T(8,128)(2,1)S(1)} %get-tuple-element.64.refs_2_.refs_0_, bf16[8,1024,128]{2,1,0:T(8,128)(2,1)S(1)} %get-tuple-element.65.refs_3_.refs_1_, ...), custom_call_target="tpu_custom_call", output_to_operand_aliasing={{2}: (8, {})} | custom-call | flops 1 | bytes 1 | tf_op jit(solution)/shard_map/key_side/pallas_call | solution.py:49
  47.3 0.0 collective-permute-done.12.refs_10_
  47.3 0.0 collective-permute-done.11.refs_9_
  47.3 0.9 %collective-permute-done.10.refs_8_ = f32[4,1024]{1,0:T(4,128)S(1)} collective-permute-done((f32[4,1024]{1,0:T(4,128)S(1)}, f32[4,1024]{1,0:T(4,128)S(1)}, u32[]{:S(2)}, u32[]{:S(2)}) %collective-permute-start.10) | collective-permute-done | bytes 16416 | tf_op jit(solution)/shard_map/ppermute | solution.py:477
  48.3 0.0 collective-permute-done.9.refs_6_
  48.3 1.7 %key_side.3 = (bf16[8,1024,128]{2,1,0:T(8,128)(2,1)}, bf16[8,1024,128]{2,1,0:T(8,128)(2,1)}, f32[4,1024]{1,0:T(4,128)}) custom-call(bf16[8,1024,128]{2,1,0:T(8,128)(2,1)S(1)} %get-tuple-element.64.refs_2_.refs_0_, bf16[8,1024,128]{2,1,0:T(8,128)(2,1)S(1)} %get-tuple-element.65.refs_3_.refs_1_, ...), custom_call_target="tpu_custom_call", output_to_operand_aliasing={{0}: (11, {}), {1}: (12, {})} | custom-call | flops 1 | bytes 1 | tf_op jit(solution)/shard_map/key_side/pallas_call | solution.py:49
  (4 shorter events, 0.2 us)
Async XLA Ops:
  2.6 10.2 %collective-permute-start = (f32[4,128,128]{2,1,0:T(8,128)S(1)}, f32[4,128,128]{2,1,0:T(8,128)S(1)}, u32[]{:S(2)}, u32[]{:S(2)}) collective-permute-start(f32[4,128,128]{2,1,0:T(8,128)S(1)} %get-tuple-element.63.refs_6_.refs_0_), channel_id=1, source_target_pairs={{0,4},{4,0},{8,12},{12,8},{16,20},{20,16},{24,28},{28,24},{1,5},{5... | collective-permute-start | bytes 786440 | tf_op jit(solution)/shard_map/ppermute | solution.py:389
  5.6 3.1 %copy-start = (f32[4,1024]{1,0:T(4,128)S(1)}, f32[4,1024]{1,0:T(4,128)}, u32[]{:S(2)}) copy-start(f32[4,1024]{1,0:T(4,128)} %refs_0_.23) | copy-start | bytes 49156
  8.6 9.8 %collective-permute-start.2 = (f32[4,128,128]{2,1,0:T(8,128)S(1)}, f32[4,128,128]{2,1,0:T(8,128)S(1)}, u32[]{:S(2)}, u32[]{:S(2)}) collective-permute-start(f32[4,128,128]{2,1,0:T(8,128)S(1)} %get-tuple-element.68.refs_3_.refs_0_), channel_id=1, source_target_pairs={{0,4},{4,0},{8,12},{12,8},{16,20},{20,16},{24,28},{28,24},{1,5},{5... | collective-permute-start | bytes 786440 | tf_op jit(solution)/shard_map/ppermute | solution.py:389
  12.8 8.1 %collective-permute-start.1 = (f32[4,128,128]{2,1,0:T(8,128)S(1)}, f32[4,128,128]{2,1,0:T(8,128)S(1)}, u32[]{:S(2)}, u32[]{:S(2)}) collective-permute-start(f32[4,128,128]{2,1,0:T(8,128)S(1)} %mix.8.refs_8_), channel_id=1, source_target_pairs={{0,8},{4,12},{8,0},{12,4},{16,24},{20,28},{24,16},{28,20},{1,9},{5... | collective-permute-start | bytes 786440 | tf_op jit(solution)/shard_map/ppermute | solution.py:437
  18.4 7.8 %collective-permute-start.4 = (f32[4,128,128]{2,1,0:T(8,128)S(1)}, f32[4,128,128]{2,1,0:T(8,128)S(1)}, u32[]{:S(2)}, u32[]{:S(2)}) collective-permute-start(f32[4,128,128]{2,1,0:T(8,128)S(1)} %mix.9.refs_4_), channel_id=1, source_target_pairs={{0,8},{4,12},{8,0},{12,4},{16,24},{20,28},{24,16},{28,20},{1,9},{5... | collective-permute-start | bytes 786440 | tf_op jit(solution)/shard_map/ppermute | solution.py:437
  21.0 6.8 %collective-permute-start.3 = (f32[4,128,128]{2,1,0:T(8,128)S(1)}, f32[4,128,128]{2,1,0:T(8,128)S(1)}, u32[]{:S(2)}, u32[]{:S(2)}) collective-permute-start(f32[4,128,128]{2,1,0:T(8,128)S(1)} %mix.10.refs_8_), channel_id=1, source_target_pairs={{0,4},{4,0},{8,16},{12,20},{16,8},{20,12},{24,28},{28,24},{1,5},{5... | collective-permute-start | bytes 786440 | tf_op jit(solution)/shard_map/ppermute | solution.py:437
  26.3 7.1 %collective-permute-start.6 = (f32[4,128,128]{2,1,0:T(8,128)S(1)}, f32[4,128,128]{2,1,0:T(8,128)S(1)}, u32[]{:S(2)}, u32[]{:S(2)}) collective-permute-start(f32[4,128,128]{2,1,0:T(8,128)S(1)} %mix.11.refs_2_), channel_id=1, source_target_pairs={{0,4},{4,0},{8,16},{12,20},{16,8},{20,12},{24,28},{28,24},{1,5},{5... | collective-permute-start | bytes 786440 | tf_op jit(solution)/shard_map/ppermute | solution.py:437
  27.8 7.5 %collective-permute-start.5 = (f32[4,128,128]{2,1,0:T(8,128)S(1)}, f32[4,128,128]{2,1,0:T(8,128)S(1)}, u32[]{:S(2)}, u32[]{:S(2)}) collective-permute-start(f32[4,128,128]{2,1,0:T(8,128)S(1)} %mix.12.refs_8_), channel_id=1, source_target_pairs={{0,8},{4,12},{8,0},{12,4},{16,24},{20,28},{24,16},{28,20},{1,9},{5... | collective-permute-start | bytes 786440 | tf_op jit(solution)/shard_map/ppermute | solution.py:437
  33.5 6.9 %collective-permute-start.8 = (f32[4,128,128]{2,1,0:T(8,128)S(1)}, f32[4,128,128]{2,1,0:T(8,128)S(1)}, u32[]{:S(2)}, u32[]{:S(2)}) collective-permute-start(f32[4,128,128]{2,1,0:T(8,128)S(1)} %mix.13.refs_3_), channel_id=1, source_target_pairs={{0,8},{4,12},{8,0},{12,4},{16,24},{20,28},{24,16},{28,20},{1,9},{5... | collective-permute-start | bytes 786440 | tf_op jit(solution)/shard_map/ppermute | solution.py:437
  35.4 9.8 %collective-permute-start.7 = (f32[4,128,128]{2,1,0:T(8,128)S(1)}, f32[4,128,128]{2,1,0:T(8,128)S(1)}, u32[]{:S(2)}, u32[]{:S(2)}) collective-permute-start(f32[4,128,128]{2,1,0:T(8,128)S(1)} %mix.14.refs_8_), channel_id=1, source_target_pairs={{0,4},{4,0},{8,12},{12,8},{16,20},{20,16},{24,28},{28,24},{1,5},{5... | collective-permute-start | bytes 786440 | tf_op jit(solution)/shard_map/ppermute | solution.py:437
  40.5 7.8 %collective-permute-start.9 = (f32[4,128,128]{2,1,0:T(8,128)S(1)}, f32[4,128,128]{2,1,0:T(8,128)S(1)}, u32[]{:S(2)}, u32[]{:S(2)}) collective-permute-start(f32[4,128,128]{2,1,0:T(8,128)S(1)} %mix.15.refs_18_), channel_id=1, source_target_pairs={{0,4},{4,0},{8,12},{12,8},{16,20},{20,16},{24,28},{28,24},{1,5},{5... | collective-permute-start | bytes 786440 | tf_op jit(solution)/shard_map/ppermute | solution.py:437
  43.4 3.9 %collective-permute-start.12 = (f32[4,1024]{1,0:T(4,128)S(1)}, f32[4,1024]{1,0:T(4,128)S(1)}, u32[]{:S(2)}, u32[]{:S(2)}) collective-permute-start(f32[4,1024]{1,0:T(4,128)S(1)} %get-tuple-element.111.refs_9_.refs_7_), channel_id=1, source_target_pairs={{0,3},{1,0},{2,1},{3,2},{4,7},{5,4},{6,5},{7,6},{8,11},{9,8},{10,9... | collective-permute-start | bytes 49160 | tf_op jit(solution)/shard_map/ppermute | solution.py:477
  43.5 3.8 %collective-permute-start.11 = (f32[4,1024]{1,0:T(4,128)S(1)}, f32[4,1024]{1,0:T(4,128)S(1)}, u32[]{:S(2)}, u32[]{:S(2)}) collective-permute-start(f32[4,1024]{1,0:T(4,128)S(1)} %get-tuple-element.111.refs_9_.refs_7_), channel_id=1, source_target_pairs={{0,2},{1,3},{2,0},{3,1},{4,6},{5,7},{6,4},{7,5},{8,10},{9,11},{10,... | collective-permute-start | bytes 49160 | tf_op jit(solution)/shard_map/ppermute | solution.py:477
  45.1 3.2 %collective-permute-start.10 = (f32[4,1024]{1,0:T(4,128)S(1)}, f32[4,1024]{1,0:T(4,128)S(1)}, u32[]{:S(2)}, u32[]{:S(2)}) collective-permute-start(f32[4,1024]{1,0:T(4,128)S(1)} %get-tuple-element.111.refs_9_.refs_7_), channel_id=1, source_target_pairs={{0,1},{1,2},{2,3},{3,0},{4,5},{5,6},{6,7},{7,4},{8,9},{9,10},{10,1... | collective-permute-start | bytes 49160 | tf_op jit(solution)/shard_map/ppermute | solution.py:477
